TPU v7x, 32 devices: a whole 2x2x4 slice. The times are simulated.
32 devices in a mesh: group: 16 (over z, y, core), mp: 2 (over x).
Axes of the slice: x: 2, y: 2, z: 4, core: 2. Of those that a mesh axis runs over, the one named last changes fastest.
Arguments:
- anchor: float32 [16, 2048, 2048], P(None, 'group', 'mp'), may hold values from -6 to 6
- momentum: float32 [16, 2048, 2048], P(None, 'group', 'mp'), may hold values from -3 to 3
- deltas: float32 [16, 2, 2048, 2048], P('group', None, None, 'mp'), may hold values from -3 to 3
- old_path: int32 [16, 2], replicated, may hold values from 0 to 7, as said below
- new_path: int32 [16, 2], replicated, may hold values from 0 to 7, as said below
- tokens: bfloat16 [16, 1024, 2048], P('group', None, 'mp'), may hold values from -40 to 40
- cotangent: bfloat16 [16, 1024, 2048], P('group', None, 'mp'), may hold values from -6 to 6
Outputs:
- new_anchor: float32 [16, 2048, 2048], P(None, 'group', 'mp')
- new_momentum: float32 [16, 2048, 2048], P(None, 'group', 'mp')
- grads: bfloat16 [16, 2, 2048, 2048], P('group', None, None, 'mp')
Inputs may be any that keep to these rules, and one draw needn't show every extreme that they name: `old_path`: for each of the 2 levels, every one of the 8 modules is named by at least one group. `new_path`: for each of the 2 levels, every one of the 8 modules is named by at least one group.
All inputs are finite; a program needn't handle non-finite values.
Results may differ from a plain program's by a relative error of at most 0.014.
Values may be sent and summed in bfloat16 or wider, within the bound.
No kernel may reach another device: no remote copies, remote signals or barrier semaphores. Data moves between devices by JAX's collectives and lax.ppermute only.
A program may use at most 192 MiB of HBM per device.

v0:
```python
import math

import jax
import jax.numpy as jnp
from jax import lax
from jax.sharding import PartitionSpec as P

D = 2048
MODS = 8
LEVELS = 2


outer_rate = 0.7
momentum_rate = 0.9
epsilon = 1e-06


def silu_slope(values):
    sigmoid_part = jax.nn.sigmoid(values)
    return sigmoid_part * (1.0 + values * (1.0 - sigmoid_part))


def normalize(hidden):
    values = hidden.astype(jnp.float32)
    squares = lax.psum(jnp.sum(values * values, axis=-1), "mp")
    scale = lax.rsqrt(squares / D + epsilon)
    normed = lax.all_gather(
        (values * scale[:, None]).astype(jnp.bfloat16), "mp", axis=1, tiled=True
    )
    return (normed, scale)


def outer_update(received, anchor_rows, momentum_rows, old_columns, new_columns):
    groups_count = received.shape[0]
    levels_count = received.shape[1]
    module_count = anchor_rows.shape[0]
    offsets = jnp.arange(levels_count, dtype=jnp.int32) * MODS
    old_index = (old_columns + offsets[None, :]).reshape(-1)
    selector = (old_index[None, :] == jnp.arange(module_count, dtype=jnp.int32)[:, None]).astype(
        jnp.float32
    )
    sums = jnp.dot(
        selector, received.reshape(groups_count * levels_count, -1), precision=lax.Precision.HIGHEST
    )
    counts = jnp.sum(selector, axis=1)
    outer_grad = (sums / counts[:, None]).reshape(anchor_rows.shape)
    new_momentum = momentum_rate * momentum_rows + outer_grad
    new_anchor = anchor_rows - outer_rate * (outer_grad + momentum_rate * new_momentum)
    new_index = new_columns + offsets[None, :]
    outgoing = jnp.take(new_anchor, new_index, axis=0).astype(jnp.bfloat16)
    return (new_anchor, new_momentum, outgoing)


def shards(anchor, momentum, deltas, old_path, new_path, tokens, cotangent):
    factor = 1.0 / math.sqrt(D)
    first_state = tokens[0]
    upstream = cotangent[0].astype(jnp.float32)
    first_normed, first_scale = normalize(first_state)
    anchor_parts = []
    momentum_parts = []
    weight_parts = []
    for level in range(LEVELS):
        received = lax.all_to_all(
            deltas[:, level : level + 1].astype(jnp.bfloat16),
            "group",
            split_axis=2,
            concat_axis=0,
            tiled=True,
        ).astype(jnp.float32)
        part_anchor, part_momentum, outgoing = outer_update(
            received,
            anchor[level * MODS : (level + 1) * MODS],
            momentum[level * MODS : (level + 1) * MODS],
            old_path[:, level : level + 1],
            new_path[:, level : level + 1],
        )
        loaded = lax.all_to_all(outgoing, "group", split_axis=0, concat_axis=2, tiled=True)
        anchor_parts.append(part_anchor)
        momentum_parts.append(part_momentum)
        weight_parts.append(loaded[0, 0])
    new_anchor = jnp.concatenate(anchor_parts, axis=0)
    new_momentum = jnp.concatenate(momentum_parts, axis=0)
    first_weight = weight_parts[0]
    second_weight = weight_parts[1]
    first_pre = jnp.dot(first_normed, first_weight, preferred_element_type=jnp.float32) * factor
    second_state = (first_state.astype(jnp.float32) + jax.nn.silu(first_pre)).astype(jnp.bfloat16)
    second_normed, second_scale = normalize(second_state)
    second_pre = jnp.dot(second_normed, second_weight, preferred_element_type=jnp.float32) * factor
    second_slope = (upstream * silu_slope(second_pre)).astype(jnp.bfloat16)
    second_grad = (
        lax.dot_general(
            second_normed,
            second_slope,
            (((0,), (0,)), ((), ())),
            preferred_element_type=jnp.float32,
        )
        * factor
    ).astype(jnp.bfloat16)
    terms = (
        lax.dot_general(
            second_slope,
            second_weight,
            (((1,), (1,)), ((), ())),
            preferred_element_type=jnp.float32,
        )
        * factor
    )
    normed_grad = lax.psum_scatter(
        terms.astype(jnp.bfloat16), "mp", scatter_dimension=1, tiled=True
    ).astype(jnp.float32)
    middle = second_state.astype(jnp.float32)
    inner = lax.psum(jnp.sum(normed_grad * middle, axis=-1), "mp")
    state_grad = (
        upstream
        + second_scale[:, None] * normed_grad
        - middle * (second_scale**3 * inner / D)[:, None]
    )
    first_slope = (state_grad * silu_slope(first_pre)).astype(jnp.bfloat16)
    first_grad = (
        lax.dot_general(
            first_normed, first_slope, (((0,), (0,)), ((), ())), preferred_element_type=jnp.float32
        )
        * factor
    ).astype(jnp.bfloat16)
    grads = jnp.stack([first_grad, second_grad])[None]
    return (new_anchor, new_momentum, grads)


def solution(mesh):
    in_specs = (
        P(None, "group", "mp"),
        P(None, "group", "mp"),
        P("group", None, None, "mp"),
        P(),
        P(),
        P("group", None, "mp"),
        P("group", None, "mp"),
    )
    out_specs = (P(None, "group", "mp"), P(None, "group", "mp"), P("group", None, None, "mp"))
    return jax.shard_map(shards, mesh=mesh, in_specs=in_specs, out_specs=out_specs, check_vma=False)
```

profile of v0, /device:TPU:16, one launch (start us, length us, event | category | flops | bytes accessed | tf_op | source)
XLA Modules:
  0.0 661.7 jit_solution(7644956937958381356)
XLA Ops:
  7.2 27.6 %copy.56 = bf16[1,2,2048,1024]{3,1,0,2:T(2,128)(2,1)S(1)} copy(f32[1,2,2048,1024]{3,2,1,0:T(8,128)} %param.11) | data formatting | bytes 25165824 | tf_op args[2]
  34.8 13.0 %fusion.24 = (bf16[1,1,2048,1024]{3,1,0,2:T(2,128)(2,1)}, bf16[1,1,2048,1024]{3,1,0,2:T(2,128)(2,1)}) fusion(bf16[1,2,2048,1024]{3,1,0,2:T(2,128)(2,1)S(1)} %copy.56), kind=kLoop, calls=%fused_computation.65 | loop fusion | bytes 16777216 | tf_op jit(solution)/shard_map/slice | solution.py:64
  47.9 0.5 broadcast.141
  48.4 26.0 %reduce.4 = bf16[2048,1024]{1,0:T(8,128)(2,1)} reduce(bf16[2048,1,1,1024]{3,2,1,0:T(2,128)(2,1)} %bitcast.59, bf16[]{:T(256)} %broadcast.141), dimensions={1,2}, to_apply=%bitcast.42.reduce_sub_computation | reduce | bytes 8388610
  74.4 11.4 %reshape.98 = bf16[16,2,65536]{2,1,0:T(2,128)(2,1)} reshape(bf16[2048,1024]{1,0:T(8,128)(2,1)} %reduce.4) | data formatting | bytes 8388608
  85.7 6.2 all-to-all-start
  91.9 26.0 %reduce.5 = bf16[2048,1024]{1,0:T(8,128)(2,1)} reduce(bf16[2048,1,1,1024]{3,2,1,0:T(2,128)(2,1)} %bitcast.58, bf16[]{:T(256)} %broadcast.141), dimensions={1,2}, to_apply=%bitcast.40.reduce_sub_computation | reduce | bytes 8388610
  117.9 11.4 %reshape.96 = bf16[16,2,65536]{2,1,0:T(2,128)(2,1)} reshape(bf16[2048,1024]{1,0:T(8,128)(2,1)} %reduce.5) | data formatting | bytes 8388608
  129.3 55.3 %all-to-all-done = bf16[16,2,65536]{2,1,0:T(2,128)(2,1)} async-done(((bf16[16,2,65536]{2,1,0:T(2,128)(2,1)}), bf16[16,2,65536]{2,1,0:T(2,128)(2,1)}, u32[]{:S(2)}, u32[]{:S(2)}) %all-to-all-start) | async-done | bytes 4194336 | tf_op jit(solution)/shard_map/all_to_all | solution.py:63
  184.6 5.0 all-to-all-start.1
  189.6 0.0 copy-done.6
  189.6 0.1 convert_reduce_fusion
  189.8 0.0 copy-done.5
  189.8 12.3 %reshape.99 = bf16[2048,1,1,1024]{3,2,1,0:T(2,128)(2,1)} reshape(bf16[16,2,65536]{2,1,0:T(2,128)(2,1)} %all-to-all-done) | data formatting | bytes 8388608
  202.1 27.8 %bitcast_reduce_fusion = bf16[2048,1024]{1,0:T(8,128)(2,1)} fusion(bf16[2048,1,1,1024]{3,2,1,0:T(2,128)(2,1)} %reshape.99), kind=kLoop, calls=%fused_computation.66 | loop fusion | bytes 8388608 | tf_op jit(solution)/shard_map/all_to_all | solution.py:63
  229.9 4.8 reshape.62
  234.7 47.4 %all-to-all-done.1 = bf16[16,2,65536]{2,1,0:T(2,128)(2,1)} async-done(((bf16[16,2,65536]{2,1,0:T(2,128)(2,1)}), bf16[16,2,65536]{2,1,0:T(2,128)(2,1)}, u32[]{:S(2)}, u32[]{:S(2)}) %all-to-all-start.1) | async-done | bytes 4194336 | tf_op jit(solution)/shard_map/all_to_all | solution.py:63
  282.1 12.3 %reshape.97 = bf16[2048,1,1,1024]{3,2,1,0:T(2,128)(2,1)} reshape(bf16[16,2,65536]{2,1,0:T(2,128)(2,1)} %all-to-all-done.1) | data formatting | bytes 8388608
  294.4 27.8 %bitcast_reduce_fusion.1 = bf16[2048,1024]{1,0:T(8,128)(2,1)} fusion(bf16[2048,1,1,1024]{3,2,1,0:T(2,128)(2,1)} %reshape.97), kind=kLoop, calls=%fused_computation.67 | loop fusion | bytes 8388608 | tf_op jit(solution)/shard_map/all_to_all | solution.py:63
  322.2 4.8 reshape.64
  327.1 3.0 convolution_divide_fusion.1
  330.1 0.0 slice-start
  330.1 0.4 copy-done.3
  330.5 2.8 convolution_divide_fusion
  333.3 0.0 slice-done
  333.3 1.7 slice-done.1
  335.1 13.7 %multiply_subtract_fusion.1 = (f32[8,128,1024]{2,1,0:T(8,128)}, f32[8,128,1024]{2,1,0:T(8,128)}, f32[8,128,1024]{2,1,0:T(8,128)}, f32[8,128,1024]{2,1,0:T(8,128)}) fusion(f32[16,128,1024]{2,1,0:T(8,128)S(1)} %bitcast.61, f32[8,128,1024]{2,0,1:T(8,128)S(1)} %bitcast.62, f32[16,128,1024]{2,1,0:T(8,128)} %param.10, f32[8,128,1024]{2,0,1:T(8,128)} %bitcast.63), kind=kLoop, calls=%fused_computation.38 | loop fusion | flops 12582912 | bytes 41943040 | tf_op jit(solution)/shard_map/sub | solution.py:48
  348.8 5.2 gather_fusion
  353.9 5.7 fusion.1
  359.6 4.7 all-to-all-start.2
  364.3 0.0 all-gather.3.cloned.1.call-start
  364.4 2.9 copy.41
  367.2 0.5 fusion.6
  367.7 4.9 psum.21
  372.7 1.9 fusion.7
  374.6 0.0 all-gather.3.cloned.1.call-update
  374.6 5.2 gather_fusion.1
  379.8 5.8 fusion
  385.6 71.4 %all-to-all-done.2 = bf16[16,1,128,1024]{3,2,1,0:T(8,128)(2,1)} async-done(((bf16[16,1,128,1024]{3,2,1,0:T(8,128)(2,1)}), bf16[16,1,128,1024]{3,2,1,0:T(8,128)(2,1)}, u32[]{:S(2)}, u32[]{:S(2)}) %all-to-all-start.2) | async-done | bytes 4194336 | tf_op jit(solution)/shard_map/all_to_all | solution.py:77
  457.0 4.7 all-to-all-start.3
  461.7 0.4 all-gather.5.cloned.1.call-start
  462.1 0.0 all-gather.3.cloned.1.call-done
  462.2 12.0 %fusion.9 = (f32[1024]{0:T(1024)S(1)}, bf16[1024,1024]{0,1:T(8,128)(2,1)}, f32[1024,1024]{0,1:T(8,128)}) fusion(bf16[1,1024,1024]{1,2,0:T(8,128)(2,1)S(1)} %copy.41, bf16[1024,2048]{0,1:T(8,128)(2,1)} %all-gather.3.cloned.1.call-done, bf16[2048,1024]{1,0:T(8,128)(2,1)} %bitcast.10), kind=kOutput, calls=%fused_computation.32 | convolution fusion | flops 4306500608 | bytes 16781312 | tf_op jit(solution)/shard_map/dot_general | solution.py:85
  474.2 5.0 psum.22
  479.2 3.5 fusion.10
  482.7 0.0 all-gather.5.cloned.1.call-update
  482.8 0.2 reduce-scatter.2.cloned.1.call-start
  483.0 0.0 copy-done.4
  483.0 2.6 copy.42
  485.6 68.8 %all-to-all-done.3 = bf16[16,1,128,1024]{3,2,1,0:T(8,128)(2,1)} async-done(((bf16[16,1,128,1024]{3,2,1,0:T(8,128)(2,1)}), bf16[16,1,128,1024]{3,2,1,0:T(8,128)(2,1)}, u32[]{:S(2)}, u32[]{:S(2)}) %all-to-all-start.3) | async-done | bytes 4194336 | tf_op jit(solution)/shard_map/all_to_all | solution.py:77
  554.4 10.1 %fusion.2 = bf16[1024,1024]{0,1:T(8,128)(2,1)S(1)} fusion(bf16[1024,2048]{0,1:T(8,128)(2,1)} %all-gather.5.cloned.1.call-done, bf16[2048,1024]{1,0:T(8,128)(2,1)} %bitcast.15, bf16[1,1024,1024]{1,2,0:T(8,128)(2,1)} %copy.42), kind=kOutput, calls=%fused_computation.25 | convolution fusion | flops 4306501632 | bytes 12582912 | tf_op jit(solution)/shard_map/dot_general | solution.py:88
  564.5 0.0 copy-start.7
  564.5 1.3 copy-done.7
  565.8 8.3 %multiply_convert_fusion.2 = bf16[1024,2048]{0,1:T(8,128)(2,1)} fusion(bf16[2048,1024]{1,0:T(8,128)(2,1)} %bitcast.15, bf16[1024,1024]{0,1:T(8,128)(2,1)S(1)} %fusion.2), kind=kOutput, calls=%fused_computation.14 | convolution fusion | flops 4299161600 | bytes 10485760 | tf_op jit(solution)/shard_map/dot_general | solution.py:100
  574.2 0.0 reduce-scatter.2.cloned.1.call-update
  574.2 8.7 %pad_maximum_fusion = f32[16,128,1024]{2,1,0:T(8,128)} fusion(f32[8,128,1024]{2,1,0:T(8,128)} %get-tuple-element.7, f32[8,128,1024]{2,1,0:T(8,128)} %get-tuple-element.6), kind=kLoop, calls=%fused_computation.5 | loop fusion | flops 2097152 | bytes 16777216 | tf_op jit(solution)/shard_map/concatenate | solution.py:81
  582.9 0.0 copy-done.1
  582.9 4.3 pad_maximum_fusion.1
  587.1 8.9 %fusion.13 = bf16[1,2048,1024]{2,1,0:T(8,128)(2,1)} fusion(bf16[1024,2048]{0,1:T(8,128)(2,1)} %all-gather.5.cloned.1.call-done, bf16[1024,1024]{0,1:T(8,128)(2,1)S(1)} %copy-done.8), kind=kOutput, calls=%fused_computation.41 | convolution fusion | flops 4299161600 | bytes 10485760 | tf_op jit(solution)/shard_map/dot_general | solution.py:91
  596.1 32.2 %reduce-scatter.2.cloned.1.call-done = bf16[1024,1024]{0,1:T(8,128)(2,1)} async-done(((bf16[1024,2048]{0,1:T(8,128)(2,1)}), bf16[1024,1024]{0,1:T(8,128)(2,1)}) %reduce-scatter.2.cloned.1.call-update) | async-done | bytes 2097168 | tf_op jit(solution)/shard_map/reduce_scatter | solution.py:108
  628.2 2.5 fusion.11
  630.7 4.9 psum.23
  635.6 11.7 %fusion.12 = bf16[1,2048,1024]{2,1,0:T(8,128)(2,1)} fusion(bf16[1024,2048]{0,1:T(8,128)(2,1)} %all-gather.3.cloned.1.call-done, bf16[1024,1024]{0,1:T(8,128)(2,1)} %reduce-scatter.2.cloned.1.call-done, bf16[1024,1024]{0,1:T(8,128)(2,1)S(1)} %copy-done.2, f32[1024,1024]{0,1:T(8,128)} %get-tuple-element.18, bf16[1,1024,1024]{1,2,0:T(8,128)(2,1)} %copy.42, ...), kind=kOutput, calls=%fused_computation.40 | convolution fusion | flops 4316987392 | bytes 18882560 | tf_op jit(solution)/shard_map/dot_general | solution.py:120
  647.4 7.6 %maximum_bitcast_fusion = bf16[1,2,2048,1024]{3,2,1,0:T(8,128)(2,1)} fusion(bf16[1,2048,1024]{2,1,0:T(8,128)(2,1)} %fusion.13, bf16[1,2048,1024]{2,1,0:T(8,128)(2,1)} %fusion.12), kind=kLoop, calls=%fused_computation.7 | loop fusion | flops 4194304 | bytes 16777216 | tf_op jit(solution)/shard_map/broadcast_in_dim | solution.py:125
  (21 shorter events, 0.1 us)
Async XLA Ops:
  85.7 98.9 %all-to-all-start = ((bf16[16,2,65536]{2,1,0:T(2,128)(2,1)}), bf16[16,2,65536]{2,1,0:T(2,128)(2,1)}, u32[]{:S(2)}, u32[]{:S(2)}) async-start(bf16[16,2,65536]{2,1,0:T(2,128)(2,1)} %reshape.98), calls=%async_computation | async-start | bytes 8388608 | tf_op jit(solution)/shard_map/all_to_all | solution.py:63
  129.3 60.3 %copy-start.6 = (s32[16,2]{0,1:T(2,128)S(1)}, s32[16,2]{0,1:T(2,128)}, u32[]{:S(2)}) copy-start(s32[16,2]{0,1:T(2,128)} %param.12) | copy-start | bytes 388
  129.3 60.5 %copy-start.5 = (s32[16,2]{0,1:T(2,128)S(1)}, s32[16,2]{0,1:T(2,128)}, u32[]{:S(2)}) copy-start(s32[16,2]{0,1:T(2,128)} %param.13) | copy-start | bytes 388
  184.6 97.5 %all-to-all-start.1 = ((bf16[16,2,65536]{2,1,0:T(2,128)(2,1)}), bf16[16,2,65536]{2,1,0:T(2,128)(2,1)}, u32[]{:S(2)}, u32[]{:S(2)}) async-start(bf16[16,2,65536]{2,1,0:T(2,128)(2,1)} %reshape.96), calls=%async_computation.1 | async-start | bytes 8388608 | tf_op jit(solution)/shard_map/all_to_all | solution.py:63
  327.1 3.4 copy-start.3
  330.1 3.2 slice-start
  330.5 4.6 slice-start.1
  359.6 97.4 %all-to-all-start.2 = ((bf16[16,1,128,1024]{3,2,1,0:T(8,128)(2,1)}), bf16[16,1,128,1024]{3,2,1,0:T(8,128)(2,1)}, u32[]{:S(2)}, u32[]{:S(2)}) async-start(bf16[16,1,128,1024]{3,2,1,0:T(8,128)(2,1)} %fusion.1), calls=%async_computation.2 | async-start | bytes 8388608 | tf_op jit(solution)/shard_map/all_to_all | solution.py:77
  364.3 97.8 %all-gather.3.cloned.1.call-start = ((), (), s32[]{:S(2)}) async-start(), calls=%async_computation.5 | async-start | bytes 6291456 | tf_op jit(solution)/shard_map/all_gather | solution.py:27
  457.0 97.4 %all-to-all-start.3 = ((bf16[16,1,128,1024]{3,2,1,0:T(8,128)(2,1)}), bf16[16,1,128,1024]{3,2,1,0:T(8,128)(2,1)}, u32[]{:S(2)}, u32[]{:S(2)}) async-start(bf16[16,1,128,1024]{3,2,1,0:T(8,128)(2,1)} %fusion), calls=%async_computation.3 | async-start | bytes 8388608 | tf_op jit(solution)/shard_map/all_to_all | solution.py:77
  461.7 92.7 %all-gather.5.cloned.1.call-start = ((), (), s32[]{:S(2)}) async-start(), calls=%async_computation.6 | async-start | bytes 6291456 | tf_op jit(solution)/shard_map/all_gather | solution.py:27
  474.2 8.8 %copy-start.4 = (bf16[1,1024,1024]{2,1,0:T(8,128)(2,1)S(1)}, bf16[1,1024,1024]{2,1,0:T(8,128)(2,1)}, u32[]{:S(2)}) copy-start(bf16[1,1024,1024]{2,1,0:T(8,128)(2,1)} %param.15) | copy-start | bytes 6291460
  482.8 145.4 %reduce-scatter.2.cloned.1.call-start = ((), (), s32[]{:S(2)}) async-start(), calls=%async_computation.7 | async-start | bytes 6291456 | tf_op jit(solution)/shard_map/reduce_scatter | solution.py:108
  564.5 1.3 copy-start.7
  574.2 8.7 %copy-start = (f32[8,128,1024]{2,1,0:T(8,128)S(1)}, f32[8,128,1024]{2,1,0:T(8,128)}, u32[]{:S(2)}) copy-start(f32[8,128,1024]{2,1,0:T(8,128)} %get-tuple-element.8) | copy-start | bytes 12582916
  574.2 8.7 %copy-start.1 = (f32[8,128,1024]{2,1,0:T(8,128)S(1)}, f32[8,128,1024]{2,1,0:T(8,128)}, u32[]{:S(2)}) copy-start(f32[8,128,1024]{2,1,0:T(8,128)} %get-tuple-element.9) | copy-start | bytes 12582916
  582.9 4.3 copy-start.8
  587.1 41.1 %copy-start.2 = (bf16[1024,1024]{0,1:T(8,128)(2,1)S(1)}, bf16[1024,1024]{0,1:T(8,128)(2,1)}, u32[]{:S(2)}) copy-start(bf16[1024,1024]{0,1:T(8,128)(2,1)} %get-tuple-element.5) | copy-start | bytes 6291460
Sparse Core Ops, SparseCore 0:
  374.7 57.6 all-gather.2
  482.9 57.6 all-gather.4
  574.3 53.8 reduce-scatter.1
where the time goes:
time: 671 us; the launch traced here: 662 us
  waiting for transfers between devices  275 us (41%)
  local copies, waits for them, and re-layouts  173 us (26%)
  other arithmetic  106 us (16%)
  matrix products  56.9 us (8%)
  starting transfers between devices  21.2 us (3%)
  blocking collectives  14.9 us (2%)
  between operations  14.1 us (2%)
    all_to_all x2, waiting for transfers between devices, shards(): lax.all_to_all(outgoing, 'group', split_axis=0, concat_axis=2, tiled=True)  140 us
    all_to_all x2, waiting for transfers between devices, shards(): lax.all_to_all(deltas[:, level:level + 1].astype(jnp.bfloat16), 'group',...  103 us
    unnamed x30, local copies, waits for them, and re-layouts  84.5 us
    all_to_all x2, local copies, waits for them, and re-layouts, shards(): lax.all_to_all(deltas[:, level:level + 1].astype(jnp.bfloat16), 'group',...  55.6 us
    unnamed x3, other arithmetic  52 us
    reduce_scatter x1, waiting for transfers between devices, shards(): lax.psum_scatter(terms.astype(jnp.bfloat16), 'mp', scatter_dimension=1, t...  32.2 us
    sub x1, other arithmetic, outer_update(): anchor_rows - outer_rate * (outer_grad + momentum_rate * new_momentum)  13.7 us
  transfers between devices with their start and end apart: 7, of which 5 were waited for; matrix products, arithmetic and copies ran while one was open for 21% of the time, Pallas kernels for 0%

commit v1 on v0

v1 whole, which is shorter than its diff:
```python
import functools
import math

import jax
import jax.numpy as jnp
from jax import lax
from jax.experimental import pallas as pl
from jax.experimental.pallas import tpu as pltpu
from jax.sharding import PartitionSpec as P

outer_rate = 0.7
momentum_rate = 0.9
epsilon = 1e-06

VMEM = 60 * 1024 * 1024
TAIL_CHUNKS = 4

f32 = jnp.float32
bf16 = jnp.bfloat16


def params(**kw):
    return pltpu.CompilerParams(vmem_limit_bytes=VMEM, **kw)


def silu_slope(values):
    sigmoid_part = jax.nn.sigmoid(values)
    return sigmoid_part * (1.0 + values * (1.0 - sigmoid_part))


def cast_kernel(src, dst):
    dst[...] = src[...].reshape(dst.shape).astype(dst.dtype)


def cast_level(deltas, level, groups):
    _, _, depth, columns = deltas.shape
    rows = depth // groups
    per = 2 if groups % 2 == 0 else 1
    return pl.pallas_call(
        cast_kernel,
        grid=(groups // per,),
        in_specs=[pl.BlockSpec((1, 1, per * rows, columns), lambda i: (0, level, i, 0))],
        out_specs=pl.BlockSpec((per, rows, columns), lambda i: (i, 0, 0)),
        out_shape=jax.ShapeDtypeStruct((groups, rows, columns), bf16),
        compiler_params=params(),
        cost_estimate=pl.CostEstimate(
            flops=0, bytes_accessed=depth * columns * 6, transcendentals=0
        ),
    )(deltas)


def update_kernel(groups, mods, aliased, old, new, received, anchor, momentum, *rest):
    new_anchor, new_momentum, outgoing, total = rest[2:] if aliased else rest
    total[...] = jnp.zeros_like(total)
    for g in range(groups):
        m = old[g]
        total[m] = total[m] + received[g].astype(f32)
    for m in range(mods):
        count = jnp.int32(0)
        for g in range(groups):
            count = count + jnp.where(old[g] == m, 1, 0)
        outer_grad = total[m] / count.astype(f32)
        moved = momentum_rate * momentum[m] + outer_grad
        new_momentum[m] = moved
        total[m] = anchor[m] - outer_rate * (outer_grad + momentum_rate * moved)
        new_anchor[m] = total[m]
    for g in range(groups):
        outgoing[g] = total[new[g]].astype(outgoing.dtype)


def outer_update(received, anchor, momentum, old, new, level, levels, previous):
    groups, rows, columns = received.shape
    modules = anchor.shape[0]
    mods = modules // levels
    tile = 32 if rows % 32 == 0 else rows
    state = pl.BlockSpec((mods, tile, columns), lambda i, *_: (level, i, 0))
    block = pl.BlockSpec((groups, tile, columns), lambda i, *_: (0, i, 0))
    anywhere = pl.BlockSpec(memory_space=pl.ANY)
    aliased = previous is not None
    whole = jax.ShapeDtypeStruct(anchor.shape, f32)
    return pl.pallas_call(
        functools.partial(update_kernel, groups, mods, aliased),
        grid_spec=pltpu.PrefetchScalarGridSpec(
            num_scalar_prefetch=2,
            grid=(rows // tile,),
            in_specs=[block, state, state] + ([anywhere, anywhere] if aliased else []),
            out_specs=[state, state, block],
            scratch_shapes=[pltpu.VMEM((mods, tile, columns), f32)],
        ),
        out_shape=[whole, whole, jax.ShapeDtypeStruct(received.shape, bf16)],
        input_output_aliases={5: 0, 6: 1} if aliased else {},
        compiler_params=params(),
        cost_estimate=pl.CostEstimate(
            flops=0,
            bytes_accessed=rows * columns * (groups * 4 + mods * 16),
            transcendentals=0,
        ),
    )(old, new, received, anchor, momentum, *(previous or ()))


def grad_kernel(factor, aliased, normed, slope, *rest):
    out = rest[-1]
    product = lax.dot_general(
        normed[...], slope[...], (((0,), (0,)), ((), ())), preferred_element_type=f32
    )
    out[...] = (product * factor).astype(out.dtype).reshape(out.shape)


def level_grad(normed, slope, factor, level, levels, previous):
    rows, depth = normed.shape
    columns = slope.shape[1]
    tile = min(512, depth)
    aliased = previous is not None
    return pl.pallas_call(
        functools.partial(grad_kernel, factor, aliased),
        grid=(depth // tile,),
        in_specs=[
            pl.BlockSpec((rows, tile), lambda i: (0, i)),
            pl.BlockSpec((rows, columns), lambda i: (0, 0)),
        ]
        + ([pl.BlockSpec(memory_space=pl.ANY)] if aliased else []),
        out_specs=pl.BlockSpec((1, 1, tile, columns), lambda i: (0, level, i, 0)),
        out_shape=jax.ShapeDtypeStruct((1, levels, depth, columns), bf16),
        input_output_aliases={2: 0} if aliased else {},
        compiler_params=params(),
        cost_estimate=pl.CostEstimate(
            flops=2 * rows * depth * columns,
            bytes_accessed=2 * (rows * depth + rows * columns + depth * columns),
            transcendentals=0,
        ),
    )(normed, slope, *((previous,) if aliased else ()))


def gathered(own):
    return lax.all_gather(own, "mp", axis=1, tiled=True)


def normalize(whole):
    values = whole.astype(f32)
    scale = lax.rsqrt(jnp.mean(values * values, axis=-1, keepdims=True) + epsilon)
    return (values * scale).astype(bf16), scale


def shards(anchor, momentum, deltas, old_path, new_path, tokens, cotangent):
    groups = lax.axis_size("group")
    parts = lax.axis_size("mp")
    place = lax.axis_index("mp")
    levels = deltas.shape[1]
    depth = deltas.shape[2]
    columns = deltas.shape[3]
    factor = 1.0 / math.sqrt(depth)

    def exchange(blocks):
        return lax.all_to_all(blocks, "group", split_axis=0, concat_axis=0, tiled=True)

    received = [exchange(cast_level(deltas, level, groups)) for level in range(levels)]
    first_normed, _ = normalize(gathered(tokens[0]))

    previous = None
    loaded = []
    for level in range(levels):
        part_anchor, part_momentum, outgoing = outer_update(
            received[level],
            anchor,
            momentum,
            old_path[:, level],
            new_path[:, level],
            level,
            levels,
            previous,
        )
        previous = (part_anchor, part_momentum)
        loaded.append(exchange(outgoing).reshape(depth, columns))
    new_anchor, new_momentum = previous
    first_weight, second_weight = loaded

    first_state = tokens[0].astype(f32)
    upstream = cotangent[0].astype(f32)
    first_pre = jnp.dot(first_normed, first_weight, preferred_element_type=f32) * factor
    second_state = (first_state + jax.nn.silu(first_pre)).astype(bf16)
    second_normed, second_scale = normalize(gathered(second_state))

    rows = second_state.shape[0]
    run = rows // TAIL_CHUNKS
    own_features = depth // parts
    split_weight = second_weight.reshape(parts, own_features, columns)
    slopes, kept, arriving = [], [], []
    for r in range(TAIL_CHUNKS):
        here = slice(r * run, (r + 1) * run)
        pre = jnp.dot(second_normed[here], second_weight, preferred_element_type=f32) * factor
        slope = (upstream[here] * silu_slope(pre)).astype(bf16)
        dot = jnp.sum(slope.astype(f32) * pre, axis=-1)
        slopes.append((slope, dot))
        terms = []
        for step in range(parts):
            owner = lax.rem(place + step, parts)
            weight = lax.dynamic_index_in_dim(split_weight, owner, 0, keepdims=False)
            term = lax.dot_general(
                slope, weight, (((1,), (1,)), ((), ())), preferred_element_type=f32
            )
            terms.append((term * factor).astype(bf16))
        kept.append(terms[0])
        arriving.append(
            [
                lax.ppermute(
                    terms[step], "mp", [(p, (p + step) % parts) for p in range(parts)]
                )
                for step in range(1, parts)
            ]
        )
    inner = jnp.concatenate([dot for _, dot in slopes], axis=0)
    inner = lax.psum(inner, "mp")[:, None] / second_scale
    second_slope = jnp.concatenate([slope for slope, _ in slopes], axis=0)
    grads = level_grad(second_normed, second_slope, factor, 1, levels, None)
    first_slopes = []
    for r in range(TAIL_CHUNKS):
        here = slice(r * run, (r + 1) * run)
        normed_grad = kept[r].astype(f32)
        for term in arriving[r]:
            normed_grad = normed_grad + term.astype(f32)
        scale = second_scale[here]
        state_grad = (
            upstream[here]
            + scale * normed_grad
            - second_state[here].astype(f32) * (scale**3 * inner[here] / depth)
        )
        first_slopes.append((state_grad * silu_slope(first_pre[here])).astype(bf16))
    first_slope = jnp.concatenate(first_slopes, axis=0)
    grads = level_grad(first_normed, first_slope, factor, 0, levels, grads)
    return (new_anchor, new_momentum, grads)


def solution(mesh):
    in_specs = (
        P(None, "group", "mp"),
        P(None, "group", "mp"),
        P("group", None, None, "mp"),
        P(),
        P(),
        P("group", None, "mp"),
        P("group", None, "mp"),
    )
    out_specs = (P(None, "group", "mp"), P(None, "group", "mp"), P("group", None, None, "mp"))
    return jax.shard_map(shards, mesh=mesh, in_specs=in_specs, out_specs=out_specs, check_vma=False)
```

time: 671 us -> 509 us (0.76)
  local copies, waits for them, and re-layouts: 173 us -> 3.1 us
  other arithmetic: 106 us -> 15.4 us
  Pallas kernels: 0 us -> 54.2 us
  waiting for transfers between devices: 275 us -> 329 us
    unnamed x30 -> x24, local copies, waits for them, and re-layouts: 84.5 us -> 2.48 us
    all_to_all x2 -> x0, local copies, waits for them, and re-layouts: 55.6 us -> none  [shards(): lax.all_to_all(deltas[:, level:level + 1].astype(jnp.bfloat16), 'group',...]
    all_gather x2, waiting for transfers between devices: 0.02 us -> 55.4 us  [gathered(): return lax.all_gather(own, 'mp', axis=1, tiled=True)]
    pallas_call x0 -> x6, Pallas kernels: none -> 54.2 us  [the longest x2 22 us: outer_update(): pl.pallas_call(functools.partial(update_kernel, groups, mods, aliased), g...]
    unnamed x3 -> x0, other arithmetic: 52 us -> none
    reduce_scatter x1 -> x0, waiting for transfers between devices: 32.2 us -> none  [shards(): lax.psum_scatter(terms.astype(jnp.bfloat16), 'mp', scatter_dimension=1, t...]
    all_to_all x4, waiting for transfers between devices: 243 us -> 260 us  [exchange(): lax.all_to_all(blocks, 'group', split_axis=0, concat_axis=0, tiled=True)]
    sub x1 -> x0, other arithmetic: 13.7 us -> none  [outer_update(): anchor_rows - outer_rate * (outer_grad + momentum_rate * new_momentum)]
  transfers between devices with their start and end apart: 7 -> 10, of which waited for: 5 -> 7; matrix products, arithmetic and copies ran while one was open for 21% -> 6% of each run, Pallas kernels for 0% -> 8%
where the time goes in v1:
time: 509 us; the launch traced here: 506 us
  waiting for transfers between devices  329 us (65%)
  Pallas kernels  54.2 us (11%)
  matrix products  52.5 us (10%)
  starting transfers between devices  25.4 us (5%)
  other arithmetic  15.4 us (3%)
  between operations  14.3 us (3%)
  blocking collectives  12.3 us (2%)
    all_to_all x4, waiting for transfers between devices, exchange(): lax.all_to_all(blocks, 'group', split_axis=0, concat_axis=0, tiled=True)  260 us
    all_gather x2, waiting for transfers between devices, gathered(): return lax.all_gather(own, 'mp', axis=1, tiled=True)  55.4 us
    dot_general x8, matrix products, shards(): lax.dot_general(slope, weight, (((1,), (1,)), ((), ())), preferred_elemen...  25.2 us
    pallas_call x2, Pallas kernels, outer_update(): pl.pallas_call(functools.partial(update_kernel, groups, mods, aliased), g...  22 us
    all_to_all x4, starting transfers between devices, exchange(): lax.all_to_all(blocks, 'group', split_axis=0, concat_axis=0, tiled=True)  20.2 us
    dot_general x4, matrix products, shards(): jnp.dot(second_normed[here], second_weight, preferred_element_type=f32)  17.2 us
    pallas_call x2, Pallas kernels, level_grad(): pl.pallas_call(functools.partial(grad_kernel, factor, aliased), grid=(dep...  16.9 us
    pallas_call x2, Pallas kernels, cast_level(): pl.pallas_call(cast_kernel, grid=(groups // per,), in_specs=[pl.BlockSpec...  15.4 us
  transfers between devices with their start and end apart: 10, of which 7 were waited for; matrix products, arithmetic and copies ran while one was open for 6% of the time, Pallas kernels for 8%

profile of v1, /device:TPU:16, one launch (start us, length us, event | category | flops | bytes accessed | tf_op | source)
XLA Modules:
  0.0 506.4 jit_solution(11970252905565511955)
XLA Ops:
  7.2 7.7 %shard_map.95 = bf16[16,128,1024]{2,1,0:T(8,128)(2,1)} custom-call(f32[1,2,2048,1024]{3,2,1,0:T(8,128)} %src.3), custom_call_target="tpu_custom_call" | custom-call | bytes 12582912 | tf_op jit(solution)/shard_map/pallas_call | solution.py:39
  14.9 6.2 %all-to-all-start.1 = ((bf16[16,128,1024]{2,1,0:T(8,128)(2,1)}), bf16[16,128,1024]{2,1,0:T(8,128)(2,1)}, u32[]{:S(2)}, u32[]{:S(2)}) async-start(bf16[16,128,1024]{2,1,0:T(8,128)(2,1)} %shard_map.95), calls=%async_computation.1 | async-start | bytes 8388608 | tf_op jit(solution)/shard_map/all_to_all | solution.py:154
  21.0 7.7 %shard_map.94 = bf16[16,128,1024]{2,1,0:T(8,128)(2,1)} custom-call(f32[1,2,2048,1024]{3,2,1,0:T(8,128)} %src.3), custom_call_target="tpu_custom_call" | custom-call | bytes 12582912 | tf_op jit(solution)/shard_map/pallas_call | solution.py:39
  28.7 85.0 %all-to-all-done.1.received = bf16[16,128,1024]{2,1,0:T(8,128)(2,1)} async-done(((bf16[16,128,1024]{2,1,0:T(8,128)(2,1)}), bf16[16,128,1024]{2,1,0:T(8,128)(2,1)}, u32[]{:S(2)}, u32[]{:S(2)}) %all-to-all-start.1) | async-done | bytes 4194336 | tf_op jit(solution)/shard_map/all_to_all | solution.py:154
  113.7 4.7 all-to-all-start
  118.4 0.0 copy-done.9
  118.4 0.0 copy-done.10
  118.4 0.6 slice_bitcast_fusion.4
  119.0 10.8 %shard_map.96 = (f32[16,128,1024]{2,1,0:T(8,128)}, f32[16,128,1024]{2,1,0:T(8,128)}, bf16[16,128,1024]{2,1,0:T(8,128)(2,1)}) custom-call(s32[16]{0:T(128)} %get-tuple-element.44.old, s32[16]{0:T(128)} %get-tuple-element.37.new, bf16[16,128,1024]{2,1,0:T(8,128)(2,1)} %all-to-all-done.1.received, f32[16,128,1024]{2,1,0:T(8,128)} %anchor.3, ...), custom_call_target="tpu_custom_call" | custom-call | bytes 25165824 | tf_op jit(solution)/shard_map/pallas_call | solution.py:81
  129.9 81.2 %all-to-all-done.received = bf16[16,128,1024]{2,1,0:T(8,128)(2,1)} async-done(((bf16[16,128,1024]{2,1,0:T(8,128)(2,1)}), bf16[16,128,1024]{2,1,0:T(8,128)(2,1)}, u32[]{:S(2)}, u32[]{:S(2)}) %all-to-all-start) | async-done | bytes 4194336 | tf_op jit(solution)/shard_map/all_to_all | solution.py:154
  211.1 4.7 all-to-all-start.2
  215.8 0.0 all-gather.6.cloned.1.call-start
  215.8 0.7 all-gather.6.cloned.1.call-update
  216.5 11.1 %shard_map.97 = (f32[16,128,1024]{2,1,0:T(8,128)}, f32[16,128,1024]{2,1,0:T(8,128)}, bf16[16,128,1024]{2,1,0:T(8,128)(2,1)}) custom-call(s32[16]{0:T(128)} %get-tuple-element.43.old, s32[16]{0:T(128)} %get-tuple-element.38.new, bf16[16,128,1024]{2,1,0:T(8,128)(2,1)} %all-to-all-done.received, ...), custom_call_target="tpu_custom_call", output_to_operand_aliasing={{0}: (5, {}), {1}: (6, {})} | custom-call | bytes 25165824 | tf_op jit(solution)/shard_map/pallas_call | solution.py:81
  227.6 80.8 %all-to-all-done.2 = bf16[16,128,1024]{2,1,0:T(8,128)(2,1)} async-done(((bf16[16,128,1024]{2,1,0:T(8,128)(2,1)}), bf16[16,128,1024]{2,1,0:T(8,128)(2,1)}, u32[]{:S(2)}, u32[]{:S(2)}) %all-to-all-start.2) | async-done | bytes 4194336 | tf_op jit(solution)/shard_map/all_to_all | solution.py:154
  308.5 4.7 all-to-all-start.3
  313.2 0.0 all-gather.4.cloned.1.call-start
  313.2 0.0 all-gather.6.cloned.1.call-done
  313.2 0.0 copy-start.1
  313.3 3.2 fusion.2
  316.5 0.2 copy-done.1
  316.7 0.7 fusion.3.normed
  317.4 0.0 copy-start.2
  317.4 0.8 copy-done.6
  318.3 10.2 %fusion.4 = (bf16[1024,1024]{1,0:T(8,128)(2,1)}, f32[1024,1024]{1,0:T(8,128)}) fusion(bf16[1,1024,1024]{2,1,0:T(8,128)(2,1)S(1)} %copy-done.6, bf16[1024,2048]{1,0:T(8,128)(2,1)S(1)} %fusion.3.normed, bf16[2048,1024]{1,0:T(8,128)(2,1)} %bitcast.8), kind=kOutput, calls=%fused_computation.9 | convolution fusion | flops 4303355904 | bytes 16777216 | tf_op jit(solution)/shard_map/dot_general | solution.py:179
  328.5 0.0 copy-done.2
  328.5 0.0 all-gather.4.cloned.1.call-update
  328.5 0.0 copy-done.5
  328.5 2.4 convert_element_type.120
  330.9 55.4 %all-gather.4.cloned.1.call-done = bf16[1024,2048]{1,0:T(8,128)(2,1)} async-done(((bf16[1024,1024]{1,0:T(8,128)(2,1)}), bf16[1024,2048]{1,0:T(8,128)(2,1)}) %all-gather.4.cloned.1.call-update) | async-done | bytes 4194320 | tf_op jit(solution)/shard_map/all_gather | solution.py:135
  386.3 3.2 fusion
  389.5 0.2 copy-done
  389.8 2.7 fusion.1.normed
  392.5 13.4 %all-to-all-done.3 = bf16[16,128,1024]{2,1,0:T(8,128)(2,1)} async-done(((bf16[16,128,1024]{2,1,0:T(8,128)(2,1)}), bf16[16,128,1024]{2,1,0:T(8,128)(2,1)}, u32[]{:S(2)}, u32[]{:S(2)}) %all-to-all-start.3) | async-done | bytes 4194336 | tf_op jit(solution)/shard_map/all_to_all | solution.py:154
  405.9 3.9 convolution_multiply_fusion.1
  409.8 0.0 copy-done.4
  409.8 3.4 convolution_multiply_fusion.2
  413.2 3.4 convolution_multiply_fusion.3
  416.7 6.4 %multiply_reduce_fusion.3 = (f32[256]{0:T(256)S(1)}, bf16[256,1024]{1,0:T(8,128)(2,1)S(1)}, f32[256]{0:T(256)S(1)}, bf16[256,1024]{1,0:T(8,128)(2,1)S(1)}, f32[2...) fusion(f32[1,1024,1024]{2,1,0:T(8,128)} %convert_element_type.120, ...), kind=kOutput, calls=%fused_computation.79 | convolution fusion | flops 1086585856 | bytes 14684160 | tf_op jit(solution)/shard_map/dot_general | solution.py:190
  423.1 0.0 copy-start.8
  423.1 3.3 fusion.53
  426.4 3.1 fusion.56
  429.6 3.2 fusion.59
  432.7 3.2 fusion.62
  435.9 0.0 copy-done.8
  435.9 1.5 pad_maximum_fusion.1.slope
  437.4 1.5 collective-permute-start.3
  438.9 12.3 %psum.7 = f32[1024]{0:T(1024)S(1)} all-reduce(f32[1024]{0:T(1024)S(1)} %pad_maximum_fusion.2), channel_id=1, replica_groups=mesh['group'=16,'mp'=2] {'mp'}, use_global_device_ids=true, to_apply=%region_6.7 | all-reduce | flops 1024 | bytes 8192 | tf_op jit(solution)/shard_map/psum | solution.py:212
  451.3 1.6 collective-permute-start.2
  452.8 0.5 collective-permute-start.1
  453.4 1.5 collective-permute-start
  454.9 8.4 %shard_map.98.rest_0_ = bf16[1,2,2048,1024]{3,2,1,0:T(8,128)(2,1)} custom-call(bf16[1024,2048]{1,0:T(8,128)(2,1)} %fusion.1.normed, bf16[1024,1024]{1,0:T(8,128)(2,1)} %pad_maximum_fusion.1.slope), custom_call_target="tpu_custom_call" | custom-call | flops 4294967296 | bytes 10485760 | tf_op jit(solution)/shard_map/pallas_call | solution.py:114
  463.3 0.0 collective-permute-done.3
  463.4 3.8 multiply_convert_fusion
  467.2 0.0 collective-permute-done.2
  467.2 0.0 copy-done.3
  467.2 1.2 copy-done.11
  468.4 2.9 multiply_convert_fusion.1
  471.3 6.5 %collective-permute-done.1 = bf16[256,1024]{1,0:T(8,128)(2,1)} collective-permute-done((bf16[256,1024]{1,0:T(8,128)(2,1)}, bf16[256,1024]{1,0:T(8,128)(2,1)}, u32[]{:S(2)}, u32[]{:S(2)}) %collective-permute-start.1) | collective-permute-done | bytes 524320 | tf_op jit(solution)/shard_map/ppermute | solution.py:205
  477.8 2.9 multiply_convert_fusion.2
  480.6 6.1 %collective-permute-done = bf16[256,1024]{1,0:T(8,128)(2,1)} collective-permute-done((bf16[256,1024]{1,0:T(8,128)(2,1)}, bf16[256,1024]{1,0:T(8,128)(2,1)}, u32[]{:S(2)}, u32[]{:S(2)}) %collective-permute-start) | collective-permute-done | bytes 524320 | tf_op jit(solution)/shard_map/ppermute | solution.py:205
  486.7 2.9 multiply_convert_fusion.3
  489.6 1.5 pad_maximum_fusion.slope
  491.1 8.4 %shard_map.99 = bf16[1,2,2048,1024]{3,2,1,0:T(8,128)(2,1)} custom-call(bf16[1024,2048]{1,0:T(8,128)(2,1)} %copy-done.2, bf16[1024,1024]{1,0:T(8,128)(2,1)} %pad_maximum_fusion.slope, bf16[1,2,2048,1024]{3,2,1,0:T(8,128)(2,1)} %shard_map.98.rest_0_), custom_call_target="tpu_custom_call", output_to_operand_aliasing={{}: (2, {})} | custom-call | flops 4294967296 | bytes 10485760 | tf_op jit(solution)/shard_map/pallas_call | solution.py:114
  (20 shorter events, 0.1 us)
Async XLA Ops:
  14.9 98.9 %all-to-all-start.1 = ((bf16[16,128,1024]{2,1,0:T(8,128)(2,1)}), bf16[16,128,1024]{2,1,0:T(8,128)(2,1)}, u32[]{:S(2)}, u32[]{:S(2)}) async-start(bf16[16,128,1024]{2,1,0:T(8,128)(2,1)} %shard_map.95), calls=%async_computation.1 | async-start | bytes 8388608 | tf_op jit(solution)/shard_map/all_to_all | solution.py:154
  28.7 89.7 %copy-start.9 = (s32[16,2]{0,1:T(2,128)S(1)}, s32[16,2]{0,1:T(2,128)}, u32[]{:S(2)}) copy-start(s32[16,2]{0,1:T(2,128)} %param.11) | copy-start | bytes 388
  28.7 89.7 %copy-start.10 = (s32[16,2]{0,1:T(2,128)S(1)}, s32[16,2]{0,1:T(2,128)}, u32[]{:S(2)}) copy-start(s32[16,2]{0,1:T(2,128)} %param.10) | copy-start | bytes 388
  113.7 97.4 %all-to-all-start = ((bf16[16,128,1024]{2,1,0:T(8,128)(2,1)}), bf16[16,128,1024]{2,1,0:T(8,128)(2,1)}, u32[]{:S(2)}, u32[]{:S(2)}) async-start(bf16[16,128,1024]{2,1,0:T(8,128)(2,1)} %shard_map.94), calls=%async_computation | async-start | bytes 8388608 | tf_op jit(solution)/shard_map/all_to_all | solution.py:154
  211.1 97.4 %all-to-all-start.2 = ((bf16[16,128,1024]{2,1,0:T(8,128)(2,1)}), bf16[16,128,1024]{2,1,0:T(8,128)(2,1)}, u32[]{:S(2)}, u32[]{:S(2)}) async-start(bf16[16,128,1024]{2,1,0:T(8,128)(2,1)} %get-tuple-element.13), calls=%async_computation.2 | async-start | bytes 8388608 | tf_op jit(solution)/shard_map/all_to_all | solution.py:154
  215.8 97.4 %all-gather.6.cloned.1.call-start = ((), (), s32[]{:S(2)}) async-start(), calls=%async_computation.5 | async-start | bytes 6291456 | tf_op jit(solution)/shard_map/all_gather | solution.py:135
  308.5 97.4 %all-to-all-start.3 = ((bf16[16,128,1024]{2,1,0:T(8,128)(2,1)}), bf16[16,128,1024]{2,1,0:T(8,128)(2,1)}, u32[]{:S(2)}, u32[]{:S(2)}) async-start(bf16[16,128,1024]{2,1,0:T(8,128)(2,1)} %get-tuple-element.14), calls=%async_computation.3 | async-start | bytes 8388608 | tf_op jit(solution)/shard_map/all_to_all | solution.py:154
  313.2 73.1 %all-gather.4.cloned.1.call-start = ((), (), s32[]{:S(2)}) async-start(), calls=%async_computation.4 | async-start | bytes 6291456 | tf_op jit(solution)/shard_map/all_gather | solution.py:135
  313.2 3.5 copy-start.1
  316.7 1.6 copy-start.6
  317.4 11.0 %copy-start.2 = (bf16[1024,2048]{1,0:T(8,128)(2,1)}, bf16[1024,2048]{1,0:T(8,128)(2,1)S(1)}, u32[]{:S(2)}) copy-start(bf16[1024,2048]{1,0:T(8,128)(2,1)S(1)} %fusion.3.normed) | copy-start | bytes 12582916
  318.3 10.2 %copy-start.5 = (bf16[1,1024,1024]{2,1,0:T(8,128)(2,1)S(1)}, bf16[1,1024,1024]{2,1,0:T(8,128)(2,1)}, u32[]{:S(2)}) copy-start(bf16[1,1024,1024]{2,1,0:T(8,128)(2,1)} %param.13) | copy-start | bytes 6291460
  386.3 3.4 copy-start
  405.9 3.9 copy-start.4
  423.1 12.8 %copy-start.8 = (bf16[256,1024]{1,0:T(8,128)(2,1)}, bf16[256,1024]{1,0:T(8,128)(2,1)S(1)}, u32[]{:S(2)}) copy-start(bf16[256,1024]{1,0:T(8,128)(2,1)S(1)} %get-tuple-element.24) | copy-start | bytes 1572868
  437.4 25.9 %collective-permute-start.3 = (bf16[256,1024]{1,0:T(8,128)(2,1)}, bf16[256,1024]{1,0:T(8,128)(2,1)}, u32[]{:S(2)}, u32[]{:S(2)}) collective-permute-start(bf16[256,1024]{1,0:T(8,128)(2,1)} %fusion.53), channel_id=1, source_target_pairs={{0,1},{1,0},{2,3},{3,2},{4,5},{5,4},{6,7},{7,6},{8,9},{9,8},{10,11... | collective-permute-start | bytes 1572872 | tf_op jit(solution)/shard_map/ppermute | solution.py:205
  451.3 12.1 %copy-start.7 = (bf16[1024,1024]{1,0:T(8,128)(2,1)S(1)}, bf16[1024,1024]{1,0:T(8,128)(2,1)}, u32[]{:S(2)}) copy-start(bf16[1024,1024]{1,0:T(8,128)(2,1)} %get-tuple-element.41) | copy-start | bytes 6291460
  451.3 15.9 %collective-permute-start.2 = (bf16[256,1024]{1,0:T(8,128)(2,1)}, bf16[256,1024]{1,0:T(8,128)(2,1)}, u32[]{:S(2)}, u32[]{:S(2)}) collective-permute-start(bf16[256,1024]{1,0:T(8,128)(2,1)} %fusion.56), channel_id=1, source_target_pairs={{0,1},{1,0},{2,3},{3,2},{4,5},{5,4},{6,7},{7,6},{8,9},{9,8},{10,11... | collective-permute-start | bytes 1572872 | tf_op jit(solution)/shard_map/ppermute | solution.py:205
  452.8 24.9 %collective-permute-start.1 = (bf16[256,1024]{1,0:T(8,128)(2,1)}, bf16[256,1024]{1,0:T(8,128)(2,1)}, u32[]{:S(2)}, u32[]{:S(2)}) collective-permute-start(bf16[256,1024]{1,0:T(8,128)(2,1)} %fusion.59), channel_id=1, source_target_pairs={{0,1},{1,0},{2,3},{3,2},{4,5},{5,4},{6,7},{7,6},{8,9},{9,8},{10,11... | collective-permute-start | bytes 1572872 | tf_op jit(solution)/shard_map/ppermute | solution.py:205
  453.4 33.4 %collective-permute-start = (bf16[256,1024]{1,0:T(8,128)(2,1)}, bf16[256,1024]{1,0:T(8,128)(2,1)}, u32[]{:S(2)}, u32[]{:S(2)}) collective-permute-start(bf16[256,1024]{1,0:T(8,128)(2,1)} %fusion.62), channel_id=1, source_target_pairs={{0,1},{1,0},{2,3},{3,2},{4,5},{5,4},{6,7},{7,6},{8,9},{9,8},{10,11... | collective-permute-start | bytes 1572872 | tf_op jit(solution)/shard_map/ppermute | solution.py:205
  463.4 3.8 copy-start.3
  463.4 5.0 copy-start.11
Sparse Core Ops, SparseCore 0:
  218.2 57.6 all-gather.5
  328.6 57.6 all-gather.3

commit v2 on v1

v2 whole, which is shorter than its diff:
```python
import functools
import math

import jax
import jax.numpy as jnp
from jax import lax
from jax.experimental import pallas as pl
from jax.experimental.pallas import tpu as pltpu
from jax.sharding import PartitionSpec as P

outer_rate = 0.7
momentum_rate = 0.9
epsilon = 1e-06

MEBI = 1024 * 1024
RUN = 256
HALVES = 1
LIGHT = 16

f32 = jnp.float32
bf16 = jnp.bfloat16


def params(mebi=60):
    return pltpu.CompilerParams(vmem_limit_bytes=mebi * MEBI)


def silu_slope(values):
    sigmoid_part = jax.nn.sigmoid(values)
    return sigmoid_part * (1.0 + values * (1.0 - sigmoid_part))


def cast_kernel(src, dst):
    dst[...] = src[...].reshape(dst.shape).astype(dst.dtype)


def cast_level(deltas, level, groups):
    _, _, depth, columns = deltas.shape
    rows = depth // groups
    per = 4 if groups % 4 == 0 else 1
    return pl.pallas_call(
        cast_kernel,
        grid=(groups // per,),
        in_specs=[pl.BlockSpec((1, 1, per * rows, columns), lambda i: (0, level, i, 0))],
        out_specs=pl.BlockSpec((per, rows, columns), lambda i: (i, 0, 0)),
        out_shape=jax.ShapeDtypeStruct((groups, rows, columns), bf16),
        compiler_params=params(),
        cost_estimate=pl.CostEstimate(
            flops=0, bytes_accessed=depth * columns * 6, transcendentals=0
        ),
    )(deltas)


def update_kernel(groups, mods, aliased, old, new, received, anchor, momentum, *rest):
    new_anchor, new_momentum, outgoing, total = rest[2:] if aliased else rest
    total[...] = jnp.zeros_like(total)
    for g in range(groups):
        m = old[g]
        total[m] = total[m] + received[g].astype(f32)
    for m in range(mods):
        count = jnp.int32(0)
        for g in range(groups):
            count = count + jnp.where(old[g] == m, 1, 0)
        outer_grad = total[m] / count.astype(f32)
        moved = momentum_rate * momentum[m] + outer_grad
        new_momentum[m] = moved
        total[m] = anchor[m] - outer_rate * (outer_grad + momentum_rate * moved)
        new_anchor[m] = total[m]
    for g in range(groups):
        outgoing[g] = total[new[g]].astype(outgoing.dtype)


def outer_update(received, anchor, momentum, old, new, level, levels, previous):
    groups, rows, columns = received.shape
    modules = anchor.shape[0]
    mods = modules // levels
    tile = 32 if rows % 32 == 0 else rows
    state = pl.BlockSpec((mods, tile, columns), lambda i, *_: (level, i, 0))
    block = pl.BlockSpec((groups, tile, columns), lambda i, *_: (0, i, 0))
    anywhere = pl.BlockSpec(memory_space=pl.ANY)
    aliased = previous is not None
    whole = jax.ShapeDtypeStruct(anchor.shape, f32)
    return pl.pallas_call(
        functools.partial(update_kernel, groups, mods, aliased),
        grid_spec=pltpu.PrefetchScalarGridSpec(
            num_scalar_prefetch=2,
            grid=(rows // tile,),
            in_specs=[block, state, state] + ([anywhere, anywhere] if aliased else []),
            out_specs=[state, state, block],
            scratch_shapes=[pltpu.VMEM((mods, tile, columns), f32)],
        ),
        out_shape=[whole, whole, jax.ShapeDtypeStruct(received.shape, bf16)],
        input_output_aliases={5: 0, 6: 1} if aliased else {},
        compiler_params=params(),
        cost_estimate=pl.CostEstimate(
            flops=0,
            bytes_accessed=rows * columns * (groups * 4 + mods * 16),
            transcendentals=0,
        ),
    )(old, new, received, anchor, momentum, *(previous or ()))


OVER_ROWS = (((0,), (0,)), ((), ()))
OVER_COLUMNS = (((1,), (1,)), ((), ()))


def cost(flops, values, transcendentals=0):
    return pl.CostEstimate(flops=flops, bytes_accessed=values, transcendentals=transcendentals)


def norm_kernel(parts, depth, place, *refs):
    blocks = refs[:parts]
    out, scale = refs[parts : parts + 2]
    step = pl.program_id(1)

    @pl.when(step == 0)
    def _():
        total = jnp.zeros(scale.shape, f32)
        for block in blocks:
            values = block[...].astype(f32)
            total = total + jnp.sum(values * values, axis=-1, keepdims=True)
        scale[...] = lax.rsqrt(total / depth + epsilon)

    for at, block in enumerate(blocks):

        @pl.when(step == at)
        def _(block=block):
            out[...] = (block[...].astype(f32) * scale[...]).astype(out.dtype)


def normalize(own, parts, place):
    rows, width = own.shape
    depth = width * parts
    blocks = [own] + [lax.ppermute(own, "mp", around(parts, step)) for step in range(1, parts)]
    tile = min(256, rows)
    block = pl.BlockSpec((tile, width), lambda i, j, at: (i, 0))
    return pl.pallas_call(
        functools.partial(norm_kernel, parts, depth),
        grid_spec=pltpu.PrefetchScalarGridSpec(
            num_scalar_prefetch=1,
            grid=(rows // tile, parts),
            in_specs=[block] * parts,
            out_specs=[
                pl.BlockSpec(
                    (tile, width), lambda i, j, at: (i, lax.rem(at[0] + parts - j, parts))
                ),
                pl.BlockSpec((tile, 1), lambda i, j, at: (i, 0)),
            ],
        ),
        out_shape=[
            jax.ShapeDtypeStruct((rows, depth), bf16),
            jax.ShapeDtypeStruct((rows, 1), f32),
        ],
        compiler_params=params(),
        cost_estimate=cost(0, 4 * rows * depth),
    )(place.reshape(1).astype(jnp.int32), *blocks)


def grad_kernel(factor, normed, slope, out):
    product = lax.dot_general(normed[...], slope[...], OVER_ROWS, preferred_element_type=f32)
    out[...] = (product * factor).astype(out.dtype).reshape(out.shape)


def last_level_grad(normed, slope, factor, levels):
    rows, depth = normed.shape
    columns = slope.shape[1]
    tile = min(512, depth)
    return pl.pallas_call(
        functools.partial(grad_kernel, factor),
        grid=(depth // tile,),
        in_specs=[
            pl.BlockSpec((rows, tile), lambda i: (0, i)),
            pl.BlockSpec((rows, columns), lambda i: (0, 0)),
        ],
        out_specs=pl.BlockSpec((1, 1, tile, columns), lambda i: (0, levels - 1, i, 0)),
        out_shape=jax.ShapeDtypeStruct((1, levels, depth, columns), bf16),
        compiler_params=params(24),
        cost_estimate=cost(
            2 * rows * depth * columns // LIGHT,
            2 * (rows * depth + rows * columns + depth * columns) // LIGHT,
        ),
    )(normed, slope)


def state_kernel(factor, normed, weight, state, following, gate):
    pre = jnp.dot(normed[...], weight[...], preferred_element_type=f32) * factor
    sigmoid_part = jax.nn.sigmoid(pre)
    following[...] = (state[...].astype(f32) + pre * sigmoid_part).astype(bf16)
    gate[...] = sigmoid_part * (1.0 + pre * (1.0 - sigmoid_part))


def first_forward(normed, weight, state, factor):
    rows, depth = normed.shape
    columns = weight.shape[1]
    tile = min(256, rows)
    mine = pl.BlockSpec((tile, columns), lambda i: (i, 0))
    return pl.pallas_call(
        functools.partial(state_kernel, factor),
        grid=(rows // tile,),
        in_specs=[
            pl.BlockSpec((tile, depth), lambda i: (i, 0)),
            pl.BlockSpec((depth, columns), lambda i: (0, 0)),
            mine,
        ],
        out_specs=[mine, mine],
        out_shape=[
            jax.ShapeDtypeStruct((rows, columns), bf16),
            jax.ShapeDtypeStruct((rows, columns), f32),
        ],
        compiler_params=params(),
        cost_estimate=cost(
            2 * rows * depth * columns,
            2 * (rows * depth + 4 * rows * columns + depth * columns),
            rows * columns,
        ),
    )(normed, weight, state)


def slope_kernel(factor, width, at, normed, weight, upstream, *rest):
    slope, share, terms = rest[-3:]
    pre = jnp.dot(normed[...], weight[...], preferred_element_type=f32) * factor
    value = (upstream[...].astype(f32) * silu_slope(pre)).astype(bf16)
    slope[...] = value
    total = jnp.sum(value.astype(f32) * pre, axis=-1, keepdims=True)
    share[...] = jnp.broadcast_to(total, share.shape)
    start = pl.multiple_of(at[0] * width, width)
    product = lax.dot_general(
        value, weight[pl.ds(start, width), :], OVER_COLUMNS, preferred_element_type=f32
    )
    terms[...] = (product * factor).astype(terms.dtype)


def second_forward(normed, weight, upstream, where, width, factor, half, previous):
    rows, depth = normed.shape
    columns = weight.shape[1]
    tile = min(256, rows // HALVES)
    steps = rows // HALVES // tile
    first = half * steps
    mine = pl.BlockSpec((tile, columns), lambda i, at: (first + i, 0))
    return pl.pallas_call(
        functools.partial(slope_kernel, factor, width),
        grid_spec=pltpu.PrefetchScalarGridSpec(
            num_scalar_prefetch=1,
            grid=(steps,),
            in_specs=[
                pl.BlockSpec((tile, depth), lambda i, at: (first + i, 0)),
                pl.BlockSpec((depth, columns), lambda i, at: (0, 0)),
                mine,
            ]
            + [pl.BlockSpec(memory_space=pl.ANY)] * len(previous),
            out_specs=[
                mine,
                pl.BlockSpec((tile, 128), lambda i, at: (first + i, 0)),
                pl.BlockSpec((tile, width), lambda i, at: (i, 0)),
            ],
        ),
        out_shape=[
            jax.ShapeDtypeStruct((rows, columns), bf16),
            jax.ShapeDtypeStruct((rows, 128), f32),
            jax.ShapeDtypeStruct((rows // HALVES, width), bf16),
        ],
        input_output_aliases={4 + n: n for n in range(len(previous))},
        compiler_params=params(),
        cost_estimate=cost(
            2 * rows // HALVES * columns * (depth + width) // LIGHT,
            2 * (rows // HALVES * (depth + 2 * columns) + depth * columns) // LIGHT,
        ),
    )(where.reshape(1).astype(jnp.int32), normed, weight, upstream, *previous)


def term_kernel(factor, where, slope, weight, out):
    product = lax.dot_general(slope[...], weight[...], OVER_COLUMNS, preferred_element_type=f32)
    out[...] = (product * factor).astype(out.dtype)


def term(slope, weight, where, width, factor):
    rows, columns = slope.shape
    tile = min(512, rows)
    return pl.pallas_call(
        functools.partial(term_kernel, factor),
        grid_spec=pltpu.PrefetchScalarGridSpec(
            num_scalar_prefetch=1,
            grid=(rows // tile,),
            in_specs=[
                pl.BlockSpec((tile, columns), lambda i, at: (i, 0)),
                pl.BlockSpec((width, columns), lambda i, at: (at[0], 0)),
            ],
            out_specs=pl.BlockSpec((tile, width), lambda i, at: (i, 0)),
        ),
        out_shape=jax.ShapeDtypeStruct((rows, width), bf16),
        compiler_params=params(24),
        cost_estimate=cost(
            2 * rows * columns * width // LIGHT,
            2 * (rows * columns + columns * width + rows * width) // LIGHT,
        ),
    )(where.reshape(1).astype(jnp.int32), slope, weight)


def first_kernel(factor, cells, *refs):
    normed, scale, share, upstream, state, gate, kept = refs[:7]
    terms = refs[7:-3]
    out, slope = refs[-2:]
    count = len(terms) // len(cells)

    @pl.when(pl.program_id(0) == 0)
    def _():
        for number, (top, height, left, width) in enumerate(cells):
            span = slice(top, top + height)
            here = slice(left, left + width)
            normed_grad = kept[span, here].astype(f32)
            for other in terms[number * count : (number + 1) * count]:
                normed_grad = normed_grad + other[...].astype(f32)
            state_grad = (
                upstream[span, here].astype(f32)
                + scale[span, :] * normed_grad
                - state[span, here].astype(f32) * share[span, :]
            )
            slope[span, here] = (state_grad * gate[span, here]).astype(bf16)

    product = lax.dot_general(normed[...], slope[...], OVER_ROWS, preferred_element_type=f32)
    out[...] = (product * factor).astype(out.dtype).reshape(out.shape)


def first_level_grad(normed, scale, share, mine, cells, terms, block, width, factor, grads, mebi):
    rows, depth = normed.shape
    tile = min(512, depth)
    column = pl.BlockSpec((rows, 1), lambda i: (0, 0))
    part = pl.BlockSpec((rows, width), lambda i: (0, block))
    return pl.pallas_call(
        functools.partial(first_kernel, factor, cells),
        grid=(depth // tile,),
        in_specs=[pl.BlockSpec((rows, tile), lambda i: (0, i)), column, column]
        + [part] * len(mine)
        + [pl.BlockSpec(value.shape, lambda i: (0, 0)) for value in terms]
        + [pl.BlockSpec(memory_space=pl.ANY)],
        out_specs=pl.BlockSpec((1, 1, tile, width), lambda i: (0, 0, i, block)),
        out_shape=jax.ShapeDtypeStruct(grads.shape, bf16),
        scratch_shapes=[pltpu.VMEM((rows, width), bf16)],
        input_output_aliases={3 + len(mine) + len(terms): 0},
        compiler_params=params(mebi),
        cost_estimate=cost(
            2 * rows * depth * width // LIGHT,
            2 * (rows * depth + 7 * rows * width + depth * width) // LIGHT,
        ),
    )(normed, scale, share, *mine, *terms, grads)


def around(parts, step):
    return [(p, (p + step) % parts) for p in range(parts)]


def after(value, *others):
    return lax.optimization_barrier((value, *others))[0]


def shards(anchor, momentum, deltas, old_path, new_path, tokens, cotangent):
    groups = lax.axis_size("group")
    parts = lax.axis_size("mp")
    place = lax.axis_index("mp")
    levels = deltas.shape[1]
    depth = deltas.shape[2]
    columns = deltas.shape[3]
    factor = 1.0 / math.sqrt(depth)

    def exchange(blocks):
        return lax.all_to_all(blocks, "group", split_axis=0, concat_axis=0, tiled=True)

    received = [exchange(cast_level(deltas, level, groups)) for level in range(levels)]
    first_normed, _ = normalize(tokens[0], parts, place)
    received[0] = after(received[0], first_normed)

    previous = None
    loaded = []
    for level in range(levels):
        part_anchor, part_momentum, outgoing = outer_update(
            received[level],
            anchor,
            momentum,
            old_path[:, level],
            new_path[:, level],
            level,
            levels,
            previous,
        )
        previous = (part_anchor, part_momentum)
        loaded.append(exchange(outgoing).reshape(depth, columns))
    new_anchor, new_momentum = previous
    first_weight, second_weight = loaded

    upstream = cotangent[0]
    second_state, gate = first_forward(first_normed, first_weight, tokens[0], factor)
    second_normed, second_scale = normalize(second_state, parts, place)

    own_features = depth // parts
    width = min(RUN, own_features)
    runs = own_features // width

    def place_of(step, run):
        return lax.rem(place + step, parts) * runs + run

    def send(values):
        return [lax.ppermute(values[n], "mp", around(parts, n + 1)) for n in range(len(values))]

    def terms_of(source, run, steps):
        return [
            term(source, second_weight, place_of(step, run), width, factor) for step in steps
        ]

    rows = second_normed.shape[0]
    previous = ()
    leading = []
    for half in range(HALVES):
        slope, share, terms = second_forward(
            second_normed,
            second_weight,
            upstream,
            place_of(1, 0),
            width,
            factor,
            half,
            previous,
        )
        previous = (slope, share)
        leading.append(terms)
    own_share = share[:, 0].reshape(-1, 128)
    leading = [lax.ppermute(after(terms, own_share), "mp", around(parts, 1)) for terms in leading]
    share = own_share
    for other in send([own_share] * (parts - 1)):
        share = share + other
    sent = terms_of(slope, 0, range(2, parts))
    rest = [lax.ppermute(value, "mp", around(parts, n + 2)) for n, value in enumerate(sent)]
    height = rows // HALVES
    arrived = [[]]
    for half in range(HALVES):
        arrived[0].append(
            (
                half * height,
                height,
                [leading[half]] + [value[half * height : (half + 1) * height] for value in rest],
            )
        )
    last = slope
    source = slope
    for run in range(1, runs):
        if run == 3:
            kept = term(after(slope, last), second_weight, place, own_features, factor)
            source = after(slope, kept, *leading)
        sent = terms_of(source, run, range(1, parts))
        last = sent[0]
        arrived.append([(0, rows, send(sent))])
    if runs <= 3:
        kept = term(after(slope, last), second_weight, place, own_features, factor)
    grads = last_level_grad(second_normed, after(slope, last), factor, levels)
    scaled = second_scale**2 * after(share, grads).reshape(rows, 1) / depth
    mine = [upstream, second_state, gate, kept]
    bounds = [0, runs - 1, runs] if runs > 1 else [0, runs]
    for begin, end in zip(bounds[:-1], bounds[1:]):
        cells, terms = [], []
        for run in range(begin, end):
            for top, tall, values in arrived[run]:
                cells.append((top, tall, (run - begin) * width, width))
                terms += values
        grads = first_level_grad(
            first_normed,
            second_scale,
            scaled,
            mine,
            cells,
            terms,
            begin // (end - begin),
            (end - begin) * width,
            factor,
            grads,
            24 if end == runs else 40,
        )
    return (new_anchor, new_momentum, grads)


def solution(mesh):
    in_specs = (
        P(None, "group", "mp"),
        P(None, "group", "mp"),
        P("group", None, None, "mp"),
        P(),
        P(),
        P("group", None, "mp"),
        P("group", None, "mp"),
    )
    out_specs = (P(None, "group", "mp"), P(None, "group", "mp"), P("group", None, None, "mp"))
    return jax.shard_map(shards, mesh=mesh, in_specs=in_specs, out_specs=out_specs, check_vma=False)
```

time: 509 us -> 467 us (0.917)
  matrix products: 52.5 us -> 0 us
  Pallas kernels: 54.2 us -> 105 us
  other arithmetic: 15.4 us -> 1.1 us
  between operations: 14.3 us -> 0.71 us
  blocking collectives: 12.3 us -> 0 us
  waiting for transfers between devices: 329 us -> 318 us
  local copies, waits for them, and re-layouts: 3.1 us -> 12.5 us
    ppermute x4 -> x7, waiting for transfers between devices: 12.6 us -> 100 us  [the longest x2 92.1 us: normalize(): lax.ppermute(own, 'mp', around(parts, step))]
    all_gather x2 -> x0, waiting for transfers between devices: 55.4 us -> none  [gathered(): return lax.all_gather(own, 'mp', axis=1, tiled=True)]
    pallas_call x2 -> x11, Pallas kernels: 16.9 us -> 71.4 us  [the longest x2 17.8 us: normalize(): pl.pallas_call(functools.partial(norm_kernel, parts, depth), grid_spec=pl...]
    dot_general x13 -> x0, matrix products: 52.5 us -> none  [the longest x8 25.2 us: shards(): lax.dot_general(slope, weight, (((1,), (1,)), ((), ())), preferred_elemen...]
    all_to_all x4, waiting for transfers between devices: 260 us -> 218 us  [exchange(): lax.all_to_all(blocks, 'group', split_axis=0, concat_axis=0, tiled=True)]
    psum x1 -> x0, blocking collectives: 12.3 us -> none  [shards(): inner = lax.psum(inner, 'mp')[:, None] / second_scale]
    unnamed x24 -> x28, local copies, waits for them, and re-layouts: 2.48 us -> 9.62 us
    reduce_sum x2 -> x0, other arithmetic: 6.44 us -> none  [normalize(): jnp.mean(values * values, axis=-1, keepdims=True) + epsilon]
  transfers between devices with their start and end apart: 10 -> 11, of which waited for: 7 -> 7; matrix products, arithmetic and copies ran while one was open for 6% -> 1% of each run, Pallas kernels for 8% -> 18%
where the time goes in v2:
time: 467 us; the launch traced here: 466 us
  waiting for transfers between devices  318 us (68%)
  Pallas kernels  105 us (22%)
  starting transfers between devices  28.9 us (6%)
  local copies, waits for them, and re-layouts  12.5 us (3%)
    all_to_all x4, waiting for transfers between devices, exchange(): lax.all_to_all(blocks, 'group', split_axis=0, concat_axis=0, tiled=True)  218 us
    ppermute x2, waiting for transfers between devices, normalize(): lax.ppermute(own, 'mp', around(parts, step))  92.1 us
    pallas_call x2, Pallas kernels, outer_update(): pl.pallas_call(functools.partial(update_kernel, groups, mods, aliased), g...  21.6 us
    all_to_all x4, starting transfers between devices, exchange(): lax.all_to_all(blocks, 'group', split_axis=0, concat_axis=0, tiled=True)  20.2 us
    pallas_call x2, Pallas kernels, normalize(): pl.pallas_call(functools.partial(norm_kernel, parts, depth), grid_spec=pl...  17.8 us
    pallas_call x2, Pallas kernels, first_level_grad(): pl.pallas_call(functools.partial(first_kernel, factor, cells), grid=(dept...  13.8 us
    pallas_call x4, Pallas kernels, term(): pl.pallas_call(functools.partial(term_kernel, factor), grid_spec=pltpu.Pr...  12.5 us
    pallas_call x2, Pallas kernels, cast_level(): pl.pallas_call(cast_kernel, grid=(groups // per,), in_specs=[pl.BlockSpec...  11.6 us
  transfers between devices with their start and end apart: 11, of which 7 were waited for; matrix products, arithmetic and copies ran while one was open for 1% of the time, Pallas kernels for 18%

profile of v2, /device:TPU:16, one launch (start us, length us, event | category | flops | bytes accessed | tf_op | source)
XLA Modules:
  0.0 465.8 jit_solution(6382869493918777350)
XLA Ops:
  0.6 5.8 %shard_map.95 = bf16[16,128,1024]{2,1,0:T(8,128)(2,1)} custom-call(f32[1,2,2048,1024]{3,2,1,0:T(8,128)} %src.3), custom_call_target="tpu_custom_call" | custom-call | bytes 12582912 | tf_op jit(solution)/shard_map/pallas_call | solution.py:41
  6.4 6.2 %all-to-all-start.1 = ((bf16[16,128,1024]{2,1,0:T(8,128)(2,1)}), bf16[16,128,1024]{2,1,0:T(8,128)(2,1)}, u32[]{:S(2)}, u32[]{:S(2)}) async-start(bf16[16,128,1024]{2,1,0:T(8,128)(2,1)} %shard_map.95), calls=%async_computation.1 | async-start | bytes 8388608 | tf_op jit(solution)/shard_map/all_to_all | solution.py:366
  12.6 5.8 %shard_map.94 = bf16[16,128,1024]{2,1,0:T(8,128)(2,1)} custom-call(f32[1,2,2048,1024]{3,2,1,0:T(8,128)} %src.3), custom_call_target="tpu_custom_call" | custom-call | bytes 12582912 | tf_op jit(solution)/shard_map/pallas_call | solution.py:41
  18.4 0.0 copy-start.10
  18.4 0.0 copy-start.12
  18.4 0.0 copy-start.13
  18.4 86.9 %all-to-all-done.1.received = bf16[16,128,1024]{2,1,0:T(8,128)(2,1)} async-done(((bf16[16,128,1024]{2,1,0:T(8,128)(2,1)}), bf16[16,128,1024]{2,1,0:T(8,128)(2,1)}, u32[]{:S(2)}, u32[]{:S(2)}) %all-to-all-start.1) | async-done | bytes 4194336 | tf_op jit(solution)/shard_map/all_to_all | solution.py:366
  105.3 4.7 %all-to-all-start = ((bf16[16,128,1024]{2,1,0:T(8,128)(2,1)}), bf16[16,128,1024]{2,1,0:T(8,128)(2,1)}, u32[]{:S(2)}, u32[]{:S(2)}) async-start(bf16[16,128,1024]{2,1,0:T(8,128)(2,1)} %shard_map.94), calls=%async_computation | async-start | bytes 8388608 | tf_op jit(solution)/shard_map/all_to_all | solution.py:366
  110.0 0.0 copy-done.10
  110.0 1.6 collective-permute-start
  111.5 0.0 copy-done.12
  111.5 0.0 copy-done.13
  111.5 0.6 slice_bitcast_fusion
  112.1 45.7 %collective-permute-done.refs_1_ = bf16[1024,1024]{1,0:T(8,128)(2,1)} collective-permute-done((bf16[1024,1024]{1,0:T(8,128)(2,1)S(1)}, bf16[1024,1024]{1,0:T(8,128)(2,1)}, u32[]{:S(2)}, u32[]{:S(2)}) %collective-permute-start) | collective-permute-done | bytes 2097184 | tf_op jit(solution)/shard_map/ppermute | solution.py:134
  157.8 8.9 %shard_map.96 = (bf16[1024,2048]{1,0:T(8,128)(2,1)}, f32[1024,1]{1,0:T(8,128)}) custom-call(s32[1]{0:T(128)} %bitcast.4.place.where, bf16[1024,1024]{1,0:T(8,128)(2,1)} %bitcast.23, bf16[1024,1024]{1,0:T(8,128)(2,1)} %collective-permute-done.refs_1_), custom_call_target="tpu_custom_call" | custom-call | bytes 8388608 | tf_op jit(solution)/shard_map/pallas_call | solution.py:137
  166.7 10.8 %shard_map.97 = (f32[16,128,1024]{2,1,0:T(8,128)}, f32[16,128,1024]{2,1,0:T(8,128)}, bf16[16,128,1024]{2,1,0:T(8,128)(2,1)}) custom-call(s32[16]{0:T(128)} %get-tuple-element.48.old, s32[16]{0:T(128)} %get-tuple-element.43.new, bf16[16,128,1024]{2,1,0:T(8,128)(2,1)} %all-to-all-done.1.received, f32[16,128,1024]{2,1,0:T(8,128)} %anchor.3, ...), custom_call_target="tpu_custom_call" | custom-call | bytes 25165824 | tf_op jit(solution)/shard_map/pallas_call | solution.py:83
  177.5 25.1 %all-to-all-done.received = bf16[16,128,1024]{2,1,0:T(8,128)(2,1)} async-done(((bf16[16,128,1024]{2,1,0:T(8,128)(2,1)}), bf16[16,128,1024]{2,1,0:T(8,128)(2,1)}, u32[]{:S(2)}, u32[]{:S(2)}) %all-to-all-start) | async-done | bytes 4194336 | tf_op jit(solution)/shard_map/all_to_all | solution.py:366
  202.7 4.7 %all-to-all-start.2 = ((bf16[16,128,1024]{2,1,0:T(8,128)(2,1)}), bf16[16,128,1024]{2,1,0:T(8,128)(2,1)}, u32[]{:S(2)}, u32[]{:S(2)}) async-start(bf16[16,128,1024]{2,1,0:T(8,128)(2,1)} %get-tuple-element.29), calls=%async_computation.2 | async-start | bytes 8388608 | tf_op jit(solution)/shard_map/all_to_all | solution.py:366
  207.3 10.8 %shard_map.98 = (f32[16,128,1024]{2,1,0:T(8,128)}, f32[16,128,1024]{2,1,0:T(8,128)}, bf16[16,128,1024]{2,1,0:T(8,128)(2,1)}) custom-call(s32[16]{0:T(128)} %get-tuple-element.47.old, s32[16]{0:T(128)} %get-tuple-element.44.new, bf16[16,128,1024]{2,1,0:T(8,128)(2,1)} %all-to-all-done.received, ...), custom_call_target="tpu_custom_call", output_to_operand_aliasing={{0}: (5, {}), {1}: (6, {})} | custom-call | bytes 25165824 | tf_op jit(solution)/shard_map/pallas_call | solution.py:83
  218.2 81.9 %all-to-all-done.2 = bf16[16,128,1024]{2,1,0:T(8,128)(2,1)} async-done(((bf16[16,128,1024]{2,1,0:T(8,128)(2,1)}), bf16[16,128,1024]{2,1,0:T(8,128)(2,1)}, u32[]{:S(2)}, u32[]{:S(2)}) %all-to-all-start.2) | async-done | bytes 4194336 | tf_op jit(solution)/shard_map/all_to_all | solution.py:366
  300.0 4.7 %all-to-all-start.3 = ((bf16[16,128,1024]{2,1,0:T(8,128)(2,1)}), bf16[16,128,1024]{2,1,0:T(8,128)(2,1)}, u32[]{:S(2)}, u32[]{:S(2)}) async-start(bf16[16,128,1024]{2,1,0:T(8,128)(2,1)} %get-tuple-element.33), calls=%async_computation.3 | async-start | bytes 8388608 | tf_op jit(solution)/shard_map/all_to_all | solution.py:366
  304.7 10.7 %shard_map.99 = (bf16[1024,1024]{1,0:T(8,128)(2,1)}, f32[1024,1024]{1,0:T(8,128)}) custom-call(bf16[1024,2048]{1,0:T(8,128)(2,1)} %get-tuple-element.23.normed.refs_0_, bf16[2048,1024]{1,0:T(8,128)(2,1)} %bitcast.6.weight, bf16[1024,1024]{1,0:T(8,128)(2,1)} %bitcast.24), custom_call_target="tpu_custom_call" | custom-call | flops 4294967296 | bytes 16777216 | tf_op jit(solution)/shard_map/pallas_call | solution.py:197
  315.4 1.5 collective-permute-start.1
  316.9 46.4 %collective-permute-done.1.refs_1_ = bf16[1024,1024]{1,0:T(8,128)(2,1)S(1)} collective-permute-done((bf16[1024,1024]{1,0:T(8,128)(2,1)}, bf16[1024,1024]{1,0:T(8,128)(2,1)S(1)}, u32[]{:S(2)}, u32[]{:S(2)}) %collective-permute-start.1) | collective-permute-done | bytes 2097184 | tf_op jit(solution)/shard_map/ppermute | solution.py:134
  363.3 0.0 copy-start.11
  363.3 1.3 copy-done.11
  364.6 8.9 %shard_map.100 = (bf16[1024,2048]{1,0:T(8,128)(2,1)}, f32[1024,1]{1,0:T(8,128)}) custom-call(s32[1]{0:T(128)} %bitcast.4.place.where, bf16[1024,1024]{1,0:T(8,128)(2,1)} %get-tuple-element.30.refs_0_.refs_4_, bf16[1024,1024]{1,0:T(8,128)(2,1)} %copy-done.11), custom_call_target="tpu_custom_call" | custom-call | bytes 8388608 | tf_op jit(solution)/shard_map/pallas_call | solution.py:137
  373.5 23.9 %all-to-all-done.3 = bf16[16,128,1024]{2,1,0:T(8,128)(2,1)} async-done(((bf16[16,128,1024]{2,1,0:T(8,128)(2,1)}), bf16[16,128,1024]{2,1,0:T(8,128)(2,1)}, u32[]{:S(2)}, u32[]{:S(2)}) %all-to-all-start.3) | async-done | bytes 4194336 | tf_op jit(solution)/shard_map/all_to_all | solution.py:366
  397.4 10.2 %shard_map.101 = (bf16[1024,1024]{1,0:T(8,128)(2,1)}, f32[1024,128]{1,0:T(8,128)}, bf16[1024,256]{1,0:T(8,128)(2,1)}) custom-call(s32[1]{0:T(128)} %bitcast.7.at, bf16[1024,2048]{1,0:T(8,128)(2,1)} %get-tuple-element.32.normed, bf16[2048,1024]{1,0:T(8,128)(2,1)} %bitcast.8.weight, bf16[1024,1024]{1,0:T(8,128)(2,1)} %bitcast.20), custom_call_target="tpu_custom_call" | custom-call | flops 301989888 | bytes 786432 | tf_op jit(solution)/shard_map/pallas_call | solution.py:240
  407.6 1.2 slice_reduce_fusion
  408.8 1.6 collective-permute-start.3
  410.4 0.5 collective-permute-start.2
  410.9 0.0 copy-start
  410.9 1.6 copy-done
  412.5 2.7 shard_map.102
  415.2 0.0 copy-start.1
  415.2 1.5 collective-permute-start.6
  416.7 2.7 shard_map.106
  419.4 0.6 collective-permute-start.5
  420.1 0.0 copy-done.1
  420.1 4.2 shard_map.103.refs_6_
  424.2 0.0 copy-start.4
  424.3 1.3 copy-done.4
  425.6 0.0 collective-permute-done.3.refs_7_
  425.6 2.9 shard_map.104
  428.5 1.4 collective-permute-start.4
  429.9 0.0 collective-permute-done.2
  429.9 0.0 copy-done.6
  429.9 0.0 copy-start.9
  429.9 0.0 copy-start.2
  429.9 6.5 %shard_map.105.refs_10_ = bf16[1,2,2048,1024]{3,2,1,0:T(8,128)(2,1)} custom-call(bf16[1024,2048]{1,0:T(8,128)(2,1)S(1)} %copy-done.6, bf16[1024,1024]{1,0:T(8,128)(2,1)S(1)} %copy-done.1), custom_call_target="tpu_custom_call" | custom-call | flops 268435456 | bytes 655360 | tf_op jit(solution)/shard_map/pallas_call | solution.py:168
  436.4 1.0 copy.14
  437.4 0.0 copy-done.9
  437.4 1.1 multiply_multiply_fusion.refs_2_
  438.5 8.1 %collective-permute-done.5.refs_8_ = bf16[1024,256]{1,0:T(8,128)(2,1)} collective-permute-done((bf16[1024,256]{1,0:T(8,128)(2,1)}, bf16[1024,256]{1,0:T(8,128)(2,1)}, u32[]{:S(2)}, u32[]{:S(2)}) %collective-permute-start.5) | collective-permute-done | bytes 524320 | tf_op jit(solution)/shard_map/ppermute | solution.py:402
  446.6 0.0 collective-permute-done.6.refs_9_
  446.6 0.0 copy-done.2
  446.6 1.6 copy-done.3
  448.2 1.6 copy-done.5
  449.8 2.2 copy-done.7
  452.0 9.0 %shard_map.107.refs_8_ = bf16[1,2,2048,1024]{3,2,1,0:T(8,128)(2,1)} custom-call(bf16[1024,2048]{1,0:T(8,128)(2,1)S(1)} %copy-done.7, f32[1024,1]{1,0:T(8,128)S(1)} %copy-done.9, f32[1024,1]{1,0:T(8,128)S(1)} %multiply_multiply_fusion.refs_2_, bf16[1024,1024]{1,0:T(8,128)(2,1)S(1)} %bitcast.21, ...), custom_call_target="tpu_custom_call", output_to_operand_aliasing={{}: (10, {})} | custom-call | flops 201326592 | bytes 1146880 | tf_op jit(solution)/shard_map/pallas_call | solution.py:329
  461.0 0.0 collective-permute-done.4.refs_7_
  461.0 0.0 copy-done.8
  461.0 4.8 %shard_map.108 = bf16[1,2,2048,1024]{3,2,1,0:T(8,128)(2,1)} custom-call(bf16[1024,2048]{1,0:T(8,128)(2,1)S(1)} %copy-done.7, f32[1024,1]{1,0:T(8,128)S(1)} %copy-done.9, f32[1024,1]{1,0:T(8,128)S(1)} %multiply_multiply_fusion.refs_2_, bf16[1024,1024]{1,0:T(8,128)(2,1)S(1)} %bitcast.22, ...), custom_call_target="tpu_custom_call", output_to_operand_aliasing={{}: (8, {})} | custom-call | flops 67108864 | bytes 557056 | tf_op jit(solution)/shard_map/pallas_call | solution.py:329
  (6 shorter events, 0.0 us)
Async XLA Ops:
  6.4 98.9 %all-to-all-start.1 = ((bf16[16,128,1024]{2,1,0:T(8,128)(2,1)}), bf16[16,128,1024]{2,1,0:T(8,128)(2,1)}, u32[]{:S(2)}, u32[]{:S(2)}) async-start(bf16[16,128,1024]{2,1,0:T(8,128)(2,1)} %shard_map.95), calls=%async_computation.1 | async-start | bytes 8388608 | tf_op jit(solution)/shard_map/all_to_all | solution.py:366
  18.4 91.6 %copy-start.10 = (bf16[1,1024,1024]{2,1,0:T(8,128)(2,1)S(1)}, bf16[1,1024,1024]{2,1,0:T(8,128)(2,1)}, u32[]{:S(2)}) copy-start(bf16[1,1024,1024]{2,1,0:T(8,128)(2,1)} %param.12) | copy-start | bytes 6291460
  18.4 93.2 %copy-start.12 = (s32[16,2]{0,1:T(2,128)S(1)}, s32[16,2]{0,1:T(2,128)}, u32[]{:S(2)}) copy-start(s32[16,2]{0,1:T(2,128)} %param.11) | copy-start | bytes 388
  18.4 93.2 %copy-start.13 = (s32[16,2]{0,1:T(2,128)S(1)}, s32[16,2]{0,1:T(2,128)}, u32[]{:S(2)}) copy-start(s32[16,2]{0,1:T(2,128)} %param.10) | copy-start | bytes 388
  105.3 97.4 %all-to-all-start = ((bf16[16,128,1024]{2,1,0:T(8,128)(2,1)}), bf16[16,128,1024]{2,1,0:T(8,128)(2,1)}, u32[]{:S(2)}, u32[]{:S(2)}) async-start(bf16[16,128,1024]{2,1,0:T(8,128)(2,1)} %shard_map.94), calls=%async_computation | async-start | bytes 8388608 | tf_op jit(solution)/shard_map/all_to_all | solution.py:366
  110.0 47.9 %collective-permute-start = (bf16[1024,1024]{1,0:T(8,128)(2,1)S(1)}, bf16[1024,1024]{1,0:T(8,128)(2,1)}, u32[]{:S(2)}, u32[]{:S(2)}) collective-permute-start(bf16[1024,1024]{1,0:T(8,128)(2,1)S(1)} %bitcast.25), channel_id=1, source_target_pairs={{0,1},{1,0},{2,3},{3,2},{4,5},{5,4},{6,7},{7,6},{8,9},{9,8},{10,11... | collective-permute-start | bytes 6291464 | tf_op jit(solution)/shard_map/ppermute | solution.py:134
  202.7 97.4 %all-to-all-start.2 = ((bf16[16,128,1024]{2,1,0:T(8,128)(2,1)}), bf16[16,128,1024]{2,1,0:T(8,128)(2,1)}, u32[]{:S(2)}, u32[]{:S(2)}) async-start(bf16[16,128,1024]{2,1,0:T(8,128)(2,1)} %get-tuple-element.29), calls=%async_computation.2 | async-start | bytes 8388608 | tf_op jit(solution)/shard_map/all_to_all | solution.py:366
  300.0 97.4 %all-to-all-start.3 = ((bf16[16,128,1024]{2,1,0:T(8,128)(2,1)}), bf16[16,128,1024]{2,1,0:T(8,128)(2,1)}, u32[]{:S(2)}, u32[]{:S(2)}) async-start(bf16[16,128,1024]{2,1,0:T(8,128)(2,1)} %get-tuple-element.33), calls=%async_computation.3 | async-start | bytes 8388608 | tf_op jit(solution)/shard_map/all_to_all | solution.py:366
  315.4 47.9 %collective-permute-start.1 = (bf16[1024,1024]{1,0:T(8,128)(2,1)}, bf16[1024,1024]{1,0:T(8,128)(2,1)S(1)}, u32[]{:S(2)}, u32[]{:S(2)}) collective-permute-start(bf16[1024,1024]{1,0:T(8,128)(2,1)} %get-tuple-element.30.refs_0_.refs_4_), channel_id=1, source_target_pairs={{0,1},{1,0},{2,3},{3,2},{4,5},{5,4},{6,7},{7,6},{8,9},{9,8},{10,11... | collective-permute-start | bytes 6291464 | tf_op jit(solution)/shard_map/ppermute | solution.py:134
  363.3 1.3 copy-start.11
  408.8 16.7 %collective-permute-start.3 = (bf16[1024,256]{1,0:T(8,128)(2,1)}, bf16[1024,256]{1,0:T(8,128)(2,1)S(1)}, u32[]{:S(2)}, u32[]{:S(2)}) collective-permute-start(bf16[1024,256]{1,0:T(8,128)(2,1)} %get-tuple-element.38), channel_id=1, source_target_pairs={{0,1},{1,0},{2,3},{3,2},{4,5},{5,4},{6,7},{7,6},{8,9},{9,8},{10,11... | collective-permute-start | bytes 1572872 | tf_op jit(solution)/shard_map/ppermute | solution.py:426
  410.4 19.5 %collective-permute-start.2 = (f32[8,128]{1,0:T(8,128)S(1)}, f32[8,128]{1,0:T(8,128)S(1)}, u32[]{:S(2)}, u32[]{:S(2)}) collective-permute-start(f32[8,128]{1,0:T(8,128)S(1)} %bitcast.26), channel_id=1, source_target_pairs={{0,1},{1,0},{2,3},{3,2},{4,5},{5,4},{6,7},{7,6},{8,9},{9,8},{10,11... | collective-permute-start | bytes 12296 | tf_op jit(solution)/shard_map/ppermute | solution.py:402
  410.9 1.6 copy-start
  415.2 4.8 %copy-start.1 = (bf16[1024,1024]{1,0:T(8,128)(2,1)S(1)}, bf16[1024,1024]{1,0:T(8,128)(2,1)}, u32[]{:S(2)}) copy-start(bf16[1024,1024]{1,0:T(8,128)(2,1)} %get-tuple-element.40.slope) | copy-start | bytes 6291460
  415.2 31.4 %collective-permute-start.6 = (bf16[1024,256]{1,0:T(8,128)(2,1)}, bf16[1024,256]{1,0:T(8,128)(2,1)}, u32[]{:S(2)}, u32[]{:S(2)}) collective-permute-start(bf16[1024,256]{1,0:T(8,128)(2,1)} %shard_map.102), channel_id=1, source_target_pairs={{0,1},{1,0},{2,3},{3,2},{4,5},{5,4},{6,7},{7,6},{8,9},{9,8},{10,11... | collective-permute-start | bytes 1572872 | tf_op jit(solution)/shard_map/ppermute | solution.py:402
  419.4 27.2 %collective-permute-start.5 = (bf16[1024,256]{1,0:T(8,128)(2,1)}, bf16[1024,256]{1,0:T(8,128)(2,1)}, u32[]{:S(2)}, u32[]{:S(2)}) collective-permute-start(bf16[1024,256]{1,0:T(8,128)(2,1)} %shard_map.106), channel_id=1, source_target_pairs={{0,1},{1,0},{2,3},{3,2},{4,5},{5,4},{6,7},{7,6},{8,9},{9,8},{10,11... | collective-permute-start | bytes 1572872 | tf_op jit(solution)/shard_map/ppermute | solution.py:402
  424.2 1.3 copy-start.4
  425.6 4.3 copy-start.6
  428.5 32.5 %collective-permute-start.4 = (bf16[1024,256]{1,0:T(8,128)(2,1)}, bf16[1024,256]{1,0:T(8,128)(2,1)}, u32[]{:S(2)}, u32[]{:S(2)}) collective-permute-start(bf16[1024,256]{1,0:T(8,128)(2,1)} %shard_map.104), channel_id=1, source_target_pairs={{0,1},{1,0},{2,3},{3,2},{4,5},{5,4},{6,7},{7,6},{8,9},{9,8},{10,11... | collective-permute-start | bytes 1572872 | tf_op jit(solution)/shard_map/ppermute | solution.py:402
  429.9 7.5 %copy-start.9 = (f32[1024,1]{1,0:T(8,128)S(1)}, f32[1024,1]{1,0:T(8,128)}, u32[]{:S(2)}) copy-start(f32[1024,1]{1,0:T(8,128)} %get-tuple-element.31.refs_1_) | copy-start | bytes 12292
  429.9 16.7 %copy-start.2 = (bf16[1024,1024]{1,0:T(8,128)(2,1)S(1)}, bf16[1024,1024]{1,0:T(8,128)(2,1)}, u32[]{:S(2)}) copy-start(bf16[1024,1024]{1,0:T(8,128)(2,1)} %get-tuple-element.30.refs_0_.refs_4_) | copy-start | bytes 6291460
  446.6 1.6 copy-start.3
  448.2 1.6 copy-start.5
  449.8 2.2 copy-start.7
  452.0 9.0 %copy-start.8 = (f32[1024,1024]{1,0:T(8,128)S(1)}, f32[1024,1024]{1,0:T(8,128)}, u32[]{:S(2)}) copy-start(f32[1024,1024]{1,0:T(8,128)} %get-tuple-element.42.refs_5_) | copy-start | bytes 12582916

commit v3 on v2

--- a/solution.py
+++ b/solution.py
@@ -14,8 +14,8 @@
 
 MEBI = 1024 * 1024
 RUN = 256
-HALVES = 1
 LIGHT = 16
+HEAVY = 4
 
 f32 = jnp.float32
 bf16 = jnp.bfloat16
@@ -174,10 +174,9 @@
         ],
         out_specs=pl.BlockSpec((1, 1, tile, columns), lambda i: (0, levels - 1, i, 0)),
         out_shape=jax.ShapeDtypeStruct((1, levels, depth, columns), bf16),
-        compiler_params=params(24),
+        compiler_params=params(30),
         cost_estimate=cost(
-            2 * rows * depth * columns // LIGHT,
-            2 * (rows * depth + rows * columns + depth * columns) // LIGHT,
+            2 * rows * depth * columns, 2 * (rows * depth + rows * columns + depth * columns)
         ),
     )(normed, slope)
 
@@ -216,56 +215,63 @@
     )(normed, weight, state)
 
 
-def slope_kernel(factor, width, at, normed, weight, upstream, *rest):
-    slope, share, terms = rest[-3:]
+def slope_kernel(factor, width, at, normed, weight, upstream, slope, share, message):
     pre = jnp.dot(normed[...], weight[...], preferred_element_type=f32) * factor
     value = (upstream[...].astype(f32) * silu_slope(pre)).astype(bf16)
     slope[...] = value
     total = jnp.sum(value.astype(f32) * pre, axis=-1, keepdims=True)
-    share[...] = jnp.broadcast_to(total, share.shape)
+    total = jnp.broadcast_to(total, (total.shape[0], 128)).T[: share.shape[0]]
+    share[...] = total
     start = pl.multiple_of(at[0] * width, width)
     product = lax.dot_general(
         value, weight[pl.ds(start, width), :], OVER_COLUMNS, preferred_element_type=f32
     )
-    terms[...] = (product * factor).astype(terms.dtype)
-
-
-def second_forward(normed, weight, upstream, where, width, factor, half, previous):
+    height = value.shape[0]
+    message[0, :height, :] = (product * factor).astype(message.dtype)
+    high = total.astype(message.dtype)
+    total = total - high.astype(f32)
+    middle = total.astype(message.dtype)
+    low = (total - middle.astype(f32)).astype(message.dtype)
+    at = lax.broadcasted_iota(jnp.int32, total.shape, 0)
+    pieces = jnp.where(at == 0, high.astype(f32), jnp.where(at == 1, middle.astype(f32), 0.0))
+    pieces = jnp.where(at == 2, low.astype(f32), pieces)
+    pieces = jnp.concatenate([pieces, jnp.zeros_like(pieces)], axis=0)
+    message[0, height:, :] = pieces.astype(message.dtype)
+
+
+def second_forward(normed, weight, upstream, where, width, factor):
     rows, depth = normed.shape
     columns = weight.shape[1]
-    tile = min(256, rows // HALVES)
-    steps = rows // HALVES // tile
-    first = half * steps
-    mine = pl.BlockSpec((tile, columns), lambda i, at: (first + i, 0))
+    tile = width
+    steps = rows // tile
+    mine = pl.BlockSpec((tile, columns), lambda i, at: (i, 0))
     return pl.pallas_call(
         functools.partial(slope_kernel, factor, width),
         grid_spec=pltpu.PrefetchScalarGridSpec(
             num_scalar_prefetch=1,
             grid=(steps,),
             in_specs=[
-                pl.BlockSpec((tile, depth), lambda i, at: (first + i, 0)),
+                pl.BlockSpec((tile, depth), lambda i, at: (i, 0)),
                 pl.BlockSpec((depth, columns), lambda i, at: (0, 0)),
                 mine,
-            ]
-            + [pl.BlockSpec(memory_space=pl.ANY)] * len(previous),
+            ],
             out_specs=[
                 mine,
-                pl.BlockSpec((tile, 128), lambda i, at: (first + i, 0)),
-                pl.BlockSpec((tile, width), lambda i, at: (i, 0)),
+                pl.BlockSpec((8, tile), lambda i, at: (0, i)),
+                pl.BlockSpec((1, tile + 16, width), lambda i, at: (i, 0, 0)),
             ],
         ),
         out_shape=[
             jax.ShapeDtypeStruct((rows, columns), bf16),
-            jax.ShapeDtypeStruct((rows, 128), f32),
-            jax.ShapeDtypeStruct((rows // HALVES, width), bf16),
+            jax.ShapeDtypeStruct((8, rows), f32),
+            jax.ShapeDtypeStruct((steps, tile + 16, width), bf16),
         ],
-        input_output_aliases={4 + n: n for n in range(len(previous))},
         compiler_params=params(),
         cost_estimate=cost(
-            2 * rows // HALVES * columns * (depth + width) // LIGHT,
-            2 * (rows // HALVES * (depth + 2 * columns) + depth * columns) // LIGHT,
-        ),
-    )(where.reshape(1).astype(jnp.int32), normed, weight, upstream, *previous)
+            2 * rows * columns * (depth + width) // LIGHT,
+            2 * (rows * (depth + 2 * columns) + depth * columns) // LIGHT,
+        ),
+    )(where.reshape(1).astype(jnp.int32), normed, weight, upstream)
 
 
 def term_kernel(factor, where, slope, weight, out):
@@ -288,7 +294,7 @@
             out_specs=pl.BlockSpec((tile, width), lambda i, at: (i, 0)),
         ),
         out_shape=jax.ShapeDtypeStruct((rows, width), bf16),
-        compiler_params=params(24),
+        compiler_params=params(30),
         cost_estimate=cost(
             2 * rows * columns * width // LIGHT,
             2 * (rows * columns + columns * width + rows * width) // LIGHT,
@@ -296,51 +302,65 @@
     )(where.reshape(1).astype(jnp.int32), slope, weight)
 
 
-def first_kernel(factor, cells, *refs):
+def first_kernel(factor, runs, *refs):
     normed, scale, share, upstream, state, gate, kept = refs[:7]
-    terms = refs[7:-3]
-    out, slope = refs[-2:]
-    count = len(terms) // len(cells)
-
-    @pl.when(pl.program_id(0) == 0)
+    terms = refs[7:-4]
+    out, slope, total = refs[-3:]
+    tile, columns = slope.shape
+    width = columns // runs
+    count = len(terms) // runs
+    step = pl.program_id(0)
+    last = pl.num_programs(0) - 1
+    for run in range(runs):
+        here = slice(run * width, (run + 1) * width)
+        normed_grad = kept[:, here].astype(f32)
+        for other in terms[run * count : (run + 1) * count]:
+            arrived = other[0, :tile, :] if len(other.shape) == 3 else other[...]
+            normed_grad = normed_grad + arrived.astype(f32)
+        state_grad = (
+            upstream[:, here].astype(f32)
+            + scale[...] * normed_grad
+            - state[:, here].astype(f32) * share[...]
+        )
+        slope[:, here] = (state_grad * gate[:, here]).astype(bf16)
+    product = lax.dot_general(normed[...], slope[...], OVER_ROWS, preferred_element_type=f32)
+
+    @pl.when(step == 0)
     def _():
-        for number, (top, height, left, width) in enumerate(cells):
-            span = slice(top, top + height)
-            here = slice(left, left + width)
-            normed_grad = kept[span, here].astype(f32)
-            for other in terms[number * count : (number + 1) * count]:
-                normed_grad = normed_grad + other[...].astype(f32)
-            state_grad = (
-                upstream[span, here].astype(f32)
-                + scale[span, :] * normed_grad
-                - state[span, here].astype(f32) * share[span, :]
-            )
-            slope[span, here] = (state_grad * gate[span, here]).astype(bf16)
-
-    product = lax.dot_general(normed[...], slope[...], OVER_ROWS, preferred_element_type=f32)
-    out[...] = (product * factor).astype(out.dtype).reshape(out.shape)
-
-
-def first_level_grad(normed, scale, share, mine, cells, terms, block, width, factor, grads, mebi):
+        total[...] = product
+
+    @pl.when(jnp.logical_and(step > 0, step < last))
+    def _():
+        total[...] = total[...] + product
+
+    @pl.when(step == last)
+    def _():
+        whole = jnp.where(step > 0, total[...] + product, product)
+        out[...] = (whole * factor).astype(out.dtype).reshape(out.shape)
+
+
+def first_level_grad(normed, scale, share, mine, terms, runs, block, width, tile, factor, grads):
     rows, depth = normed.shape
-    tile = min(512, depth)
-    column = pl.BlockSpec((rows, 1), lambda i: (0, 0))
-    part = pl.BlockSpec((rows, width), lambda i: (0, block))
-    return pl.pallas_call(
-        functools.partial(first_kernel, factor, cells),
-        grid=(depth // tile,),
-        in_specs=[pl.BlockSpec((rows, tile), lambda i: (0, i)), column, column]
+    columns = runs * width
+    column = pl.BlockSpec((tile, 1), lambda i: (i, 0))
+    part = pl.BlockSpec((tile, columns), lambda i: (i, block))
+    message = pl.BlockSpec((1, tile + 16, width), lambda i: (i, 0, 0))
+    plain = pl.BlockSpec((tile, width), lambda i: (i, 0))
+    return pl.pallas_call(
+        functools.partial(first_kernel, factor, runs),
+        grid=(rows // tile,),
+        in_specs=[pl.BlockSpec((tile, depth), lambda i: (i, 0)), column, column]
         + [part] * len(mine)
-        + [pl.BlockSpec(value.shape, lambda i: (0, 0)) for value in terms]
+        + [message if value.ndim == 3 else plain for value in terms]
         + [pl.BlockSpec(memory_space=pl.ANY)],
-        out_specs=pl.BlockSpec((1, 1, tile, width), lambda i: (0, 0, i, block)),
+        out_specs=pl.BlockSpec((1, 1, depth, columns), lambda i: (0, 0, 0, block)),
         out_shape=jax.ShapeDtypeStruct(grads.shape, bf16),
-        scratch_shapes=[pltpu.VMEM((rows, width), bf16)],
+        scratch_shapes=[pltpu.VMEM((tile, columns), bf16), pltpu.VMEM((depth, columns), f32)],
         input_output_aliases={3 + len(mine) + len(terms): 0},
-        compiler_params=params(mebi),
+        compiler_params=params(44),
         cost_estimate=cost(
-            2 * rows * depth * width // LIGHT,
-            2 * (rows * depth + 7 * rows * width + depth * width) // LIGHT,
+            2 * rows * depth * columns * HEAVY,
+            2 * (rows * depth + 7 * rows * columns + depth * columns) * HEAVY,
         ),
     )(normed, scale, share, *mine, *terms, grads)
 
@@ -407,71 +427,48 @@
         ]
 
     rows = second_normed.shape[0]
-    previous = ()
-    leading = []
-    for half in range(HALVES):
-        slope, share, terms = second_forward(
-            second_normed,
-            second_weight,
-            upstream,
-            place_of(1, 0),
-            width,
-            factor,
-            half,
-            previous,
-        )
-        previous = (slope, share)
-        leading.append(terms)
-    own_share = share[:, 0].reshape(-1, 128)
-    leading = [lax.ppermute(after(terms, own_share), "mp", around(parts, 1)) for terms in leading]
-    share = own_share
-    for other in send([own_share] * (parts - 1)):
-        share = share + other
-    sent = terms_of(slope, 0, range(2, parts))
-    rest = [lax.ppermute(value, "mp", around(parts, n + 2)) for n, value in enumerate(sent)]
-    height = rows // HALVES
-    arrived = [[]]
-    for half in range(HALVES):
-        arrived[0].append(
-            (
-                half * height,
-                height,
-                [leading[half]] + [value[half * height : (half + 1) * height] for value in rest],
-            )
-        )
-    last = slope
+    slope, own_share, message = second_forward(
+        second_normed, second_weight, upstream, place_of(1, 0), width, factor
+    )
+    message = lax.ppermute(message, "mp", around(parts, 1))
+    share = own_share[0] + jnp.sum(message[:, width : width + 3].astype(f32), axis=1).reshape(-1)
+    arrived = [[message]]
+    for step in range(2, parts):
+        share = share + lax.ppermute(own_share, "mp", around(parts, step))[0]
+        [value] = terms_of(slope, 0, [step])
+        arrived[0].append(lax.ppermute(value, "mp", around(parts, step)))
     source = slope
-    for run in range(1, runs):
-        if run == 3:
-            kept = term(after(slope, last), second_weight, place, own_features, factor)
-            source = after(slope, kept, *leading)
-        sent = terms_of(source, run, range(1, parts))
-        last = sent[0]
-        arrived.append([(0, rows, send(sent))])
-    if runs <= 3:
-        kept = term(after(slope, last), second_weight, place, own_features, factor)
-    grads = last_level_grad(second_normed, after(slope, last), factor, levels)
+    kept = grads = None
+    for run in range(1, runs + 2):
+        if run < runs:
+            sent = terms_of(source, run, range(1, parts))
+            arrived.append(send(sent))
+            source = after(slope, sent[0])
+        if kept is None:
+            kept = term(source, second_weight, place, own_features, factor)
+            source = after(slope, kept)
+        elif grads is None:
+            grads = last_level_grad(second_normed, source, factor, levels)
+            source = after(slope, grads)
+        if run < runs:
+            source = after(source, *arrived[run - 1])
     scaled = second_scale**2 * after(share, grads).reshape(rows, 1) / depth
     mine = [upstream, second_state, gate, kept]
     bounds = [0, runs - 1, runs] if runs > 1 else [0, runs]
     for begin, end in zip(bounds[:-1], bounds[1:]):
-        cells, terms = [], []
-        for run in range(begin, end):
-            for top, tall, values in arrived[run]:
-                cells.append((top, tall, (run - begin) * width, width))
-                terms += values
+        terms = [value for run in range(begin, end) for value in arrived[run]]
         grads = first_level_grad(
             first_normed,
             second_scale,
             scaled,
             mine,
-            cells,
             terms,
+            end - begin,
             begin // (end - begin),
-            (end - begin) * width,
+            width,
+            width,
             factor,
             grads,
-            24 if end == runs else 40,
         )
     return (new_anchor, new_momentum, grads)
 

time: 467 us -> 464 us (level)
    unnamed x28 -> x35, local copies, waits for them, and re-layouts: 9.62 us -> 5.94 us
  transfers between devices with their start and end apart: 11 -> 10, of which waited for: 7 -> 8; matrix products, arithmetic and copies ran while one was open for 1% -> 1% of each run, Pallas kernels for 18% -> 18%
where the time goes in v3:
time: 464 us; the launch traced here: 463 us
  waiting for transfers between devices  319 us (69%)
  Pallas kernels  106 us (23%)
  starting transfers between devices  28.1 us (6%)
  local copies, waits for them, and re-layouts  8.44 us (2%)
    all_to_all x4, waiting for transfers between devices, exchange(): lax.all_to_all(blocks, 'group', split_axis=0, concat_axis=0, tiled=True)  218 us
    ppermute x2, waiting for transfers between devices, normalize(): lax.ppermute(own, 'mp', around(parts, step))  92.1 us
    pallas_call x2, Pallas kernels, outer_update(): pl.pallas_call(functools.partial(update_kernel, groups, mods, aliased), g...  21.7 us
    all_to_all x4, starting transfers between devices, exchange(): lax.all_to_all(blocks, 'group', split_axis=0, concat_axis=0, tiled=True)  20.2 us
    pallas_call x2, Pallas kernels, normalize(): pl.pallas_call(functools.partial(norm_kernel, parts, depth), grid_spec=pl...  17.8 us
    pallas_call x2, Pallas kernels, first_level_grad(): pl.pallas_call(functools.partial(first_kernel, factor, runs), grid=(rows...  17.1 us
    pallas_call x2, Pallas kernels, cast_level(): pl.pallas_call(cast_kernel, grid=(groups // per,), in_specs=[pl.BlockSpec...  11.6 us
    pallas_call x1, Pallas kernels, first_forward(): pl.pallas_call(functools.partial(state_kernel, factor), grid=(rows // til...  10.7 us
  transfers between devices with their start and end apart: 10, of which 8 were waited for; matrix products, arithmetic and copies ran while one was open for 1% of the time, Pallas kernels for 18%

profile of v3, /device:TPU:16, one launch (start us, length us, event | category | flops | bytes accessed | tf_op | source)
XLA Modules:
  0.0 463.1 jit_solution(8201045068594888661)
XLA Ops:
  0.6 5.8 %shard_map.95 = bf16[16,128,1024]{2,1,0:T(8,128)(2,1)} custom-call(f32[1,2,2048,1024]{3,2,1,0:T(8,128)} %src.3), custom_call_target="tpu_custom_call" | custom-call | bytes 12582912 | tf_op jit(solution)/shard_map/pallas_call | solution.py:41
  6.4 6.2 %all-to-all-start.1 = ((bf16[16,128,1024]{2,1,0:T(8,128)(2,1)}), bf16[16,128,1024]{2,1,0:T(8,128)(2,1)}, u32[]{:S(2)}, u32[]{:S(2)}) async-start(bf16[16,128,1024]{2,1,0:T(8,128)(2,1)} %shard_map.95), calls=%async_computation.1 | async-start | bytes 8388608 | tf_op jit(solution)/shard_map/all_to_all | solution.py:386
  12.6 5.8 %shard_map.94 = bf16[16,128,1024]{2,1,0:T(8,128)(2,1)} custom-call(f32[1,2,2048,1024]{3,2,1,0:T(8,128)} %src.3), custom_call_target="tpu_custom_call" | custom-call | bytes 12582912 | tf_op jit(solution)/shard_map/pallas_call | solution.py:41
  18.4 0.0 copy-start.13
  18.4 0.0 copy-start.15
  18.4 0.0 copy-start.16
  18.4 86.9 %all-to-all-done.1.received = bf16[16,128,1024]{2,1,0:T(8,128)(2,1)} async-done(((bf16[16,128,1024]{2,1,0:T(8,128)(2,1)}), bf16[16,128,1024]{2,1,0:T(8,128)(2,1)}, u32[]{:S(2)}, u32[]{:S(2)}) %all-to-all-start.1) | async-done | bytes 4194336 | tf_op jit(solution)/shard_map/all_to_all | solution.py:386
  105.3 4.7 %all-to-all-start = ((bf16[16,128,1024]{2,1,0:T(8,128)(2,1)}), bf16[16,128,1024]{2,1,0:T(8,128)(2,1)}, u32[]{:S(2)}, u32[]{:S(2)}) async-start(bf16[16,128,1024]{2,1,0:T(8,128)(2,1)} %shard_map.94), calls=%async_computation | async-start | bytes 8388608 | tf_op jit(solution)/shard_map/all_to_all | solution.py:386
  110.0 0.0 copy-done.13
  110.0 1.6 collective-permute-start
  111.5 0.0 copy-done.15
  111.5 0.0 copy-done.16
  111.5 0.6 slice_bitcast_fusion
  112.1 45.7 %collective-permute-done.refs_1_ = bf16[1024,1024]{1,0:T(8,128)(2,1)} collective-permute-done((bf16[1024,1024]{1,0:T(8,128)(2,1)S(1)}, bf16[1024,1024]{1,0:T(8,128)(2,1)}, u32[]{:S(2)}, u32[]{:S(2)}) %collective-permute-start) | collective-permute-done | bytes 2097184 | tf_op jit(solution)/shard_map/ppermute | solution.py:134
  157.8 8.9 %shard_map.96 = (bf16[1024,2048]{1,0:T(8,128)(2,1)}, f32[1024,1]{1,0:T(8,128)}) custom-call(s32[1]{0:T(128)} %bitcast.4.place.where, bf16[1024,1024]{1,0:T(8,128)(2,1)} %bitcast.24, bf16[1024,1024]{1,0:T(8,128)(2,1)} %collective-permute-done.refs_1_), custom_call_target="tpu_custom_call" | custom-call | bytes 8388608 | tf_op jit(solution)/shard_map/pallas_call | solution.py:137
  166.7 10.9 %shard_map.97 = (f32[16,128,1024]{2,1,0:T(8,128)}, f32[16,128,1024]{2,1,0:T(8,128)}, bf16[16,128,1024]{2,1,0:T(8,128)(2,1)}) custom-call(s32[16]{0:T(128)} %get-tuple-element.52.old, s32[16]{0:T(128)} %get-tuple-element.47.new, bf16[16,128,1024]{2,1,0:T(8,128)(2,1)} %all-to-all-done.1.received, f32[16,128,1024]{2,1,0:T(8,128)} %anchor.3, ...), custom_call_target="tpu_custom_call" | custom-call | bytes 25165824 | tf_op jit(solution)/shard_map/pallas_call | solution.py:83
  177.6 25.1 %all-to-all-done.received = bf16[16,128,1024]{2,1,0:T(8,128)(2,1)} async-done(((bf16[16,128,1024]{2,1,0:T(8,128)(2,1)}), bf16[16,128,1024]{2,1,0:T(8,128)(2,1)}, u32[]{:S(2)}, u32[]{:S(2)}) %all-to-all-start) | async-done | bytes 4194336 | tf_op jit(solution)/shard_map/all_to_all | solution.py:386
  202.7 4.7 %all-to-all-start.2 = ((bf16[16,128,1024]{2,1,0:T(8,128)(2,1)}), bf16[16,128,1024]{2,1,0:T(8,128)(2,1)}, u32[]{:S(2)}, u32[]{:S(2)}) async-start(bf16[16,128,1024]{2,1,0:T(8,128)(2,1)} %get-tuple-element.31), calls=%async_computation.2 | async-start | bytes 8388608 | tf_op jit(solution)/shard_map/all_to_all | solution.py:386
  207.3 10.8 %shard_map.98 = (f32[16,128,1024]{2,1,0:T(8,128)}, f32[16,128,1024]{2,1,0:T(8,128)}, bf16[16,128,1024]{2,1,0:T(8,128)(2,1)}) custom-call(s32[16]{0:T(128)} %get-tuple-element.51.old, s32[16]{0:T(128)} %get-tuple-element.48.new, bf16[16,128,1024]{2,1,0:T(8,128)(2,1)} %all-to-all-done.received, ...), custom_call_target="tpu_custom_call", output_to_operand_aliasing={{0}: (5, {}), {1}: (6, {})} | custom-call | bytes 25165824 | tf_op jit(solution)/shard_map/pallas_call | solution.py:83
  218.2 81.9 %all-to-all-done.2 = bf16[16,128,1024]{2,1,0:T(8,128)(2,1)} async-done(((bf16[16,128,1024]{2,1,0:T(8,128)(2,1)}), bf16[16,128,1024]{2,1,0:T(8,128)(2,1)}, u32[]{:S(2)}, u32[]{:S(2)}) %all-to-all-start.2) | async-done | bytes 4194336 | tf_op jit(solution)/shard_map/all_to_all | solution.py:386
  300.0 4.7 %all-to-all-start.3 = ((bf16[16,128,1024]{2,1,0:T(8,128)(2,1)}), bf16[16,128,1024]{2,1,0:T(8,128)(2,1)}, u32[]{:S(2)}, u32[]{:S(2)}) async-start(bf16[16,128,1024]{2,1,0:T(8,128)(2,1)} %get-tuple-element.35), calls=%async_computation.3 | async-start | bytes 8388608 | tf_op jit(solution)/shard_map/all_to_all | solution.py:386
  304.7 10.7 %shard_map.99 = (bf16[1024,1024]{1,0:T(8,128)(2,1)}, f32[1024,1024]{1,0:T(8,128)}) custom-call(bf16[1024,2048]{1,0:T(8,128)(2,1)} %get-tuple-element.25.normed.refs_0_, bf16[2048,1024]{1,0:T(8,128)(2,1)} %bitcast.6.weight, bf16[1024,1024]{1,0:T(8,128)(2,1)} %bitcast.25), custom_call_target="tpu_custom_call" | custom-call | flops 4294967296 | bytes 16777216 | tf_op jit(solution)/shard_map/pallas_call | solution.py:196
  315.4 1.5 collective-permute-start.1
  316.9 46.4 %collective-permute-done.1.refs_1_ = bf16[1024,1024]{1,0:T(8,128)(2,1)S(1)} collective-permute-done((bf16[1024,1024]{1,0:T(8,128)(2,1)}, bf16[1024,1024]{1,0:T(8,128)(2,1)S(1)}, u32[]{:S(2)}, u32[]{:S(2)}) %collective-permute-start.1) | collective-permute-done | bytes 2097184 | tf_op jit(solution)/shard_map/ppermute | solution.py:134
  363.3 1.3 copy-done.14
  364.6 8.9 %shard_map.100 = (bf16[1024,2048]{1,0:T(8,128)(2,1)}, f32[1024,1]{1,0:T(8,128)}) custom-call(s32[1]{0:T(128)} %bitcast.4.place.where, bf16[1024,1024]{1,0:T(8,128)(2,1)} %get-tuple-element.32.refs_0_.refs_4_, bf16[1024,1024]{1,0:T(8,128)(2,1)} %copy-done.14), custom_call_target="tpu_custom_call" | custom-call | bytes 8388608 | tf_op jit(solution)/shard_map/pallas_call | solution.py:137
  373.5 23.9 %all-to-all-done.3 = bf16[16,128,1024]{2,1,0:T(8,128)(2,1)} async-done(((bf16[16,128,1024]{2,1,0:T(8,128)(2,1)}), bf16[16,128,1024]{2,1,0:T(8,128)(2,1)}, u32[]{:S(2)}, u32[]{:S(2)}) %all-to-all-start.3) | async-done | bytes 4194336 | tf_op jit(solution)/shard_map/all_to_all | solution.py:386
  397.4 10.2 %shard_map.101 = (bf16[1024,1024]{1,0:T(8,128)(2,1)}, f32[8,1024]{1,0:T(8,128)}, bf16[4,272,256]{2,1,0:T(8,128)(2,1)}) custom-call(s32[1]{0:T(128)} %bitcast.7.at, bf16[1024,2048]{1,0:T(8,128)(2,1)} %get-tuple-element.34.normed, bf16[2048,1024]{1,0:T(8,128)(2,1)} %bitcast.8.weight, bf16[1024,1024]{1,0:T(8,128)(2,1)} %bitcast.21), custom_call_target="tpu_custom_call" | custom-call | flops 301989888 | bytes 786432 | tf_op jit(solution)/shard_map/pallas_call | solution.py:248
  407.6 1.5 collective-permute-start.2
  409.1 0.0 copy-start
  409.1 1.6 copy-done
  410.7 2.2 shard_map.102
  412.8 0.6 collective-permute-start.3
  413.4 0.0 copy-done.1
  413.4 4.2 shard_map.103.refs_6_
  417.6 0.0 copy-start.4
  417.6 1.3 copy-done.4
  419.0 0.9 slice.22
  419.9 3.5 collective-permute-done.2.refs_7_
  423.3 0.8 copy-done.8
  424.2 2.0 shard_map.104
  426.2 1.6 collective-permute-start.5
  427.7 0.7 convert_reduce_fusion
  428.5 0.0 copy-done.6
  428.5 6.5 %shard_map.105.refs_10_ = bf16[1,2,2048,1024]{3,2,1,0:T(8,128)(2,1)} custom-call(bf16[1024,2048]{1,0:T(8,128)(2,1)S(1)} %copy-done.6, bf16[1024,1024]{1,0:T(8,128)(2,1)S(1)} %copy-done.1), custom_call_target="tpu_custom_call" | custom-call | flops 4294967296 | bytes 10485760 | tf_op jit(solution)/shard_map/pallas_call | solution.py:168
  435.0 0.0 collective-permute-done.3.refs_8_
  435.0 0.8 copy-done.10
  435.8 1.0 copy.14
  436.8 0.0 copy-start.9
  436.8 0.0 copy-start.11
  436.8 2.2 shard_map.106
  439.0 1.2 collective-permute-start.4
  440.2 0.0 copy-done.7
  440.2 0.0 copy-done.12
  440.2 0.1 multiply_multiply_fusion.refs_2_
  440.3 5.6 %collective-permute-done.5.refs_9_ = bf16[1024,256]{1,0:T(8,128)(2,1)} collective-permute-done((bf16[1024,256]{1,0:T(8,128)(2,1)S(1)}, bf16[1024,256]{1,0:T(8,128)(2,1)}, u32[]{:S(2)}, u32[]{:S(2)}) %collective-permute-start.5) | collective-permute-done | bytes 524320 | tf_op jit(solution)/shard_map/ppermute | solution.py:422
  445.9 0.0 copy-done.2
  445.9 0.0 copy-done.3
  445.9 0.0 copy-done.5
  445.9 0.0 copy-done.9
  445.9 0.0 copy-done.11
  445.9 11.0 %shard_map.107.refs_8_ = bf16[1,2,2048,1024]{3,2,1,0:T(8,128)(2,1)} custom-call(bf16[1024,2048]{1,0:T(8,128)(2,1)} %get-tuple-element.25.normed.refs_0_, f32[1024,1]{1,0:T(8,128)S(1)} %copy-done.7, f32[1024,1]{1,0:T(8,128)S(1)} %multiply_multiply_fusion.refs_2_, bf16[1024,1024]{1,0:T(8,128)(2,1)S(1)} %bitcast.22, ...), custom_call_target="tpu_custom_call", output_to_operand_aliasing={{}: (10, {})} | custom-call | flops 12884901888 | bytes 73400320 | tf_op jit(solution)/shard_map/pallas_call | solution.py:349
  457.0 0.0 collective-permute-done.4.refs_7_
  457.0 6.1 %shard_map.108 = bf16[1,2,2048,1024]{3,2,1,0:T(8,128)(2,1)} custom-call(bf16[1024,2048]{1,0:T(8,128)(2,1)} %get-tuple-element.25.normed.refs_0_, f32[1024,1]{1,0:T(8,128)S(1)} %copy-done.7, f32[1024,1]{1,0:T(8,128)S(1)} %multiply_multiply_fusion.refs_2_, bf16[1024,1024]{1,0:T(8,128)(2,1)S(1)} %bitcast.23, ...), custom_call_target="tpu_custom_call", output_to_operand_aliasing={{}: (8, {})} | custom-call | flops 4294967296 | bytes 35651584 | tf_op jit(solution)/shard_map/pallas_call | solution.py:349
  (12 shorter events, 0.0 us)
Async XLA Ops:
  6.4 98.9 %all-to-all-start.1 = ((bf16[16,128,1024]{2,1,0:T(8,128)(2,1)}), bf16[16,128,1024]{2,1,0:T(8,128)(2,1)}, u32[]{:S(2)}, u32[]{:S(2)}) async-start(bf16[16,128,1024]{2,1,0:T(8,128)(2,1)} %shard_map.95), calls=%async_computation.1 | async-start | bytes 8388608 | tf_op jit(solution)/shard_map/all_to_all | solution.py:386
  18.4 91.6 %copy-start.13 = (bf16[1,1024,1024]{2,1,0:T(8,128)(2,1)S(1)}, bf16[1,1024,1024]{2,1,0:T(8,128)(2,1)}, u32[]{:S(2)}) copy-start(bf16[1,1024,1024]{2,1,0:T(8,128)(2,1)} %param.12) | copy-start | bytes 6291460
  18.4 93.2 %copy-start.15 = (s32[16,2]{0,1:T(2,128)S(1)}, s32[16,2]{0,1:T(2,128)}, u32[]{:S(2)}) copy-start(s32[16,2]{0,1:T(2,128)} %param.11) | copy-start | bytes 388
  18.4 93.2 %copy-start.16 = (s32[16,2]{0,1:T(2,128)S(1)}, s32[16,2]{0,1:T(2,128)}, u32[]{:S(2)}) copy-start(s32[16,2]{0,1:T(2,128)} %param.10) | copy-start | bytes 388
  105.3 97.4 %all-to-all-start = ((bf16[16,128,1024]{2,1,0:T(8,128)(2,1)}), bf16[16,128,1024]{2,1,0:T(8,128)(2,1)}, u32[]{:S(2)}, u32[]{:S(2)}) async-start(bf16[16,128,1024]{2,1,0:T(8,128)(2,1)} %shard_map.94), calls=%async_computation | async-start | bytes 8388608 | tf_op jit(solution)/shard_map/all_to_all | solution.py:386
  110.0 47.9 %collective-permute-start = (bf16[1024,1024]{1,0:T(8,128)(2,1)S(1)}, bf16[1024,1024]{1,0:T(8,128)(2,1)}, u32[]{:S(2)}, u32[]{:S(2)}) collective-permute-start(bf16[1024,1024]{1,0:T(8,128)(2,1)S(1)} %bitcast.26), channel_id=1, source_target_pairs={{0,1},{1,0},{2,3},{3,2},{4,5},{5,4},{6,7},{7,6},{8,9},{9,8},{10,11... | collective-permute-start | bytes 6291464 | tf_op jit(solution)/shard_map/ppermute | solution.py:134
  202.7 97.4 %all-to-all-start.2 = ((bf16[16,128,1024]{2,1,0:T(8,128)(2,1)}), bf16[16,128,1024]{2,1,0:T(8,128)(2,1)}, u32[]{:S(2)}, u32[]{:S(2)}) async-start(bf16[16,128,1024]{2,1,0:T(8,128)(2,1)} %get-tuple-element.31), calls=%async_computation.2 | async-start | bytes 8388608 | tf_op jit(solution)/shard_map/all_to_all | solution.py:386
  300.0 97.4 %all-to-all-start.3 = ((bf16[16,128,1024]{2,1,0:T(8,128)(2,1)}), bf16[16,128,1024]{2,1,0:T(8,128)(2,1)}, u32[]{:S(2)}, u32[]{:S(2)}) async-start(bf16[16,128,1024]{2,1,0:T(8,128)(2,1)} %get-tuple-element.35), calls=%async_computation.3 | async-start | bytes 8388608 | tf_op jit(solution)/shard_map/all_to_all | solution.py:386
  315.4 47.9 %collective-permute-start.1 = (bf16[1024,1024]{1,0:T(8,128)(2,1)}, bf16[1024,1024]{1,0:T(8,128)(2,1)S(1)}, u32[]{:S(2)}, u32[]{:S(2)}) collective-permute-start(bf16[1024,1024]{1,0:T(8,128)(2,1)} %get-tuple-element.32.refs_0_.refs_4_), channel_id=1, source_target_pairs={{0,1},{1,0},{2,3},{3,2},{4,5},{5,4},{6,7},{7,6},{8,9},{9,8},{10,11... | collective-permute-start | bytes 6291464 | tf_op jit(solution)/shard_map/ppermute | solution.py:134
  363.3 1.3 copy-start.14
  407.6 15.8 %collective-permute-start.2 = (bf16[4,272,256]{2,1,0:T(8,128)(2,1)}, bf16[4,272,256]{2,1,0:T(8,128)(2,1)S(1)}, u32[]{:S(2)}, u32[]{:S(2)}) collective-permute-start(bf16[4,272,256]{2,1,0:T(8,128)(2,1)} %get-tuple-element.37), channel_id=1, source_target_pairs={{0,1},{1,0},{2,3},{3,2},{4,5},{5,4},{6,7},{7,6},{8,9},{9,8},{10,11... | collective-permute-start | bytes 1671176 | tf_op jit(solution)/shard_map/ppermute | solution.py:433
  409.1 1.6 copy-start
  410.7 2.8 copy-start.1
  412.8 22.1 %collective-permute-start.3 = (bf16[1024,256]{1,0:T(8,128)(2,1)S(1)}, bf16[1024,256]{1,0:T(8,128)(2,1)S(1)}, u32[]{:S(2)}, u32[]{:S(2)}) collective-permute-start(bf16[1024,256]{1,0:T(8,128)(2,1)S(1)} %shard_map.102), channel_id=1, source_target_pairs={{0,1},{1,0},{2,3},{3,2},{4,5},{5,4},{6,7},{7,6},{8,9},{9,8},{10,11... | collective-permute-start | bytes 1572872 | tf_op jit(solution)/shard_map/ppermute | solution.py:422
  417.6 1.3 copy-start.4
  418.9 9.5 %copy-start.6 = (bf16[1024,2048]{1,0:T(8,128)(2,1)S(1)}, bf16[1024,2048]{1,0:T(8,128)(2,1)}, u32[]{:S(2)}) copy-start(bf16[1024,2048]{1,0:T(8,128)(2,1)} %get-tuple-element.34.normed) | copy-start | bytes 12582916
  423.3 0.8 copy-start.8
  426.2 19.7 %collective-permute-start.5 = (bf16[1024,256]{1,0:T(8,128)(2,1)S(1)}, bf16[1024,256]{1,0:T(8,128)(2,1)}, u32[]{:S(2)}, u32[]{:S(2)}) collective-permute-start(bf16[1024,256]{1,0:T(8,128)(2,1)S(1)} %shard_map.104), channel_id=1, source_target_pairs={{0,1},{1,0},{2,3},{3,2},{4,5},{5,4},{6,7},{7,6},{8,9},{9,8},{10,11... | collective-permute-start | bytes 1572872 | tf_op jit(solution)/shard_map/ppermute | solution.py:422
  435.0 5.2 %copy-start.7 = (f32[1024,1]{1,0:T(8,128)S(1)}, f32[1024,1]{1,0:T(8,128)}, u32[]{:S(2)}) copy-start(f32[1024,1]{1,0:T(8,128)} %get-tuple-element.33.refs_1_) | copy-start | bytes 12292
  435.0 0.8 copy-start.10
  436.8 3.4 copy-start.12
  436.8 9.1 %copy-start.2 = (bf16[1024,1024]{1,0:T(8,128)(2,1)S(1)}, bf16[1024,1024]{1,0:T(8,128)(2,1)}, u32[]{:S(2)}) copy-start(bf16[1024,1024]{1,0:T(8,128)(2,1)} %get-tuple-element.32.refs_0_.refs_4_) | copy-start | bytes 6291460
  436.8 9.1 %copy-start.3 = (bf16[1,1024,1024]{2,1,0:T(8,128)(2,1)S(1)}, bf16[1,1024,1024]{2,1,0:T(8,128)(2,1)}, u32[]{:S(2)}) copy-start(bf16[1,1024,1024]{2,1,0:T(8,128)(2,1)} %param.13) | copy-start | bytes 6291460
  436.8 9.1 %copy-start.5 = (bf16[1024,1024]{1,0:T(8,128)(2,1)S(1)}, bf16[1024,1024]{1,0:T(8,128)(2,1)}, u32[]{:S(2)}) copy-start(bf16[1024,1024]{1,0:T(8,128)(2,1)} %copy-done.4) | copy-start | bytes 6291460
  436.8 9.1 %copy-start.9 = (bf16[4,272,256]{2,1,0:T(8,128)(2,1)S(1)}, bf16[4,272,256]{2,1,0:T(8,128)(2,1)}, u32[]{:S(2)}) copy-start(bf16[4,272,256]{2,1,0:T(8,128)(2,1)} %copy-done.8) | copy-start | bytes 1671172
  436.8 9.1 %copy-start.11 = (bf16[1024,256]{1,0:T(8,128)(2,1)S(1)}, bf16[1024,256]{1,0:T(8,128)(2,1)}, u32[]{:S(2)}) copy-start(bf16[1024,256]{1,0:T(8,128)(2,1)} %copy-done.10) | copy-start | bytes 1572868
  439.0 17.9 %collective-permute-start.4 = (bf16[1024,256]{1,0:T(8,128)(2,1)S(1)}, bf16[1024,256]{1,0:T(8,128)(2,1)S(1)}, u32[]{:S(2)}, u32[]{:S(2)}) collective-permute-start(bf16[1024,256]{1,0:T(8,128)(2,1)S(1)} %shard_map.106), channel_id=1, source_target_pairs={{0,1},{1,0},{2,3},{3,2},{4,5},{5,4},{6,7},{7,6},{8,9},{9,8},{10,11... | collective-permute-start | bytes 1572872 | tf_op jit(solution)/shard_map/ppermute | solution.py:422

commit v4 on v3

--- a/solution.py
+++ b/solution.py
@@ -37,7 +37,7 @@
 def cast_level(deltas, level, groups):
     _, _, depth, columns = deltas.shape
     rows = depth // groups
-    per = 4 if groups % 4 == 0 else 1
+    per = 8 if groups % 8 == 0 else 1
     return pl.pallas_call(
         cast_kernel,
         grid=(groups // per,),

time: 464 us -> 463 us (level)
  no operation moved by 1% of the time
where the time goes in v4:
time: 463 us; the launch traced here: 462 us
  waiting for transfers between devices  320 us (69%)
  Pallas kernels  105 us (23%)
  starting transfers between devices  28.1 us (6%)
  local copies, waits for them, and re-layouts  8.44 us (2%)
    all_to_all x4, waiting for transfers between devices, exchange(): lax.all_to_all(blocks, 'group', split_axis=0, concat_axis=0, tiled=True)  218 us
    ppermute x2, waiting for transfers between devices, normalize(): lax.ppermute(own, 'mp', around(parts, step))  92.1 us
    pallas_call x2, Pallas kernels, outer_update(): pl.pallas_call(functools.partial(update_kernel, groups, mods, aliased), g...  21.7 us
    all_to_all x4, starting transfers between devices, exchange(): lax.all_to_all(blocks, 'group', split_axis=0, concat_axis=0, tiled=True)  20.2 us
    pallas_call x2, Pallas kernels, normalize(): pl.pallas_call(functools.partial(norm_kernel, parts, depth), grid_spec=pl...  17.8 us
    pallas_call x2, Pallas kernels, first_level_grad(): pl.pallas_call(functools.partial(first_kernel, factor, runs), grid=(rows...  17.1 us
    pallas_call x1, Pallas kernels, first_forward(): pl.pallas_call(functools.partial(state_kernel, factor), grid=(rows // til...  10.7 us
    pallas_call x4, Pallas kernels, term(): pl.pallas_call(functools.partial(term_kernel, factor), grid_spec=pltpu.Pr...  10.5 us
  transfers between devices with their start and end apart: 10, of which 8 were waited for; matrix products, arithmetic and copies ran while one was open for 1% of the time, Pallas kernels for 18%

profile of v4, /device:TPU:16, one launch (start us, length us, event | category | flops | bytes accessed | tf_op | source)
XLA Modules:
  0.0 462.4 jit_solution(14933505822158280420)
XLA Ops:
  0.6 5.1 %shard_map.95 = bf16[16,128,1024]{2,1,0:T(8,128)(2,1)} custom-call(f32[1,2,2048,1024]{3,2,1,0:T(8,128)} %src.3), custom_call_target="tpu_custom_call" | custom-call | bytes 12582912 | tf_op jit(solution)/shard_map/pallas_call | solution.py:41
  5.8 6.2 %all-to-all-start.1 = ((bf16[16,128,1024]{2,1,0:T(8,128)(2,1)}), bf16[16,128,1024]{2,1,0:T(8,128)(2,1)}, u32[]{:S(2)}, u32[]{:S(2)}) async-start(bf16[16,128,1024]{2,1,0:T(8,128)(2,1)} %shard_map.95), calls=%async_computation.1 | async-start | bytes 8388608 | tf_op jit(solution)/shard_map/all_to_all | solution.py:386
  11.9 5.1 %shard_map.94 = bf16[16,128,1024]{2,1,0:T(8,128)(2,1)} custom-call(f32[1,2,2048,1024]{3,2,1,0:T(8,128)} %src.3), custom_call_target="tpu_custom_call" | custom-call | bytes 12582912 | tf_op jit(solution)/shard_map/pallas_call | solution.py:41
  17.1 0.0 copy-start.13
  17.1 0.0 copy-start.15
  17.1 0.0 copy-start.16
  17.1 87.6 %all-to-all-done.1.received = bf16[16,128,1024]{2,1,0:T(8,128)(2,1)} async-done(((bf16[16,128,1024]{2,1,0:T(8,128)(2,1)}), bf16[16,128,1024]{2,1,0:T(8,128)(2,1)}, u32[]{:S(2)}, u32[]{:S(2)}) %all-to-all-start.1) | async-done | bytes 4194336 | tf_op jit(solution)/shard_map/all_to_all | solution.py:386
  104.6 4.7 %all-to-all-start = ((bf16[16,128,1024]{2,1,0:T(8,128)(2,1)}), bf16[16,128,1024]{2,1,0:T(8,128)(2,1)}, u32[]{:S(2)}, u32[]{:S(2)}) async-start(bf16[16,128,1024]{2,1,0:T(8,128)(2,1)} %shard_map.94), calls=%async_computation | async-start | bytes 8388608 | tf_op jit(solution)/shard_map/all_to_all | solution.py:386
  109.3 0.0 copy-done.13
  109.3 1.6 collective-permute-start
  110.9 0.0 copy-done.15
  110.9 0.0 copy-done.16
  110.9 0.6 slice_bitcast_fusion
  111.5 45.7 %collective-permute-done.refs_1_ = bf16[1024,1024]{1,0:T(8,128)(2,1)} collective-permute-done((bf16[1024,1024]{1,0:T(8,128)(2,1)S(1)}, bf16[1024,1024]{1,0:T(8,128)(2,1)}, u32[]{:S(2)}, u32[]{:S(2)}) %collective-permute-start) | collective-permute-done | bytes 2097184 | tf_op jit(solution)/shard_map/ppermute | solution.py:134
  157.2 8.9 %shard_map.96 = (bf16[1024,2048]{1,0:T(8,128)(2,1)}, f32[1024,1]{1,0:T(8,128)}) custom-call(s32[1]{0:T(128)} %bitcast.4.place.where, bf16[1024,1024]{1,0:T(8,128)(2,1)} %bitcast.24, bf16[1024,1024]{1,0:T(8,128)(2,1)} %collective-permute-done.refs_1_), custom_call_target="tpu_custom_call" | custom-call | bytes 8388608 | tf_op jit(solution)/shard_map/pallas_call | solution.py:137
  166.1 10.9 %shard_map.97 = (f32[16,128,1024]{2,1,0:T(8,128)}, f32[16,128,1024]{2,1,0:T(8,128)}, bf16[16,128,1024]{2,1,0:T(8,128)(2,1)}) custom-call(s32[16]{0:T(128)} %get-tuple-element.52.old, s32[16]{0:T(128)} %get-tuple-element.47.new, bf16[16,128,1024]{2,1,0:T(8,128)(2,1)} %all-to-all-done.1.received, f32[16,128,1024]{2,1,0:T(8,128)} %anchor.3, ...), custom_call_target="tpu_custom_call" | custom-call | bytes 25165824 | tf_op jit(solution)/shard_map/pallas_call | solution.py:83
  176.9 25.1 %all-to-all-done.received = bf16[16,128,1024]{2,1,0:T(8,128)(2,1)} async-done(((bf16[16,128,1024]{2,1,0:T(8,128)(2,1)}), bf16[16,128,1024]{2,1,0:T(8,128)(2,1)}, u32[]{:S(2)}, u32[]{:S(2)}) %all-to-all-start) | async-done | bytes 4194336 | tf_op jit(solution)/shard_map/all_to_all | solution.py:386
  202.0 4.7 %all-to-all-start.2 = ((bf16[16,128,1024]{2,1,0:T(8,128)(2,1)}), bf16[16,128,1024]{2,1,0:T(8,128)(2,1)}, u32[]{:S(2)}, u32[]{:S(2)}) async-start(bf16[16,128,1024]{2,1,0:T(8,128)(2,1)} %get-tuple-element.31), calls=%async_computation.2 | async-start | bytes 8388608 | tf_op jit(solution)/shard_map/all_to_all | solution.py:386
  206.7 10.8 %shard_map.98 = (f32[16,128,1024]{2,1,0:T(8,128)}, f32[16,128,1024]{2,1,0:T(8,128)}, bf16[16,128,1024]{2,1,0:T(8,128)(2,1)}) custom-call(s32[16]{0:T(128)} %get-tuple-element.51.old, s32[16]{0:T(128)} %get-tuple-element.48.new, bf16[16,128,1024]{2,1,0:T(8,128)(2,1)} %all-to-all-done.received, ...), custom_call_target="tpu_custom_call", output_to_operand_aliasing={{0}: (5, {}), {1}: (6, {})} | custom-call | bytes 25165824 | tf_op jit(solution)/shard_map/pallas_call | solution.py:83
  217.5 81.9 %all-to-all-done.2 = bf16[16,128,1024]{2,1,0:T(8,128)(2,1)} async-done(((bf16[16,128,1024]{2,1,0:T(8,128)(2,1)}), bf16[16,128,1024]{2,1,0:T(8,128)(2,1)}, u32[]{:S(2)}, u32[]{:S(2)}) %all-to-all-start.2) | async-done | bytes 4194336 | tf_op jit(solution)/shard_map/all_to_all | solution.py:386
  299.4 4.7 %all-to-all-start.3 = ((bf16[16,128,1024]{2,1,0:T(8,128)(2,1)}), bf16[16,128,1024]{2,1,0:T(8,128)(2,1)}, u32[]{:S(2)}, u32[]{:S(2)}) async-start(bf16[16,128,1024]{2,1,0:T(8,128)(2,1)} %get-tuple-element.35), calls=%async_computation.3 | async-start | bytes 8388608 | tf_op jit(solution)/shard_map/all_to_all | solution.py:386
  304.1 10.7 %shard_map.99 = (bf16[1024,1024]{1,0:T(8,128)(2,1)}, f32[1024,1024]{1,0:T(8,128)}) custom-call(bf16[1024,2048]{1,0:T(8,128)(2,1)} %get-tuple-element.25.normed.refs_0_, bf16[2048,1024]{1,0:T(8,128)(2,1)} %bitcast.6.weight, bf16[1024,1024]{1,0:T(8,128)(2,1)} %bitcast.25), custom_call_target="tpu_custom_call" | custom-call | flops 4294967296 | bytes 16777216 | tf_op jit(solution)/shard_map/pallas_call | solution.py:196
  314.7 1.5 collective-permute-start.1
  316.2 46.4 %collective-permute-done.1.refs_1_ = bf16[1024,1024]{1,0:T(8,128)(2,1)S(1)} collective-permute-done((bf16[1024,1024]{1,0:T(8,128)(2,1)}, bf16[1024,1024]{1,0:T(8,128)(2,1)S(1)}, u32[]{:S(2)}, u32[]{:S(2)}) %collective-permute-start.1) | collective-permute-done | bytes 2097184 | tf_op jit(solution)/shard_map/ppermute | solution.py:134
  362.6 0.0 copy-start.14
  362.6 1.3 copy-done.14
  364.0 8.9 %shard_map.100 = (bf16[1024,2048]{1,0:T(8,128)(2,1)}, f32[1024,1]{1,0:T(8,128)}) custom-call(s32[1]{0:T(128)} %bitcast.4.place.where, bf16[1024,1024]{1,0:T(8,128)(2,1)} %get-tuple-element.32.refs_0_.refs_4_, bf16[1024,1024]{1,0:T(8,128)(2,1)} %copy-done.14), custom_call_target="tpu_custom_call" | custom-call | bytes 8388608 | tf_op jit(solution)/shard_map/pallas_call | solution.py:137
  372.9 23.9 %all-to-all-done.3 = bf16[16,128,1024]{2,1,0:T(8,128)(2,1)} async-done(((bf16[16,128,1024]{2,1,0:T(8,128)(2,1)}), bf16[16,128,1024]{2,1,0:T(8,128)(2,1)}, u32[]{:S(2)}, u32[]{:S(2)}) %all-to-all-start.3) | async-done | bytes 4194336 | tf_op jit(solution)/shard_map/all_to_all | solution.py:386
  396.8 10.2 %shard_map.101 = (bf16[1024,1024]{1,0:T(8,128)(2,1)}, f32[8,1024]{1,0:T(8,128)}, bf16[4,272,256]{2,1,0:T(8,128)(2,1)}) custom-call(s32[1]{0:T(128)} %bitcast.7.at, bf16[1024,2048]{1,0:T(8,128)(2,1)} %get-tuple-element.34.normed, bf16[2048,1024]{1,0:T(8,128)(2,1)} %bitcast.8.weight, bf16[1024,1024]{1,0:T(8,128)(2,1)} %bitcast.21), custom_call_target="tpu_custom_call" | custom-call | flops 301989888 | bytes 786432 | tf_op jit(solution)/shard_map/pallas_call | solution.py:248
  406.9 1.5 collective-permute-start.2
  408.4 1.6 copy-done
  410.0 2.2 shard_map.102
  412.2 0.6 collective-permute-start.3
  412.8 0.0 copy-done.1
  412.8 4.2 shard_map.103.refs_6_
  417.0 0.0 copy-start.4
  417.0 1.3 copy-done.4
  418.3 0.9 slice.22
  419.2 3.5 collective-permute-done.2.refs_7_
  422.7 0.8 copy-done.8
  423.5 2.0 shard_map.104
  425.5 1.6 collective-permute-start.5
  427.1 0.7 convert_reduce_fusion
  427.8 0.0 copy-done.6
  427.8 6.5 %shard_map.105.refs_10_ = bf16[1,2,2048,1024]{3,2,1,0:T(8,128)(2,1)} custom-call(bf16[1024,2048]{1,0:T(8,128)(2,1)S(1)} %copy-done.6, bf16[1024,1024]{1,0:T(8,128)(2,1)S(1)} %copy-done.1), custom_call_target="tpu_custom_call" | custom-call | flops 4294967296 | bytes 10485760 | tf_op jit(solution)/shard_map/pallas_call | solution.py:168
  434.3 0.0 collective-permute-done.3.refs_8_
  434.3 0.8 copy-done.10
  435.1 1.0 copy.14
  436.2 0.0 copy-start.9
  436.2 0.0 copy-start.11
  436.2 2.2 shard_map.106
  438.4 1.2 collective-permute-start.4
  439.5 0.0 copy-done.7
  439.5 0.0 copy-done.12
  439.5 0.1 multiply_multiply_fusion.refs_2_
  439.6 5.6 %collective-permute-done.5.refs_9_ = bf16[1024,256]{1,0:T(8,128)(2,1)} collective-permute-done((bf16[1024,256]{1,0:T(8,128)(2,1)S(1)}, bf16[1024,256]{1,0:T(8,128)(2,1)}, u32[]{:S(2)}, u32[]{:S(2)}) %collective-permute-start.5) | collective-permute-done | bytes 524320 | tf_op jit(solution)/shard_map/ppermute | solution.py:422
  445.3 0.0 copy-done.2
  445.3 0.0 copy-done.3
  445.3 0.0 copy-done.5
  445.3 0.0 copy-done.9
  445.3 0.0 copy-done.11
  445.3 11.0 %shard_map.107.refs_8_ = bf16[1,2,2048,1024]{3,2,1,0:T(8,128)(2,1)} custom-call(bf16[1024,2048]{1,0:T(8,128)(2,1)} %get-tuple-element.25.normed.refs_0_, f32[1024,1]{1,0:T(8,128)S(1)} %copy-done.7, f32[1024,1]{1,0:T(8,128)S(1)} %multiply_multiply_fusion.refs_2_, bf16[1024,1024]{1,0:T(8,128)(2,1)S(1)} %bitcast.22, ...), custom_call_target="tpu_custom_call", output_to_operand_aliasing={{}: (10, {})} | custom-call | flops 12884901888 | bytes 73400320 | tf_op jit(solution)/shard_map/pallas_call | solution.py:349
  456.3 0.0 collective-permute-done.4.refs_7_
  456.3 6.1 %shard_map.108 = bf16[1,2,2048,1024]{3,2,1,0:T(8,128)(2,1)} custom-call(bf16[1024,2048]{1,0:T(8,128)(2,1)} %get-tuple-element.25.normed.refs_0_, f32[1024,1]{1,0:T(8,128)S(1)} %copy-done.7, f32[1024,1]{1,0:T(8,128)S(1)} %multiply_multiply_fusion.refs_2_, bf16[1024,1024]{1,0:T(8,128)(2,1)S(1)} %bitcast.23, ...), custom_call_target="tpu_custom_call", output_to_operand_aliasing={{}: (8, {})} | custom-call | flops 4294967296 | bytes 35651584 | tf_op jit(solution)/shard_map/pallas_call | solution.py:349
  (12 shorter events, 0.0 us)
Async XLA Ops:
  5.8 98.9 %all-to-all-start.1 = ((bf16[16,128,1024]{2,1,0:T(8,128)(2,1)}), bf16[16,128,1024]{2,1,0:T(8,128)(2,1)}, u32[]{:S(2)}, u32[]{:S(2)}) async-start(bf16[16,128,1024]{2,1,0:T(8,128)(2,1)} %shard_map.95), calls=%async_computation.1 | async-start | bytes 8388608 | tf_op jit(solution)/shard_map/all_to_all | solution.py:386
  17.1 92.3 %copy-start.13 = (bf16[1,1024,1024]{2,1,0:T(8,128)(2,1)S(1)}, bf16[1,1024,1024]{2,1,0:T(8,128)(2,1)}, u32[]{:S(2)}) copy-start(bf16[1,1024,1024]{2,1,0:T(8,128)(2,1)} %param.12) | copy-start | bytes 6291460
  17.1 93.8 %copy-start.15 = (s32[16,2]{0,1:T(2,128)S(1)}, s32[16,2]{0,1:T(2,128)}, u32[]{:S(2)}) copy-start(s32[16,2]{0,1:T(2,128)} %param.11) | copy-start | bytes 388
  17.1 93.8 %copy-start.16 = (s32[16,2]{0,1:T(2,128)S(1)}, s32[16,2]{0,1:T(2,128)}, u32[]{:S(2)}) copy-start(s32[16,2]{0,1:T(2,128)} %param.10) | copy-start | bytes 388
  104.6 97.4 %all-to-all-start = ((bf16[16,128,1024]{2,1,0:T(8,128)(2,1)}), bf16[16,128,1024]{2,1,0:T(8,128)(2,1)}, u32[]{:S(2)}, u32[]{:S(2)}) async-start(bf16[16,128,1024]{2,1,0:T(8,128)(2,1)} %shard_map.94), calls=%async_computation | async-start | bytes 8388608 | tf_op jit(solution)/shard_map/all_to_all | solution.py:386
  109.3 47.9 %collective-permute-start = (bf16[1024,1024]{1,0:T(8,128)(2,1)S(1)}, bf16[1024,1024]{1,0:T(8,128)(2,1)}, u32[]{:S(2)}, u32[]{:S(2)}) collective-permute-start(bf16[1024,1024]{1,0:T(8,128)(2,1)S(1)} %bitcast.26), channel_id=1, source_target_pairs={{0,1},{1,0},{2,3},{3,2},{4,5},{5,4},{6,7},{7,6},{8,9},{9,8},{10,11... | collective-permute-start | bytes 6291464 | tf_op jit(solution)/shard_map/ppermute | solution.py:134
  202.0 97.4 %all-to-all-start.2 = ((bf16[16,128,1024]{2,1,0:T(8,128)(2,1)}), bf16[16,128,1024]{2,1,0:T(8,128)(2,1)}, u32[]{:S(2)}, u32[]{:S(2)}) async-start(bf16[16,128,1024]{2,1,0:T(8,128)(2,1)} %get-tuple-element.31), calls=%async_computation.2 | async-start | bytes 8388608 | tf_op jit(solution)/shard_map/all_to_all | solution.py:386
  299.4 97.4 %all-to-all-start.3 = ((bf16[16,128,1024]{2,1,0:T(8,128)(2,1)}), bf16[16,128,1024]{2,1,0:T(8,128)(2,1)}, u32[]{:S(2)}, u32[]{:S(2)}) async-start(bf16[16,128,1024]{2,1,0:T(8,128)(2,1)} %get-tuple-element.35), calls=%async_computation.3 | async-start | bytes 8388608 | tf_op jit(solution)/shard_map/all_to_all | solution.py:386
  314.7 47.9 %collective-permute-start.1 = (bf16[1024,1024]{1,0:T(8,128)(2,1)}, bf16[1024,1024]{1,0:T(8,128)(2,1)S(1)}, u32[]{:S(2)}, u32[]{:S(2)}) collective-permute-start(bf16[1024,1024]{1,0:T(8,128)(2,1)} %get-tuple-element.32.refs_0_.refs_4_), channel_id=1, source_target_pairs={{0,1},{1,0},{2,3},{3,2},{4,5},{5,4},{6,7},{7,6},{8,9},{9,8},{10,11... | collective-permute-start | bytes 6291464 | tf_op jit(solution)/shard_map/ppermute | solution.py:134
  362.6 1.3 copy-start.14
  406.9 15.8 %collective-permute-start.2 = (bf16[4,272,256]{2,1,0:T(8,128)(2,1)}, bf16[4,272,256]{2,1,0:T(8,128)(2,1)S(1)}, u32[]{:S(2)}, u32[]{:S(2)}) collective-permute-start(bf16[4,272,256]{2,1,0:T(8,128)(2,1)} %get-tuple-element.37), channel_id=1, source_target_pairs={{0,1},{1,0},{2,3},{3,2},{4,5},{5,4},{6,7},{7,6},{8,9},{9,8},{10,11... | collective-permute-start | bytes 1671176 | tf_op jit(solution)/shard_map/ppermute | solution.py:433
  408.4 1.6 copy-start
  410.0 2.8 copy-start.1
  412.2 22.1 %collective-permute-start.3 = (bf16[1024,256]{1,0:T(8,128)(2,1)S(1)}, bf16[1024,256]{1,0:T(8,128)(2,1)S(1)}, u32[]{:S(2)}, u32[]{:S(2)}) collective-permute-start(bf16[1024,256]{1,0:T(8,128)(2,1)S(1)} %shard_map.102), channel_id=1, source_target_pairs={{0,1},{1,0},{2,3},{3,2},{4,5},{5,4},{6,7},{7,6},{8,9},{9,8},{10,11... | collective-permute-start | bytes 1572872 | tf_op jit(solution)/shard_map/ppermute | solution.py:422
  417.0 1.3 copy-start.4
  418.3 9.5 %copy-start.6 = (bf16[1024,2048]{1,0:T(8,128)(2,1)S(1)}, bf16[1024,2048]{1,0:T(8,128)(2,1)}, u32[]{:S(2)}) copy-start(bf16[1024,2048]{1,0:T(8,128)(2,1)} %get-tuple-element.34.normed) | copy-start | bytes 12582916
  422.7 0.8 copy-start.8
  425.5 19.7 %collective-permute-start.5 = (bf16[1024,256]{1,0:T(8,128)(2,1)S(1)}, bf16[1024,256]{1,0:T(8,128)(2,1)}, u32[]{:S(2)}, u32[]{:S(2)}) collective-permute-start(bf16[1024,256]{1,0:T(8,128)(2,1)S(1)} %shard_map.104), channel_id=1, source_target_pairs={{0,1},{1,0},{2,3},{3,2},{4,5},{5,4},{6,7},{7,6},{8,9},{9,8},{10,11... | collective-permute-start | bytes 1572872 | tf_op jit(solution)/shard_map/ppermute | solution.py:422
  434.3 5.2 %copy-start.7 = (f32[1024,1]{1,0:T(8,128)S(1)}, f32[1024,1]{1,0:T(8,128)}, u32[]{:S(2)}) copy-start(f32[1024,1]{1,0:T(8,128)} %get-tuple-element.33.refs_1_) | copy-start | bytes 12292
  434.3 0.8 copy-start.10
  436.2 3.4 copy-start.12
  436.2 9.1 %copy-start.2 = (bf16[1024,1024]{1,0:T(8,128)(2,1)S(1)}, bf16[1024,1024]{1,0:T(8,128)(2,1)}, u32[]{:S(2)}) copy-start(bf16[1024,1024]{1,0:T(8,128)(2,1)} %get-tuple-element.32.refs_0_.refs_4_) | copy-start | bytes 6291460
  436.2 9.1 %copy-start.3 = (bf16[1,1024,1024]{2,1,0:T(8,128)(2,1)S(1)}, bf16[1,1024,1024]{2,1,0:T(8,128)(2,1)}, u32[]{:S(2)}) copy-start(bf16[1,1024,1024]{2,1,0:T(8,128)(2,1)} %param.13) | copy-start | bytes 6291460
  436.2 9.1 %copy-start.5 = (bf16[1024,1024]{1,0:T(8,128)(2,1)S(1)}, bf16[1024,1024]{1,0:T(8,128)(2,1)}, u32[]{:S(2)}) copy-start(bf16[1024,1024]{1,0:T(8,128)(2,1)} %copy-done.4) | copy-start | bytes 6291460
  436.2 9.1 %copy-start.9 = (bf16[4,272,256]{2,1,0:T(8,128)(2,1)S(1)}, bf16[4,272,256]{2,1,0:T(8,128)(2,1)}, u32[]{:S(2)}) copy-start(bf16[4,272,256]{2,1,0:T(8,128)(2,1)} %copy-done.8) | copy-start | bytes 1671172
  436.2 9.1 %copy-start.11 = (bf16[1024,256]{1,0:T(8,128)(2,1)S(1)}, bf16[1024,256]{1,0:T(8,128)(2,1)}, u32[]{:S(2)}) copy-start(bf16[1024,256]{1,0:T(8,128)(2,1)} %copy-done.10) | copy-start | bytes 1572868
  438.4 17.9 %collective-permute-start.4 = (bf16[1024,256]{1,0:T(8,128)(2,1)S(1)}, bf16[1024,256]{1,0:T(8,128)(2,1)S(1)}, u32[]{:S(2)}, u32[]{:S(2)}) collective-permute-start(bf16[1024,256]{1,0:T(8,128)(2,1)S(1)} %shard_map.106), channel_id=1, source_target_pairs={{0,1},{1,0},{2,3},{3,2},{4,5},{5,4},{6,7},{7,6},{8,9},{9,8},{10,11... | collective-permute-start | bytes 1572872 | tf_op jit(solution)/shard_map/ppermute | solution.py:422

commit v5 on v4

--- a/solution.py
+++ b/solution.py
@@ -454,7 +454,7 @@
             source = after(source, *arrived[run - 1])
     scaled = second_scale**2 * after(share, grads).reshape(rows, 1) / depth
     mine = [upstream, second_state, gate, kept]
-    bounds = [0, runs - 1, runs] if runs > 1 else [0, runs]
+    bounds = [0] + list(range(max(1, runs - 2), runs + 1))
     for begin, end in zip(bounds[:-1], bounds[1:]):
         terms = [value for run in range(begin, end) for value in arrived[run]]
         grads = first_level_grad(

time: 463 us -> 463 us (level)
    ppermute x3, waiting for transfers between devices: 5.65 us -> 0.51 us  [send(): lax.ppermute(values[n], 'mp', around(parts, n + 1))]
    pallas_call x2 -> x3, Pallas kernels: 17.1 us -> 20.3 us  [first_level_grad(): pl.pallas_call(functools.partial(first_kernel, factor, runs), grid=(rows...]
  transfers between devices with their start and end apart: 10 -> 10, of which waited for: 8 -> 8; matrix products, arithmetic and copies ran while one was open for 1% -> 1% of each run, Pallas kernels for 18% -> 19%
where the time goes in v5:
time: 463 us; the launch traced here: 462 us
  waiting for transfers between devices  316 us (68%)
  Pallas kernels  109 us (24%)
  starting transfers between devices  28.4 us (6%)
  local copies, waits for them, and re-layouts  7.89 us (2%)
    all_to_all x4, waiting for transfers between devices, exchange(): lax.all_to_all(blocks, 'group', split_axis=0, concat_axis=0, tiled=True)  218 us
    ppermute x2, waiting for transfers between devices, normalize(): lax.ppermute(own, 'mp', around(parts, step))  92.1 us
    pallas_call x2, Pallas kernels, outer_update(): pl.pallas_call(functools.partial(update_kernel, groups, mods, aliased), g...  21.7 us
    pallas_call x3, Pallas kernels, first_level_grad(): pl.pallas_call(functools.partial(first_kernel, factor, runs), grid=(rows...  20.3 us
    all_to_all x4, starting transfers between devices, exchange(): lax.all_to_all(blocks, 'group', split_axis=0, concat_axis=0, tiled=True)  20.2 us
    pallas_call x2, Pallas kernels, normalize(): pl.pallas_call(functools.partial(norm_kernel, parts, depth), grid_spec=pl...  17.8 us
    pallas_call x4, Pallas kernels, term(): pl.pallas_call(functools.partial(term_kernel, factor), grid_spec=pltpu.Pr...  11.2 us
    pallas_call x1, Pallas kernels, first_forward(): pl.pallas_call(functools.partial(state_kernel, factor), grid=(rows // til...  10.7 us
  transfers between devices with their start and end apart: 10, of which 8 were waited for; matrix products, arithmetic and copies ran while one was open for 1% of the time, Pallas kernels for 19%

profile of v5, /device:TPU:16, one launch (start us, length us, event | category | flops | bytes accessed | tf_op | source)
XLA Modules:
  0.0 461.5 jit_solution(13570995564206604807)
XLA Ops:
  0.6 5.1 %shard_map.95 = bf16[16,128,1024]{2,1,0:T(8,128)(2,1)} custom-call(f32[1,2,2048,1024]{3,2,1,0:T(8,128)} %src.3), custom_call_target="tpu_custom_call" | custom-call | bytes 12582912 | tf_op jit(solution)/shard_map/pallas_call | solution.py:41
  5.8 6.2 %all-to-all-start.1 = ((bf16[16,128,1024]{2,1,0:T(8,128)(2,1)}), bf16[16,128,1024]{2,1,0:T(8,128)(2,1)}, u32[]{:S(2)}, u32[]{:S(2)}) async-start(bf16[16,128,1024]{2,1,0:T(8,128)(2,1)} %shard_map.95), calls=%async_computation.1 | async-start | bytes 8388608 | tf_op jit(solution)/shard_map/all_to_all | solution.py:386
  11.9 5.1 %shard_map.94 = bf16[16,128,1024]{2,1,0:T(8,128)(2,1)} custom-call(f32[1,2,2048,1024]{3,2,1,0:T(8,128)} %src.3), custom_call_target="tpu_custom_call" | custom-call | bytes 12582912 | tf_op jit(solution)/shard_map/pallas_call | solution.py:41
  17.1 0.0 copy-start.10
  17.1 0.0 copy-start.12
  17.1 0.0 copy-start.13
  17.1 87.6 %all-to-all-done.1.received = bf16[16,128,1024]{2,1,0:T(8,128)(2,1)} async-done(((bf16[16,128,1024]{2,1,0:T(8,128)(2,1)}), bf16[16,128,1024]{2,1,0:T(8,128)(2,1)}, u32[]{:S(2)}, u32[]{:S(2)}) %all-to-all-start.1) | async-done | bytes 4194336 | tf_op jit(solution)/shard_map/all_to_all | solution.py:386
  104.6 4.7 %all-to-all-start = ((bf16[16,128,1024]{2,1,0:T(8,128)(2,1)}), bf16[16,128,1024]{2,1,0:T(8,128)(2,1)}, u32[]{:S(2)}, u32[]{:S(2)}) async-start(bf16[16,128,1024]{2,1,0:T(8,128)(2,1)} %shard_map.94), calls=%async_computation | async-start | bytes 8388608 | tf_op jit(solution)/shard_map/all_to_all | solution.py:386
  109.3 0.0 copy-done.10
  109.3 1.6 collective-permute-start
  110.9 0.0 copy-done.12
  110.9 0.0 copy-done.13
  110.9 0.6 slice_bitcast_fusion
  111.5 45.7 %collective-permute-done.refs_1_ = bf16[1024,1024]{1,0:T(8,128)(2,1)} collective-permute-done((bf16[1024,1024]{1,0:T(8,128)(2,1)S(1)}, bf16[1024,1024]{1,0:T(8,128)(2,1)}, u32[]{:S(2)}, u32[]{:S(2)}) %collective-permute-start) | collective-permute-done | bytes 2097184 | tf_op jit(solution)/shard_map/ppermute | solution.py:134
  157.2 8.9 %shard_map.96 = (bf16[1024,2048]{1,0:T(8,128)(2,1)}, f32[1024,1]{1,0:T(8,128)}) custom-call(s32[1]{0:T(128)} %bitcast.4.place.where, bf16[1024,1024]{1,0:T(8,128)(2,1)} %bitcast.25, bf16[1024,1024]{1,0:T(8,128)(2,1)} %collective-permute-done.refs_1_), custom_call_target="tpu_custom_call" | custom-call | bytes 8388608 | tf_op jit(solution)/shard_map/pallas_call | solution.py:137
  166.1 10.9 %shard_map.97 = (f32[16,128,1024]{2,1,0:T(8,128)}, f32[16,128,1024]{2,1,0:T(8,128)}, bf16[16,128,1024]{2,1,0:T(8,128)(2,1)}) custom-call(s32[16]{0:T(128)} %get-tuple-element.52.old, s32[16]{0:T(128)} %get-tuple-element.47.new, bf16[16,128,1024]{2,1,0:T(8,128)(2,1)} %all-to-all-done.1.received, f32[16,128,1024]{2,1,0:T(8,128)} %anchor.3, ...), custom_call_target="tpu_custom_call" | custom-call | bytes 25165824 | tf_op jit(solution)/shard_map/pallas_call | solution.py:83
  176.9 25.1 %all-to-all-done.received = bf16[16,128,1024]{2,1,0:T(8,128)(2,1)} async-done(((bf16[16,128,1024]{2,1,0:T(8,128)(2,1)}), bf16[16,128,1024]{2,1,0:T(8,128)(2,1)}, u32[]{:S(2)}, u32[]{:S(2)}) %all-to-all-start) | async-done | bytes 4194336 | tf_op jit(solution)/shard_map/all_to_all | solution.py:386
  202.0 4.7 %all-to-all-start.2 = ((bf16[16,128,1024]{2,1,0:T(8,128)(2,1)}), bf16[16,128,1024]{2,1,0:T(8,128)(2,1)}, u32[]{:S(2)}, u32[]{:S(2)}) async-start(bf16[16,128,1024]{2,1,0:T(8,128)(2,1)} %get-tuple-element.31), calls=%async_computation.2 | async-start | bytes 8388608 | tf_op jit(solution)/shard_map/all_to_all | solution.py:386
  206.7 10.8 %shard_map.98 = (f32[16,128,1024]{2,1,0:T(8,128)}, f32[16,128,1024]{2,1,0:T(8,128)}, bf16[16,128,1024]{2,1,0:T(8,128)(2,1)}) custom-call(s32[16]{0:T(128)} %get-tuple-element.51.old, s32[16]{0:T(128)} %get-tuple-element.48.new, bf16[16,128,1024]{2,1,0:T(8,128)(2,1)} %all-to-all-done.received, ...), custom_call_target="tpu_custom_call", output_to_operand_aliasing={{0}: (5, {}), {1}: (6, {})} | custom-call | bytes 25165824 | tf_op jit(solution)/shard_map/pallas_call | solution.py:83
  217.5 81.9 %all-to-all-done.2 = bf16[16,128,1024]{2,1,0:T(8,128)(2,1)} async-done(((bf16[16,128,1024]{2,1,0:T(8,128)(2,1)}), bf16[16,128,1024]{2,1,0:T(8,128)(2,1)}, u32[]{:S(2)}, u32[]{:S(2)}) %all-to-all-start.2) | async-done | bytes 4194336 | tf_op jit(solution)/shard_map/all_to_all | solution.py:386
  299.4 4.7 %all-to-all-start.3 = ((bf16[16,128,1024]{2,1,0:T(8,128)(2,1)}), bf16[16,128,1024]{2,1,0:T(8,128)(2,1)}, u32[]{:S(2)}, u32[]{:S(2)}) async-start(bf16[16,128,1024]{2,1,0:T(8,128)(2,1)} %get-tuple-element.35), calls=%async_computation.3 | async-start | bytes 8388608 | tf_op jit(solution)/shard_map/all_to_all | solution.py:386
  304.1 10.7 %shard_map.99 = (bf16[1024,1024]{1,0:T(8,128)(2,1)}, f32[1024,1024]{1,0:T(8,128)}) custom-call(bf16[1024,2048]{1,0:T(8,128)(2,1)} %get-tuple-element.25.normed.refs_0_, bf16[2048,1024]{1,0:T(8,128)(2,1)} %bitcast.6.weight, bf16[1024,1024]{1,0:T(8,128)(2,1)} %bitcast.26), custom_call_target="tpu_custom_call" | custom-call | flops 4294967296 | bytes 16777216 | tf_op jit(solution)/shard_map/pallas_call | solution.py:196
  314.7 1.5 collective-permute-start.1
  316.2 46.4 %collective-permute-done.1.refs_1_ = bf16[1024,1024]{1,0:T(8,128)(2,1)S(1)} collective-permute-done((bf16[1024,1024]{1,0:T(8,128)(2,1)}, bf16[1024,1024]{1,0:T(8,128)(2,1)S(1)}, u32[]{:S(2)}, u32[]{:S(2)}) %collective-permute-start.1) | collective-permute-done | bytes 2097184 | tf_op jit(solution)/shard_map/ppermute | solution.py:134
  362.6 0.0 copy-start.11
  362.6 1.3 copy-done.11
  364.0 8.9 %shard_map.100 = (bf16[1024,2048]{1,0:T(8,128)(2,1)}, f32[1024,1]{1,0:T(8,128)}) custom-call(s32[1]{0:T(128)} %bitcast.4.place.where, bf16[1024,1024]{1,0:T(8,128)(2,1)} %get-tuple-element.32.refs_0_.refs_4_, bf16[1024,1024]{1,0:T(8,128)(2,1)} %copy-done.11), custom_call_target="tpu_custom_call" | custom-call | bytes 8388608 | tf_op jit(solution)/shard_map/pallas_call | solution.py:137
  372.8 23.9 %all-to-all-done.3 = bf16[16,128,1024]{2,1,0:T(8,128)(2,1)} async-done(((bf16[16,128,1024]{2,1,0:T(8,128)(2,1)}), bf16[16,128,1024]{2,1,0:T(8,128)(2,1)}, u32[]{:S(2)}, u32[]{:S(2)}) %all-to-all-start.3) | async-done | bytes 4194336 | tf_op jit(solution)/shard_map/all_to_all | solution.py:386
  396.8 10.2 %shard_map.101 = (bf16[1024,1024]{1,0:T(8,128)(2,1)}, f32[8,1024]{1,0:T(8,128)}, bf16[4,272,256]{2,1,0:T(8,128)(2,1)}) custom-call(s32[1]{0:T(128)} %bitcast.7.at, bf16[1024,2048]{1,0:T(8,128)(2,1)} %get-tuple-element.34.normed, bf16[2048,1024]{1,0:T(8,128)(2,1)} %bitcast.8.weight, bf16[1024,1024]{1,0:T(8,128)(2,1)} %bitcast.21), custom_call_target="tpu_custom_call" | custom-call | flops 301989888 | bytes 786432 | tf_op jit(solution)/shard_map/pallas_call | solution.py:248
  406.9 1.5 collective-permute-start.2
  408.4 0.0 copy-start.2
  408.4 1.6 copy-done.2
  410.0 0.0 copy-start.3
  410.0 2.2 shard_map.102
  412.2 0.6 collective-permute-start.3
  412.8 0.0 copy-done.3
  412.8 4.2 shard_map.103.refs_6_
  417.0 0.0 copy-start.6
  417.0 0.9 slice.22
  417.9 4.8 %collective-permute-done.2.refs_7_ = bf16[4,272,256]{2,1,0:T(8,128)(2,1)S(1)} collective-permute-done((bf16[4,272,256]{2,1,0:T(8,128)(2,1)}, bf16[4,272,256]{2,1,0:T(8,128)(2,1)S(1)}, u32[]{:S(2)}, u32[]{:S(2)}) %collective-permute-start.2) | collective-permute-done | bytes 557088 | tf_op jit(solution)/shard_map/ppermute | solution.py:433
  422.7 2.7 shard_map.104
  425.4 1.5 collective-permute-start.5
  426.9 0.0 copy-done.6
  426.9 6.5 %shard_map.105.refs_9_ = bf16[1,2,2048,1024]{3,2,1,0:T(8,128)(2,1)} custom-call(bf16[1024,2048]{1,0:T(8,128)(2,1)S(1)} %copy-done.6, bf16[1024,1024]{1,0:T(8,128)(2,1)S(1)} %copy-done.3), custom_call_target="tpu_custom_call" | custom-call | flops 4294967296 | bytes 10485760 | tf_op jit(solution)/shard_map/pallas_call | solution.py:168
  433.4 0.0 copy-start.5
  433.4 0.5 collective-permute-done.3.refs_8_
  433.9 0.0 copy-start.7
  433.9 0.8 copy-done.7
  434.7 1.0 copy.15
  435.8 0.0 copy-start.4
  435.8 1.6 copy-done.4
  437.4 2.2 shard_map.106
  439.6 1.6 collective-permute-start.4
  441.1 0.0 copy-done.5
  441.1 0.0 copy-done.9
  441.1 0.1 multiply_multiply_fusion.refs_2_
  441.2 0.0 copy-done
  441.2 0.0 copy-done.1
  441.2 0.0 copy-done.8
  441.2 8.1 %shard_map.107.refs_8_ = bf16[1,2,2048,1024]{3,2,1,0:T(8,128)(2,1)} custom-call(bf16[1024,2048]{1,0:T(8,128)(2,1)} %get-tuple-element.25.normed.refs_0_, f32[1024,1]{1,0:T(8,128)S(1)} %copy-done.5, f32[1024,1]{1,0:T(8,128)S(1)} %multiply_multiply_fusion.refs_2_, bf16[1024,1024]{1,0:T(8,128)(2,1)S(1)} %bitcast.22, ...), custom_call_target="tpu_custom_call", output_to_operand_aliasing={{}: (9, {})} | custom-call | flops 8589934592 | bytes 54525952 | tf_op jit(solution)/shard_map/pallas_call | solution.py:349
  449.3 0.0 collective-permute-done.5.refs_7_
  449.3 6.2 %shard_map.108.refs_8_ = bf16[1,2,2048,1024]{3,2,1,0:T(8,128)(2,1)} custom-call(bf16[1024,2048]{1,0:T(8,128)(2,1)} %get-tuple-element.25.normed.refs_0_, f32[1024,1]{1,0:T(8,128)S(1)} %copy-done.5, f32[1024,1]{1,0:T(8,128)S(1)} %multiply_multiply_fusion.refs_2_, bf16[1024,1024]{1,0:T(8,128)(2,1)S(1)} %bitcast.23, ...), custom_call_target="tpu_custom_call", output_to_operand_aliasing={{}: (8, {})} | custom-call | flops 4294967296 | bytes 35651584 | tf_op jit(solution)/shard_map/pallas_call | solution.py:349
  455.4 0.0 collective-permute-done.4.refs_7_
  455.4 6.1 %shard_map.109 = bf16[1,2,2048,1024]{3,2,1,0:T(8,128)(2,1)} custom-call(bf16[1024,2048]{1,0:T(8,128)(2,1)} %get-tuple-element.25.normed.refs_0_, f32[1024,1]{1,0:T(8,128)S(1)} %copy-done.5, f32[1024,1]{1,0:T(8,128)S(1)} %multiply_multiply_fusion.refs_2_, bf16[1024,1024]{1,0:T(8,128)(2,1)S(1)} %bitcast.24, ...), custom_call_target="tpu_custom_call", output_to_operand_aliasing={{}: (8, {})} | custom-call | flops 4294967296 | bytes 35651584 | tf_op jit(solution)/shard_map/pallas_call | solution.py:349
  (7 shorter events, 0.0 us)
Async XLA Ops:
  5.8 98.9 %all-to-all-start.1 = ((bf16[16,128,1024]{2,1,0:T(8,128)(2,1)}), bf16[16,128,1024]{2,1,0:T(8,128)(2,1)}, u32[]{:S(2)}, u32[]{:S(2)}) async-start(bf16[16,128,1024]{2,1,0:T(8,128)(2,1)} %shard_map.95), calls=%async_computation.1 | async-start | bytes 8388608 | tf_op jit(solution)/shard_map/all_to_all | solution.py:386
  17.1 92.3 %copy-start.10 = (bf16[1,1024,1024]{2,1,0:T(8,128)(2,1)S(1)}, bf16[1,1024,1024]{2,1,0:T(8,128)(2,1)}, u32[]{:S(2)}) copy-start(bf16[1,1024,1024]{2,1,0:T(8,128)(2,1)} %param.12) | copy-start | bytes 6291460
  17.1 93.8 %copy-start.12 = (s32[16,2]{0,1:T(2,128)S(1)}, s32[16,2]{0,1:T(2,128)}, u32[]{:S(2)}) copy-start(s32[16,2]{0,1:T(2,128)} %param.11) | copy-start | bytes 388
  17.1 93.8 %copy-start.13 = (s32[16,2]{0,1:T(2,128)S(1)}, s32[16,2]{0,1:T(2,128)}, u32[]{:S(2)}) copy-start(s32[16,2]{0,1:T(2,128)} %param.10) | copy-start | bytes 388
  104.6 97.4 %all-to-all-start = ((bf16[16,128,1024]{2,1,0:T(8,128)(2,1)}), bf16[16,128,1024]{2,1,0:T(8,128)(2,1)}, u32[]{:S(2)}, u32[]{:S(2)}) async-start(bf16[16,128,1024]{2,1,0:T(8,128)(2,1)} %shard_map.94), calls=%async_computation | async-start | bytes 8388608 | tf_op jit(solution)/shard_map/all_to_all | solution.py:386
  109.3 47.9 %collective-permute-start = (bf16[1024,1024]{1,0:T(8,128)(2,1)S(1)}, bf16[1024,1024]{1,0:T(8,128)(2,1)}, u32[]{:S(2)}, u32[]{:S(2)}) collective-permute-start(bf16[1024,1024]{1,0:T(8,128)(2,1)S(1)} %bitcast.27), channel_id=1, source_target_pairs={{0,1},{1,0},{2,3},{3,2},{4,5},{5,4},{6,7},{7,6},{8,9},{9,8},{10,11... | collective-permute-start | bytes 6291464 | tf_op jit(solution)/shard_map/ppermute | solution.py:134
  202.0 97.4 %all-to-all-start.2 = ((bf16[16,128,1024]{2,1,0:T(8,128)(2,1)}), bf16[16,128,1024]{2,1,0:T(8,128)(2,1)}, u32[]{:S(2)}, u32[]{:S(2)}) async-start(bf16[16,128,1024]{2,1,0:T(8,128)(2,1)} %get-tuple-element.31), calls=%async_computation.2 | async-start | bytes 8388608 | tf_op jit(solution)/shard_map/all_to_all | solution.py:386
  299.4 97.4 %all-to-all-start.3 = ((bf16[16,128,1024]{2,1,0:T(8,128)(2,1)}), bf16[16,128,1024]{2,1,0:T(8,128)(2,1)}, u32[]{:S(2)}, u32[]{:S(2)}) async-start(bf16[16,128,1024]{2,1,0:T(8,128)(2,1)} %get-tuple-element.35), calls=%async_computation.3 | async-start | bytes 8388608 | tf_op jit(solution)/shard_map/all_to_all | solution.py:386
  314.7 47.9 %collective-permute-start.1 = (bf16[1024,1024]{1,0:T(8,128)(2,1)}, bf16[1024,1024]{1,0:T(8,128)(2,1)S(1)}, u32[]{:S(2)}, u32[]{:S(2)}) collective-permute-start(bf16[1024,1024]{1,0:T(8,128)(2,1)} %get-tuple-element.32.refs_0_.refs_4_), channel_id=1, source_target_pairs={{0,1},{1,0},{2,3},{3,2},{4,5},{5,4},{6,7},{7,6},{8,9},{9,8},{10,11... | collective-permute-start | bytes 6291464 | tf_op jit(solution)/shard_map/ppermute | solution.py:134
  362.6 1.3 copy-start.11
  406.9 15.8 %collective-permute-start.2 = (bf16[4,272,256]{2,1,0:T(8,128)(2,1)}, bf16[4,272,256]{2,1,0:T(8,128)(2,1)S(1)}, u32[]{:S(2)}, u32[]{:S(2)}) collective-permute-start(bf16[4,272,256]{2,1,0:T(8,128)(2,1)} %get-tuple-element.37), channel_id=1, source_target_pairs={{0,1},{1,0},{2,3},{3,2},{4,5},{5,4},{6,7},{7,6},{8,9},{9,8},{10,11... | collective-permute-start | bytes 1671176 | tf_op jit(solution)/shard_map/ppermute | solution.py:433
  408.4 1.6 copy-start.2
  410.0 2.8 copy-start.3
  412.2 21.7 %collective-permute-start.3 = (bf16[1024,256]{1,0:T(8,128)(2,1)S(1)}, bf16[1024,256]{1,0:T(8,128)(2,1)S(1)}, u32[]{:S(2)}, u32[]{:S(2)}) collective-permute-start(bf16[1024,256]{1,0:T(8,128)(2,1)S(1)} %shard_map.102), channel_id=1, source_target_pairs={{0,1},{1,0},{2,3},{3,2},{4,5},{5,4},{6,7},{7,6},{8,9},{9,8},{10,11... | collective-permute-start | bytes 1572872 | tf_op jit(solution)/shard_map/ppermute | solution.py:422
  417.0 10.0 %copy-start.6 = (bf16[1024,2048]{1,0:T(8,128)(2,1)S(1)}, bf16[1024,2048]{1,0:T(8,128)(2,1)}, u32[]{:S(2)}) copy-start(bf16[1024,2048]{1,0:T(8,128)(2,1)} %get-tuple-element.34.normed) | copy-start | bytes 12582916
  425.4 23.9 %collective-permute-start.5 = (bf16[1024,256]{1,0:T(8,128)(2,1)}, bf16[1024,256]{1,0:T(8,128)(2,1)}, u32[]{:S(2)}, u32[]{:S(2)}) collective-permute-start(bf16[1024,256]{1,0:T(8,128)(2,1)} %shard_map.104), channel_id=1, source_target_pairs={{0,1},{1,0},{2,3},{3,2},{4,5},{5,4},{6,7},{7,6},{8,9},{9,8},{10,11... | collective-permute-start | bytes 1572872 | tf_op jit(solution)/shard_map/ppermute | solution.py:422
  433.4 7.7 %copy-start.5 = (f32[1024,1]{1,0:T(8,128)S(1)}, f32[1024,1]{1,0:T(8,128)}, u32[]{:S(2)}) copy-start(f32[1024,1]{1,0:T(8,128)} %get-tuple-element.33.refs_1_) | copy-start | bytes 12292
  433.9 0.8 copy-start.7
  435.8 1.6 copy-start.4
  437.4 3.8 copy-start.9
  437.4 3.8 copy-start
  437.4 3.8 copy-start.1
  437.4 3.8 copy-start.8
  439.6 15.9 %collective-permute-start.4 = (bf16[1024,256]{1,0:T(8,128)(2,1)S(1)}, bf16[1024,256]{1,0:T(8,128)(2,1)S(1)}, u32[]{:S(2)}, u32[]{:S(2)}) collective-permute-start(bf16[1024,256]{1,0:T(8,128)(2,1)S(1)} %shard_map.106), channel_id=1, source_target_pairs={{0,1},{1,0},{2,3},{3,2},{4,5},{5,4},{6,7},{7,6},{8,9},{9,8},{10,11... | collective-permute-start | bytes 1572872 | tf_op jit(solution)/shard_map/ppermute | solution.py:422

commit v6 on v5

--- a/solution.py
+++ b/solution.py
@@ -281,7 +281,7 @@
 
 def term(slope, weight, where, width, factor):
     rows, columns = slope.shape
-    tile = min(512, rows)
+    tile = min(1024, rows)
     return pl.pallas_call(
         functools.partial(term_kernel, factor),
         grid_spec=pltpu.PrefetchScalarGridSpec(

time: 463 us -> 463 us (level)
  no operation moved by 1% of the time
where the time goes in v6:
time: 463 us; the launch traced here: 461 us
  waiting for transfers between devices  316 us (68%)
  Pallas kernels  108 us (23%)
  starting transfers between devices  28.4 us (6%)
  local copies, waits for them, and re-layouts  7.89 us (2%)
    all_to_all x4, waiting for transfers between devices, exchange(): lax.all_to_all(blocks, 'group', split_axis=0, concat_axis=0, tiled=True)  218 us
    ppermute x2, waiting for transfers between devices, normalize(): lax.ppermute(own, 'mp', around(parts, step))  92.1 us
    pallas_call x2, Pallas kernels, outer_update(): pl.pallas_call(functools.partial(update_kernel, groups, mods, aliased), g...  21.7 us
    pallas_call x3, Pallas kernels, first_level_grad(): pl.pallas_call(functools.partial(first_kernel, factor, runs), grid=(rows...  20.3 us
    all_to_all x4, starting transfers between devices, exchange(): lax.all_to_all(blocks, 'group', split_axis=0, concat_axis=0, tiled=True)  20.2 us
    pallas_call x2, Pallas kernels, normalize(): pl.pallas_call(functools.partial(norm_kernel, parts, depth), grid_spec=pl...  17.8 us
    pallas_call x1, Pallas kernels, first_forward(): pl.pallas_call(functools.partial(state_kernel, factor), grid=(rows // til...  10.7 us
    pallas_call x4, Pallas kernels, term(): pl.pallas_call(functools.partial(term_kernel, factor), grid_spec=pltpu.Pr...  10.4 us
  transfers between devices with their start and end apart: 10, of which 8 were waited for; matrix products, arithmetic and copies ran while one was open for 1% of the time, Pallas kernels for 19%

profile of v6, /device:TPU:16, one launch (start us, length us, event | category | flops | bytes accessed | tf_op | source)
XLA Modules:
  0.0 461.3 jit_solution(14491356842037346799)
XLA Ops:
  0.6 5.1 %shard_map.95 = bf16[16,128,1024]{2,1,0:T(8,128)(2,1)} custom-call(f32[1,2,2048,1024]{3,2,1,0:T(8,128)} %src.3), custom_call_target="tpu_custom_call" | custom-call | bytes 12582912 | tf_op jit(solution)/shard_map/pallas_call | solution.py:41
  5.8 6.2 %all-to-all-start.1 = ((bf16[16,128,1024]{2,1,0:T(8,128)(2,1)}), bf16[16,128,1024]{2,1,0:T(8,128)(2,1)}, u32[]{:S(2)}, u32[]{:S(2)}) async-start(bf16[16,128,1024]{2,1,0:T(8,128)(2,1)} %shard_map.95), calls=%async_computation.1 | async-start | bytes 8388608 | tf_op jit(solution)/shard_map/all_to_all | solution.py:386
  11.9 5.1 %shard_map.94 = bf16[16,128,1024]{2,1,0:T(8,128)(2,1)} custom-call(f32[1,2,2048,1024]{3,2,1,0:T(8,128)} %src.3), custom_call_target="tpu_custom_call" | custom-call | bytes 12582912 | tf_op jit(solution)/shard_map/pallas_call | solution.py:41
  17.1 0.0 copy-start.10
  17.1 0.0 copy-start.12
  17.1 0.0 copy-start.13
  17.1 87.6 %all-to-all-done.1.received = bf16[16,128,1024]{2,1,0:T(8,128)(2,1)} async-done(((bf16[16,128,1024]{2,1,0:T(8,128)(2,1)}), bf16[16,128,1024]{2,1,0:T(8,128)(2,1)}, u32[]{:S(2)}, u32[]{:S(2)}) %all-to-all-start.1) | async-done | bytes 4194336 | tf_op jit(solution)/shard_map/all_to_all | solution.py:386
  104.6 4.7 %all-to-all-start = ((bf16[16,128,1024]{2,1,0:T(8,128)(2,1)}), bf16[16,128,1024]{2,1,0:T(8,128)(2,1)}, u32[]{:S(2)}, u32[]{:S(2)}) async-start(bf16[16,128,1024]{2,1,0:T(8,128)(2,1)} %shard_map.94), calls=%async_computation | async-start | bytes 8388608 | tf_op jit(solution)/shard_map/all_to_all | solution.py:386
  109.3 0.0 copy-done.10
  109.3 1.6 collective-permute-start
  110.9 0.0 copy-done.12
  110.9 0.0 copy-done.13
  110.9 0.6 slice_bitcast_fusion
  111.5 45.7 %collective-permute-done.refs_1_ = bf16[1024,1024]{1,0:T(8,128)(2,1)} collective-permute-done((bf16[1024,1024]{1,0:T(8,128)(2,1)S(1)}, bf16[1024,1024]{1,0:T(8,128)(2,1)}, u32[]{:S(2)}, u32[]{:S(2)}) %collective-permute-start) | collective-permute-done | bytes 2097184 | tf_op jit(solution)/shard_map/ppermute | solution.py:134
  157.2 8.9 %shard_map.96 = (bf16[1024,2048]{1,0:T(8,128)(2,1)}, f32[1024,1]{1,0:T(8,128)}) custom-call(s32[1]{0:T(128)} %bitcast.4.place.where, bf16[1024,1024]{1,0:T(8,128)(2,1)} %bitcast.25, bf16[1024,1024]{1,0:T(8,128)(2,1)} %collective-permute-done.refs_1_), custom_call_target="tpu_custom_call" | custom-call | bytes 8388608 | tf_op jit(solution)/shard_map/pallas_call | solution.py:137
  166.1 10.9 %shard_map.97 = (f32[16,128,1024]{2,1,0:T(8,128)}, f32[16,128,1024]{2,1,0:T(8,128)}, bf16[16,128,1024]{2,1,0:T(8,128)(2,1)}) custom-call(s32[16]{0:T(128)} %get-tuple-element.52.old, s32[16]{0:T(128)} %get-tuple-element.47.new, bf16[16,128,1024]{2,1,0:T(8,128)(2,1)} %all-to-all-done.1.received, f32[16,128,1024]{2,1,0:T(8,128)} %anchor.3, ...), custom_call_target="tpu_custom_call" | custom-call | bytes 25165824 | tf_op jit(solution)/shard_map/pallas_call | solution.py:83
  176.9 25.1 %all-to-all-done.received = bf16[16,128,1024]{2,1,0:T(8,128)(2,1)} async-done(((bf16[16,128,1024]{2,1,0:T(8,128)(2,1)}), bf16[16,128,1024]{2,1,0:T(8,128)(2,1)}, u32[]{:S(2)}, u32[]{:S(2)}) %all-to-all-start) | async-done | bytes 4194336 | tf_op jit(solution)/shard_map/all_to_all | solution.py:386
  202.0 4.7 %all-to-all-start.2 = ((bf16[16,128,1024]{2,1,0:T(8,128)(2,1)}), bf16[16,128,1024]{2,1,0:T(8,128)(2,1)}, u32[]{:S(2)}, u32[]{:S(2)}) async-start(bf16[16,128,1024]{2,1,0:T(8,128)(2,1)} %get-tuple-element.31), calls=%async_computation.2 | async-start | bytes 8388608 | tf_op jit(solution)/shard_map/all_to_all | solution.py:386
  206.7 10.8 %shard_map.98 = (f32[16,128,1024]{2,1,0:T(8,128)}, f32[16,128,1024]{2,1,0:T(8,128)}, bf16[16,128,1024]{2,1,0:T(8,128)(2,1)}) custom-call(s32[16]{0:T(128)} %get-tuple-element.51.old, s32[16]{0:T(128)} %get-tuple-element.48.new, bf16[16,128,1024]{2,1,0:T(8,128)(2,1)} %all-to-all-done.received, ...), custom_call_target="tpu_custom_call", output_to_operand_aliasing={{0}: (5, {}), {1}: (6, {})} | custom-call | bytes 25165824 | tf_op jit(solution)/shard_map/pallas_call | solution.py:83
  217.5 81.9 %all-to-all-done.2 = bf16[16,128,1024]{2,1,0:T(8,128)(2,1)} async-done(((bf16[16,128,1024]{2,1,0:T(8,128)(2,1)}), bf16[16,128,1024]{2,1,0:T(8,128)(2,1)}, u32[]{:S(2)}, u32[]{:S(2)}) %all-to-all-start.2) | async-done | bytes 4194336 | tf_op jit(solution)/shard_map/all_to_all | solution.py:386
  299.4 4.7 %all-to-all-start.3 = ((bf16[16,128,1024]{2,1,0:T(8,128)(2,1)}), bf16[16,128,1024]{2,1,0:T(8,128)(2,1)}, u32[]{:S(2)}, u32[]{:S(2)}) async-start(bf16[16,128,1024]{2,1,0:T(8,128)(2,1)} %get-tuple-element.35), calls=%async_computation.3 | async-start | bytes 8388608 | tf_op jit(solution)/shard_map/all_to_all | solution.py:386
  304.1 10.7 %shard_map.99 = (bf16[1024,1024]{1,0:T(8,128)(2,1)}, f32[1024,1024]{1,0:T(8,128)}) custom-call(bf16[1024,2048]{1,0:T(8,128)(2,1)} %get-tuple-element.25.normed.refs_0_, bf16[2048,1024]{1,0:T(8,128)(2,1)} %bitcast.6.weight, bf16[1024,1024]{1,0:T(8,128)(2,1)} %bitcast.26), custom_call_target="tpu_custom_call" | custom-call | flops 4294967296 | bytes 16777216 | tf_op jit(solution)/shard_map/pallas_call | solution.py:196
  314.7 1.5 collective-permute-start.1
  316.2 46.4 %collective-permute-done.1.refs_1_ = bf16[1024,1024]{1,0:T(8,128)(2,1)S(1)} collective-permute-done((bf16[1024,1024]{1,0:T(8,128)(2,1)}, bf16[1024,1024]{1,0:T(8,128)(2,1)S(1)}, u32[]{:S(2)}, u32[]{:S(2)}) %collective-permute-start.1) | collective-permute-done | bytes 2097184 | tf_op jit(solution)/shard_map/ppermute | solution.py:134
  362.6 0.0 copy-start.11
  362.6 1.3 copy-done.11
  364.0 8.9 %shard_map.100 = (bf16[1024,2048]{1,0:T(8,128)(2,1)}, f32[1024,1]{1,0:T(8,128)}) custom-call(s32[1]{0:T(128)} %bitcast.4.place.where, bf16[1024,1024]{1,0:T(8,128)(2,1)} %get-tuple-element.32.refs_0_.refs_4_, bf16[1024,1024]{1,0:T(8,128)(2,1)} %copy-done.11), custom_call_target="tpu_custom_call" | custom-call | bytes 8388608 | tf_op jit(solution)/shard_map/pallas_call | solution.py:137
  372.8 23.9 %all-to-all-done.3 = bf16[16,128,1024]{2,1,0:T(8,128)(2,1)} async-done(((bf16[16,128,1024]{2,1,0:T(8,128)(2,1)}), bf16[16,128,1024]{2,1,0:T(8,128)(2,1)}, u32[]{:S(2)}, u32[]{:S(2)}) %all-to-all-start.3) | async-done | bytes 4194336 | tf_op jit(solution)/shard_map/all_to_all | solution.py:386
  396.8 10.2 %shard_map.101 = (bf16[1024,1024]{1,0:T(8,128)(2,1)}, f32[8,1024]{1,0:T(8,128)}, bf16[4,272,256]{2,1,0:T(8,128)(2,1)}) custom-call(s32[1]{0:T(128)} %bitcast.7.at, bf16[1024,2048]{1,0:T(8,128)(2,1)} %get-tuple-element.34.normed, bf16[2048,1024]{1,0:T(8,128)(2,1)} %bitcast.8.weight, bf16[1024,1024]{1,0:T(8,128)(2,1)} %bitcast.21), custom_call_target="tpu_custom_call" | custom-call | flops 301989888 | bytes 786432 | tf_op jit(solution)/shard_map/pallas_call | solution.py:248
  406.9 1.5 collective-permute-start.2
  408.4 0.0 copy-start.2
  408.4 1.6 copy-done.2
  410.0 0.0 copy-start.3
  410.0 1.9 shard_map.102
  411.9 0.6 collective-permute-start.3
  412.5 0.0 copy-done.3
  412.6 4.0 shard_map.103.refs_6_
  416.5 0.0 copy-start.6
  416.5 0.9 slice.22
  417.4 5.2 %collective-permute-done.2.refs_7_ = bf16[4,272,256]{2,1,0:T(8,128)(2,1)S(1)} collective-permute-done((bf16[4,272,256]{2,1,0:T(8,128)(2,1)}, bf16[4,272,256]{2,1,0:T(8,128)(2,1)S(1)}, u32[]{:S(2)}, u32[]{:S(2)}) %collective-permute-start.2) | collective-permute-done | bytes 557088 | tf_op jit(solution)/shard_map/ppermute | solution.py:433
  422.7 2.6 shard_map.104
  425.3 1.5 collective-permute-start.5
  426.8 0.0 copy-done.6
  426.8 6.5 %shard_map.105.refs_9_ = bf16[1,2,2048,1024]{3,2,1,0:T(8,128)(2,1)} custom-call(bf16[1024,2048]{1,0:T(8,128)(2,1)S(1)} %copy-done.6, bf16[1024,1024]{1,0:T(8,128)(2,1)S(1)} %copy-done.3), custom_call_target="tpu_custom_call" | custom-call | flops 4294967296 | bytes 10485760 | tf_op jit(solution)/shard_map/pallas_call | solution.py:168
  433.3 0.0 copy-start.5
  433.3 0.6 collective-permute-done.3.refs_8_
  433.9 0.0 copy-start.7
  433.9 0.8 copy-done.7
  434.7 1.0 copy.15
  435.8 0.0 copy-start.4
  435.8 1.6 copy-done.4
  437.4 1.9 shard_map.106
  439.3 1.6 collective-permute-start.4
  440.9 0.0 copy-done.5
  440.9 0.0 copy-done.9
  440.9 0.1 multiply_multiply_fusion.refs_2_
  440.9 0.0 copy-done
  440.9 0.0 copy-done.1
  440.9 0.0 copy-done.8
  441.0 8.1 %shard_map.107.refs_8_ = bf16[1,2,2048,1024]{3,2,1,0:T(8,128)(2,1)} custom-call(bf16[1024,2048]{1,0:T(8,128)(2,1)} %get-tuple-element.25.normed.refs_0_, f32[1024,1]{1,0:T(8,128)S(1)} %copy-done.5, f32[1024,1]{1,0:T(8,128)S(1)} %multiply_multiply_fusion.refs_2_, bf16[1024,1024]{1,0:T(8,128)(2,1)S(1)} %bitcast.22, ...), custom_call_target="tpu_custom_call", output_to_operand_aliasing={{}: (9, {})} | custom-call | flops 8589934592 | bytes 54525952 | tf_op jit(solution)/shard_map/pallas_call | solution.py:349
  449.0 0.0 collective-permute-done.5.refs_7_
  449.0 6.2 %shard_map.108.refs_8_ = bf16[1,2,2048,1024]{3,2,1,0:T(8,128)(2,1)} custom-call(bf16[1024,2048]{1,0:T(8,128)(2,1)} %get-tuple-element.25.normed.refs_0_, f32[1024,1]{1,0:T(8,128)S(1)} %copy-done.5, f32[1024,1]{1,0:T(8,128)S(1)} %multiply_multiply_fusion.refs_2_, bf16[1024,1024]{1,0:T(8,128)(2,1)S(1)} %bitcast.23, ...), custom_call_target="tpu_custom_call", output_to_operand_aliasing={{}: (8, {})} | custom-call | flops 4294967296 | bytes 35651584 | tf_op jit(solution)/shard_map/pallas_call | solution.py:349
  455.2 0.0 collective-permute-done.4.refs_7_
  455.2 6.1 %shard_map.109 = bf16[1,2,2048,1024]{3,2,1,0:T(8,128)(2,1)} custom-call(bf16[1024,2048]{1,0:T(8,128)(2,1)} %get-tuple-element.25.normed.refs_0_, f32[1024,1]{1,0:T(8,128)S(1)} %copy-done.5, f32[1024,1]{1,0:T(8,128)S(1)} %multiply_multiply_fusion.refs_2_, bf16[1024,1024]{1,0:T(8,128)(2,1)S(1)} %bitcast.24, ...), custom_call_target="tpu_custom_call", output_to_operand_aliasing={{}: (8, {})} | custom-call | flops 4294967296 | bytes 35651584 | tf_op jit(solution)/shard_map/pallas_call | solution.py:349
  (7 shorter events, 0.0 us)
Async XLA Ops:
  5.8 98.9 %all-to-all-start.1 = ((bf16[16,128,1024]{2,1,0:T(8,128)(2,1)}), bf16[16,128,1024]{2,1,0:T(8,128)(2,1)}, u32[]{:S(2)}, u32[]{:S(2)}) async-start(bf16[16,128,1024]{2,1,0:T(8,128)(2,1)} %shard_map.95), calls=%async_computation.1 | async-start | bytes 8388608 | tf_op jit(solution)/shard_map/all_to_all | solution.py:386
  17.1 92.3 %copy-start.10 = (bf16[1,1024,1024]{2,1,0:T(8,128)(2,1)S(1)}, bf16[1,1024,1024]{2,1,0:T(8,128)(2,1)}, u32[]{:S(2)}) copy-start(bf16[1,1024,1024]{2,1,0:T(8,128)(2,1)} %param.12) | copy-start | bytes 6291460
  17.1 93.8 %copy-start.12 = (s32[16,2]{0,1:T(2,128)S(1)}, s32[16,2]{0,1:T(2,128)}, u32[]{:S(2)}) copy-start(s32[16,2]{0,1:T(2,128)} %param.11) | copy-start | bytes 388
  17.1 93.8 %copy-start.13 = (s32[16,2]{0,1:T(2,128)S(1)}, s32[16,2]{0,1:T(2,128)}, u32[]{:S(2)}) copy-start(s32[16,2]{0,1:T(2,128)} %param.10) | copy-start | bytes 388
  104.6 97.4 %all-to-all-start = ((bf16[16,128,1024]{2,1,0:T(8,128)(2,1)}), bf16[16,128,1024]{2,1,0:T(8,128)(2,1)}, u32[]{:S(2)}, u32[]{:S(2)}) async-start(bf16[16,128,1024]{2,1,0:T(8,128)(2,1)} %shard_map.94), calls=%async_computation | async-start | bytes 8388608 | tf_op jit(solution)/shard_map/all_to_all | solution.py:386
  109.3 47.9 %collective-permute-start = (bf16[1024,1024]{1,0:T(8,128)(2,1)S(1)}, bf16[1024,1024]{1,0:T(8,128)(2,1)}, u32[]{:S(2)}, u32[]{:S(2)}) collective-permute-start(bf16[1024,1024]{1,0:T(8,128)(2,1)S(1)} %bitcast.27), channel_id=1, source_target_pairs={{0,1},{1,0},{2,3},{3,2},{4,5},{5,4},{6,7},{7,6},{8,9},{9,8},{10,11... | collective-permute-start | bytes 6291464 | tf_op jit(solution)/shard_map/ppermute | solution.py:134
  202.0 97.4 %all-to-all-start.2 = ((bf16[16,128,1024]{2,1,0:T(8,128)(2,1)}), bf16[16,128,1024]{2,1,0:T(8,128)(2,1)}, u32[]{:S(2)}, u32[]{:S(2)}) async-start(bf16[16,128,1024]{2,1,0:T(8,128)(2,1)} %get-tuple-element.31), calls=%async_computation.2 | async-start | bytes 8388608 | tf_op jit(solution)/shard_map/all_to_all | solution.py:386
  299.4 97.4 %all-to-all-start.3 = ((bf16[16,128,1024]{2,1,0:T(8,128)(2,1)}), bf16[16,128,1024]{2,1,0:T(8,128)(2,1)}, u32[]{:S(2)}, u32[]{:S(2)}) async-start(bf16[16,128,1024]{2,1,0:T(8,128)(2,1)} %get-tuple-element.35), calls=%async_computation.3 | async-start | bytes 8388608 | tf_op jit(solution)/shard_map/all_to_all | solution.py:386
  314.7 47.9 %collective-permute-start.1 = (bf16[1024,1024]{1,0:T(8,128)(2,1)}, bf16[1024,1024]{1,0:T(8,128)(2,1)S(1)}, u32[]{:S(2)}, u32[]{:S(2)}) collective-permute-start(bf16[1024,1024]{1,0:T(8,128)(2,1)} %get-tuple-element.32.refs_0_.refs_4_), channel_id=1, source_target_pairs={{0,1},{1,0},{2,3},{3,2},{4,5},{5,4},{6,7},{7,6},{8,9},{9,8},{10,11... | collective-permute-start | bytes 6291464 | tf_op jit(solution)/shard_map/ppermute | solution.py:134
  362.6 1.3 copy-start.11
  406.9 15.8 %collective-permute-start.2 = (bf16[4,272,256]{2,1,0:T(8,128)(2,1)}, bf16[4,272,256]{2,1,0:T(8,128)(2,1)S(1)}, u32[]{:S(2)}, u32[]{:S(2)}) collective-permute-start(bf16[4,272,256]{2,1,0:T(8,128)(2,1)} %get-tuple-element.37), channel_id=1, source_target_pairs={{0,1},{1,0},{2,3},{3,2},{4,5},{5,4},{6,7},{7,6},{8,9},{9,8},{10,11... | collective-permute-start | bytes 1671176 | tf_op jit(solution)/shard_map/ppermute | solution.py:433
  408.4 1.6 copy-start.2
  410.0 2.5 copy-start.3
  411.9 22.0 %collective-permute-start.3 = (bf16[1024,256]{1,0:T(8,128)(2,1)S(1)}, bf16[1024,256]{1,0:T(8,128)(2,1)S(1)}, u32[]{:S(2)}, u32[]{:S(2)}) collective-permute-start(bf16[1024,256]{1,0:T(8,128)(2,1)S(1)} %shard_map.102), channel_id=1, source_target_pairs={{0,1},{1,0},{2,3},{3,2},{4,5},{5,4},{6,7},{7,6},{8,9},{9,8},{10,11... | collective-permute-start | bytes 1572872 | tf_op jit(solution)/shard_map/ppermute | solution.py:422
  416.5 10.3 %copy-start.6 = (bf16[1024,2048]{1,0:T(8,128)(2,1)S(1)}, bf16[1024,2048]{1,0:T(8,128)(2,1)}, u32[]{:S(2)}) copy-start(bf16[1024,2048]{1,0:T(8,128)(2,1)} %get-tuple-element.34.normed) | copy-start | bytes 12582916
  425.3 23.8 %collective-permute-start.5 = (bf16[1024,256]{1,0:T(8,128)(2,1)}, bf16[1024,256]{1,0:T(8,128)(2,1)}, u32[]{:S(2)}, u32[]{:S(2)}) collective-permute-start(bf16[1024,256]{1,0:T(8,128)(2,1)} %shard_map.104), channel_id=1, source_target_pairs={{0,1},{1,0},{2,3},{3,2},{4,5},{5,4},{6,7},{7,6},{8,9},{9,8},{10,11... | collective-permute-start | bytes 1572872 | tf_op jit(solution)/shard_map/ppermute | solution.py:422
  433.3 7.6 %copy-start.5 = (f32[1024,1]{1,0:T(8,128)S(1)}, f32[1024,1]{1,0:T(8,128)}, u32[]{:S(2)}) copy-start(f32[1024,1]{1,0:T(8,128)} %get-tuple-element.33.refs_1_) | copy-start | bytes 12292
  433.9 0.8 copy-start.7
  435.8 1.6 copy-start.4
  437.4 3.5 copy-start.9
  437.4 3.6 copy-start
  437.4 3.6 copy-start.1
  437.4 3.6 copy-start.8
  439.3 15.9 %collective-permute-start.4 = (bf16[1024,256]{1,0:T(8,128)(2,1)S(1)}, bf16[1024,256]{1,0:T(8,128)(2,1)S(1)}, u32[]{:S(2)}, u32[]{:S(2)}) collective-permute-start(bf16[1024,256]{1,0:T(8,128)(2,1)S(1)} %shard_map.106), channel_id=1, source_target_pairs={{0,1},{1,0},{2,3},{3,2},{4,5},{5,4},{6,7},{7,6},{8,9},{9,8},{10,11... | collective-permute-start | bytes 1572872 | tf_op jit(solution)/shard_map/ppermute | solution.py:422
